TPU v7x, 256 devices: a whole 4x4x8 slice. The times are simulated.
256 devices in a mesh: band: 16 (over y, x_lo, core), blk: 16 (over z, x_hi).
Axes of the slice: x: 4 (x_hi: 2, x_lo: 2; x = x_hi * 2 + x_lo), y: 4, z: 8, core: 2. Of those that a mesh axis runs over, the one named last changes fastest.
Arguments:
- load_columns: float32 [16, 16, 4, 32, 384], P('band', 'blk'), may hold values from -6 to 6
- stiffness: float32 [16, 16, 4, 384, 384], P('band', 'blk')
- rigid_modes: bfloat16 [16, 16, 4, 36, 384], P('band', 'blk'), may hold values from -0.3125 to 0.3125
- neighbours: int32 [16, 16, 4, 8], P('band', 'blk'), may hold values from 0 to 5, as said below
- slot_valid: int32 [16, 16, 4, 8], P('band', 'blk'), may hold values from 0 to 1, as said below
- pair_left: int32 [16, 16, 4, 128], P('band', 'blk'), may hold values from 0 to 63
- pair_right: int32 [16, 16, 4, 128], P('band', 'blk'), may hold values from 0 to 63
- penalty: float32 [16, 16, 4, 128], P('band', 'blk'), may hold values from 0.1 to 1
Outputs:
- displacement: float32 [16, 16, 4, 32, 384], P('band', 'blk')
- residual: float32 [16, 16, 4, 32, 384], P('band', 'blk')
Inputs may be any that keep to these rules, and one draw needn't show every extreme that they name: `neighbours`: only aggregates 2 * 1 to 2 of a device name entries from 4 to 4 + 1 - 1 (the next sector's device), only aggregates 3 * 1 to 3 name entries from 5 up (the next band's device), and no aggregate of the last band does; all other entries are below 4. `slot_valid`: the valid slots of each aggregate are a prefix of its slots, slot 0 always valid; some aggregate has all 8 slots valid.
All inputs are finite; a program needn't handle non-finite values.
Results may differ from a plain program's by a relative error of at most 0.0003.
Values sent between devices are 32-bit elements; how exact they have to be, the bound alone decides.
No kernel may reach another device: no remote copies, remote signals or barrier semaphores. Data moves between devices by JAX's collectives and lax.ppermute only.
A program may use at most 192 MiB of HBM per device.

v0:
```python
import jax
import jax.numpy as jnp
from jax import lax
from jax.sharding import PartitionSpec as P

COLS = 32
BLOCKS = 64
MODES = 36
SLOTS = 8
PAIRS_SLOT = 16
RIM = 1
PRE = 2
COARSE_SWEEPS = 4


fine_damping = 0.6
coarse_damping = 0.7
highest = lax.Precision.HIGHEST


def shifted(x, axis, by):
    length = lax.axis_size(axis)
    return lax.ppermute(x, axis, [(i, (i + by) % length) for i in range(length)])


def passed_along(block, axis, distance):
    devices = range(lax.axis_size(axis))
    route = [(i - distance, i) for i in devices if i - distance in devices]
    return lax.ppermute(block, axis, route)


def block_rows(source):
    amount = source.shape[0]
    breadth = source.shape[1]
    return (
        source.reshape(amount, breadth, BLOCKS, 6)
        .transpose(0, 2, 1, 3)
        .reshape(amount * BLOCKS, breadth * 6)
    )


def unblock(summed, amount):
    breadth = summed.shape[1] // 6
    return (
        summed.reshape(amount, BLOCKS, breadth, 6)
        .transpose(0, 2, 1, 3)
        .reshape(amount, breadth, BLOCKS * 6)
    )


def pair_springs(source, near_rows, far_rows, weight):
    amount = source.shape[0]
    rows_all = block_rows(source)
    forces = weight[:, None] * (rows_all[near_rows] - rows_all[far_rows])
    summed = jax.ops.segment_sum(
        jnp.concatenate([forces, -forces]),
        jnp.concatenate([near_rows, far_rows]),
        num_segments=amount * BLOCKS,
    )
    return unblock(summed, amount)


def pair_layout(neighbours, slot_valid, pair_left, pair_right, penalty):
    aggregates = neighbours.shape[0]
    target = jnp.repeat(neighbours, PAIRS_SLOT, axis=1)
    weight = penalty * jnp.repeat(slot_valid, PAIRS_SLOT, axis=1).astype(jnp.float32)
    near_rows = (jnp.arange(aggregates, dtype=jnp.int32)[:, None] * BLOCKS + pair_left).reshape(-1)
    far_rows = (target * BLOCKS + pair_right).reshape(-1)
    return (target, weight, near_rows, far_rows)


def ahead(values):
    sector_rim = shifted(values[:RIM], "blk", -1)
    band_rim = passed_along(values[RIM : 2 * RIM], "band", -1)
    return (sector_rim, band_rim)


def behind(sector_part, band_part):
    sector_in = shifted(sector_part, "blk", 1)
    band_in = passed_along(band_part, "band", 1)
    return (sector_in, band_in)


def add_rims(values, sector_part, band_part):
    return values.at[:RIM].add(sector_part).at[RIM : 2 * RIM].add(band_part)


def invert_block(block):
    triangle = jnp.linalg.cholesky(block)
    return jax.scipy.linalg.cho_solve((triangle, True), jnp.eye(block.shape[0], dtype=block.dtype))


def shards(
    load_columns, stiffness, rigid_modes, neighbours, slot_valid, pair_left, pair_right, penalty
):
    loads = load_columns[0, 0]
    local_stiffness = stiffness[0, 0]
    local_modes = rigid_modes[0, 0]
    local_links = neighbours[0, 0]
    local_left = pair_left[0, 0]
    local_right = pair_right[0, 0]
    aggregates = loads.shape[0]
    target, weight, near_rows, far_rows = pair_layout(
        local_links, slot_valid[0, 0], local_left, local_right, penalty[0, 0]
    )
    flat_weight = weight.reshape(-1)
    totals = jax.ops.segment_sum(
        jnp.concatenate([flat_weight, flat_weight]),
        jnp.concatenate([near_rows, far_rows]),
        num_segments=(aggregates + 2 * RIM) * BLOCKS,
    )
    totals = totals.reshape(aggregates + 2 * RIM, BLOCKS)
    sector_in, band_in = behind(totals[aggregates : aggregates + RIM], totals[aggregates + RIM :])
    totals = add_rims(totals[:aggregates], sector_in, band_in)
    fine_diagonal = jnp.diagonal(local_stiffness, axis1=1, axis2=2) + jnp.repeat(totals, 6, axis=1)
    reciprocal = 1.0 / fine_diagonal
    modes_wide = local_modes.astype(jnp.float32)
    sector_modes, band_modes = ahead(modes_wide)
    mode_rows = block_rows(jnp.concatenate([modes_wide, sector_modes, band_modes]))
    grouped = (aggregates, SLOTS, PAIRS_SLOT, MODES, 6)
    near_modes = mode_rows[near_rows].reshape(grouped)
    far_modes = mode_rows[far_rows].reshape(grouped)
    scales = weight.reshape(aggregates, SLOTS, PAIRS_SLOT, 1, 1)
    coupling = -jnp.einsum("aspkd,aspld->askl", scales * near_modes, far_modes, precision=highest)
    self_term = jnp.einsum("aspkd,aspld->akl", scales * near_modes, near_modes, precision=highest)
    other_term = jnp.einsum("aspkd,aspld->askl", scales * far_modes, far_modes, precision=highest)
    landed = jax.ops.segment_sum(
        other_term.reshape(aggregates * SLOTS, MODES, MODES),
        local_links.reshape(-1),
        num_segments=aggregates + 2 * RIM,
    )
    projected = jnp.einsum("akf,afg->akg", modes_wide, local_stiffness, precision=highest)
    galerkin = jnp.einsum("akg,alg->akl", projected, modes_wide, precision=highest)
    sector_in, band_in = behind(landed[aggregates : aggregates + RIM], landed[aggregates + RIM :])
    coarse_diagonal = add_rims(galerkin + self_term + landed[:aggregates], sector_in, band_in)
    coarse_inverse = jax.vmap(invert_block)(coarse_diagonal)

    def fine_product(field):
        rim_sector, rim_band = ahead(field)
        source = jnp.concatenate([field, rim_sector, rim_band])
        springs = pair_springs(source, near_rows, far_rows, flat_weight)
        bending = jnp.einsum("acf,afg->acg", field, local_stiffness, precision=highest)
        result = bending + springs[:aggregates]
        sector_part, band_part = behind(
            springs[aggregates : aggregates + RIM], springs[aggregates + RIM :]
        )
        return add_rims(result, sector_part, band_part)

    field = jnp.zeros_like(loads)
    residual = loads
    for sweep_index in range(PRE):
        field = field + fine_damping * reciprocal[:, None, :] * residual
        residual = loads - fine_product(field)
    restricted = jnp.einsum("acf,akf->ack", residual, modes_wide, precision=highest)
    correction = coarse_damping * jnp.einsum(
        "akl,acl->ack", coarse_inverse, restricted, precision=highest
    )
    for sweep_index in range(1, COARSE_SWEEPS):
        coarse_rim_sector, coarse_rim_band = ahead(correction)
        coarse_source = jnp.concatenate([correction, coarse_rim_sector, coarse_rim_band])
        nearby = coarse_source[local_links]
        coarse_result = jnp.einsum("akl,acl->ack", coarse_diagonal, correction, precision=highest)
        coarse_result = coarse_result + jnp.einsum(
            "askl,ascl->ack", coupling, nearby, precision=highest
        )
        reverse = jnp.einsum("askl,ack->ascl", coupling, correction, precision=highest)
        spread = jax.ops.segment_sum(
            reverse.reshape(aggregates * SLOTS, COLS, MODES),
            local_links.reshape(-1),
            num_segments=aggregates + 2 * RIM,
        )
        coarse_sector_part, coarse_band_part = behind(
            spread[aggregates : aggregates + RIM], spread[aggregates + RIM :]
        )
        misfit = restricted - add_rims(
            coarse_result + spread[:aggregates], coarse_sector_part, coarse_band_part
        )
        correction = correction + coarse_damping * jnp.einsum(
            "akl,acl->ack", coarse_inverse, misfit, precision=highest
        )
    field = field + jnp.einsum("ack,akf->acf", correction, modes_wide, precision=highest)
    residual = loads - fine_product(field)
    field = field + fine_damping * reciprocal[:, None, :] * residual
    residual = loads - fine_product(field)
    return (field[None, None], residual[None, None])


def solution(mesh):
    in_specs = (
        P("band", "blk", None, None, None),
        P("band", "blk", None, None, None),
        P("band", "blk", None, None, None),
        P("band", "blk", None, None),
        P("band", "blk", None, None),
        P("band", "blk", None, None),
        P("band", "blk", None, None),
        P("band", "blk", None, None),
    )
    out_specs = (P("band", "blk", None, None, None), P("band", "blk", None, None, None))
    return jax.shard_map(shards, mesh=mesh, in_specs=in_specs, out_specs=out_specs, check_vma=False)
```

profile of v0, /device:TPU:104, one launch (start us, length us, event | category | flops | bytes accessed | tf_op | source)
XLA Modules:
  0.0 478.4 jit_solution(5218055628819014248)
XLA Ops:
  3.8 7.6 %scatter_custom_fusion = f32[384]{0:T(512)S(1)} fusion(s32[1024]{0:T(1024)S(1)} %pad_add_fusion, f32[1024]{0:T(1024)S(1)} %pad_maximum_fusion.8, f32[]{:T(128)} %constant.451.clone.1), kind=kCustom, calls=%fused_computation.187 | custom fusion | flops 1024 | bytes 1540 | tf_op jit(solution)/shard_map/scatter-add | solution.py:107
  17.5 4.5 collective-permute-start.11
  26.9 36.4 %copy.265 = f32[1,1,4,384,384]{2,4,3,1,0:T(8,128)} copy(f32[1,1,4,384,384]{4,3,2,1,0:T(8,128)} %param.45) | data formatting | bytes 4718592 | tf_op args[1]
  65.3 8.3 %gather_fusion = f32[384,4]{1,0:T(8,128)S(1)} fusion(f32[4,384,384]{0,2,1:T(8,128)} %bitcast, s32[384]{0:T(512)S(1)} %or_reduce_fusion), kind=kCustom, calls=%fused_computation | custom fusion | bytes 15360 | tf_op jit(solution)/shard_map/jit(diagonal)/gather | solution.py:115
  99.4 7.5 %scatter_custom_fusion.1 = f32[384,192]{1,0:T(8,128)} fusion(s32[1024]{0:T(1024)} %copy-done.29, f32[512,192]{1,0:T(8,128)S(1)} %get-tuple-element.224, f32[]{:T(128)} %constant.484, f32[512,192]{1,0:T(8,128)} %get-tuple-element.225, f32[]{:T(128)} %constant.451.clone.1), kind=kCustom, calls=%fused_computation.68 | custom fusion | flops 393216 | bytes 1213440 | tf_op jit(solution)/shard_map/scatter-add | solution.py:55
  117.4 4.5 collective-permute-start.4
  144.7 4.6 copy.306
  150.3 3.8 reshape.758
  154.1 6.1 %broadcast_multiply_fusion.1 = (f32[4,8,16,36,6]{2,1,0,4,3:T(8,128)}, f32[4,8,16,36,6]{2,1,0,4,3:T(8,128)S(1)}) fusion(f32[4,8,16,36,6]{2,1,0,4,3:T(8,128)} %reshape.758, f32[4,8,16]{2,1,0:T(8,128)S(1)} %broadcast_multiply_fusion.2, f32[4,8,16,36,6]{2,1,0,4,3:T(8,128)} %reshape.759), kind=kLoop, calls=%fused_computation.41 | loop fusion | flops 221184 | bytes 1771520 | tf_op jit(solution)/shard_map/mul | solution.py:125
  160.3 6.8 %fusion.2 = f32[4,8,36,36,1]{3,2,4,1,0:T(8,128)} fusion(f32[4,8,16,36,6]{3,2,4,1,0:T(8,128)S(1)} %copy-done.2, f32[4,8,16,36,6]{2,1,0,4,3:T(8,128)S(1)} %get-tuple-element.259), kind=kOutput, calls=%fused_computation.25 | convolution fusion | flops 47775744 | bytes 1050624 | tf_op jit(solution)/shard_map/aspkd,aspld->askl/dot_general | solution.py:126
  167.1 3.7 scatter_fusion
  170.8 11.3 %fusion.35 = f32[4,36,36]{1,2,0:T(8,128)S(1)} fusion(f32[4,8,16,36,6]{2,1,0,4,3:T(8,128)} %reshape.758, f32[4,8,16,36,6]{2,1,0,4,3:T(8,128)} %get-tuple-element.258), kind=kOutput, calls=%fused_computation.49 | convolution fusion | flops 47775744 | bytes 905472 | tf_op jit(solution)/shard_map/aspkd,aspld->akl/dot_general | solution.py:125
  182.2 6.4 %fusion.20 = f32[4,8,36,36]{3,2,1,0:T(8,128)S(1)} fusion(f32[4,8,16,36,6]{3,2,4,1,0:T(8,128)S(1)} %copy-done.3, f32[4,8,16,36,6]{2,1,0,4,3:T(8,128)S(1)} %copy-done.1), kind=kOutput, calls=%fused_computation.43 | convolution fusion | flops 47817216 | bytes 1050624 | tf_op jit(solution)/shard_map/aspkd,aspld->askl/dot_general | solution.py:124
  199.0 13.2 %custom-call.11 = f32[4,36,36]{2,1,0:T(8,128)S(1)} custom-call(f32[4,36,36]{2,1,0:T(8,128)S(1)} %fusion.81), custom_call_target="Cholesky" | custom-call | tf_op jit(solution)/shard_map/vmap(jit(cholesky))/cholesky | solution.py:89
  213.1 11.1 %custom-call.12 = f32[4,1,36,36]{2,3,1,0:T(8,128)S(1)} custom-call(f32[4,1,36,36]{3,2,1,0:T(8,128)S(1)} %select_bitcast_fusion), custom_call_target="InvertDiagBlocksLowerTriangular" | custom-call | tf_op jit(solution)/shard_map/vmap(jit(_cho_solve))/triangular_solve | solution.py:90
  255.5 7.5 %scatter_custom_fusion.2 = f32[384,192]{1,0:T(8,128)} fusion(s32[1024]{0:T(1024)} %copy-done.29, f32[512,192]{1,0:T(8,128)S(1)} %get-tuple-element.222, f32[]{:T(128)} %constant.484, f32[512,192]{1,0:T(8,128)} %get-tuple-element.223, f32[]{:T(128)} %constant.451.clone.1), kind=kCustom, calls=%fused_computation.72 | custom fusion | flops 393216 | bytes 1213440 | tf_op jit(solution)/shard_map/scatter-add | solution.py:55
  276.2 4.7 collective-permute-start.8
  301.0 3.4 scatter_fusion.1
  305.0 3.5 collective-permute-start.16
  321.7 4.5 collective-permute-start.19
  327.3 3.4 scatter_fusion.2
  347.1 4.5 collective-permute-start.23
  353.6 3.4 scatter_fusion.3
  357.6 3.4 collective-permute-start.24
  372.7 4.5 collective-permute-start.27
  378.9 6.4 %collective-permute-done.26 = f32[1,32,384]{2,1,0:T(8,128)S(1)} collective-permute-done((f32[1,32,384]{2,1,0:T(8,128)S(1)}, f32[1,32,384]{2,1,0:T(8,128)S(1)}, u32[]{:S(2)}, u32[]{:S(2)}) %collective-permute-start.26) | collective-permute-done | bytes 49184 | tf_op jit(solution)/shard_map/ppermute | solution.py:23
  400.3 6.8 %scatter_custom_fusion.7 = f32[384,192]{1,0:T(8,128)S(1)} fusion(s32[1024]{0:T(1024)} %copy-done.29, f32[512,192]{1,0:T(8,128)} %get-tuple-element.220, f32[]{:T(128)} %constant.484, f32[512,192]{1,0:T(8,128)} %get-tuple-element.221, f32[]{:T(128)} %constant.451.clone.1), kind=kCustom, calls=%fused_computation.76 | custom fusion | flops 393216 | bytes 1344512 | tf_op jit(solution)/shard_map/scatter-add | solution.py:55
  414.0 5.3 %collective-permute-start.28 = (f32[1,32,384]{2,1,0:T(8,128)S(1)}, f32[1,32,384]{2,1,0:T(8,128)S(1)}, u32[]{:S(2)}, u32[]{:S(2)}) collective-permute-start(f32[1,32,384]{2,1,0:T(8,128)S(1)} %copy.327), channel_id=1, source_target_pairs={{0,1},{1,2},{2,3},{3,4},{4,5},{5,6},{6,7},{7,8},{8,9},{9,10},{10,1... | collective-permute-start | bytes 147464 | tf_op jit(solution)/shard_map/ppermute | solution.py:23
  422.8 4.7 collective-permute-done.29
  431.2 4.2 collective-permute-done.30
  451.9 7.5 %scatter_custom_fusion.8 = f32[384,192]{1,0:T(8,128)} fusion(s32[1024]{0:T(1024)} %copy-done.29, f32[512,192]{1,0:T(8,128)S(1)} %get-tuple-element.218, f32[]{:T(128)} %constant.484, f32[512,192]{1,0:T(8,128)} %get-tuple-element.219, f32[]{:T(128)} %constant.451.clone.1), kind=kCustom, calls=%fused_computation.80 | custom fusion | flops 393216 | bytes 1213440 | tf_op jit(solution)/shard_map/scatter-add | solution.py:55
  473.8 3.4 collective-permute-done.33
  (315 shorter events, 259.2 us)
Async XLA Ops:
  11.5 62.3 %collective-permute-start = (f32[1,64]{1,0:T(1,128)S(1)}, f32[1,64]{1,0:T(1,128)S(1)}, u32[]{:S(2)}, u32[]{:S(2)}) collective-permute-start(f32[1,64]{1,0:T(1,128)S(1)} %get-tuple-element.261), channel_id=1, source_target_pairs={{0,1},{1,2},{2,3},{3,4},{4,5},{5,6},{6,7},{7,8},{8,9},{9,10},{10,1... | collective-permute-start | bytes 776 | tf_op jit(solution)/shard_map/ppermute | solution.py:23
  14.5 59.3 %collective-permute-start.1 = (f32[1,64]{1,0:T(1,128)S(1)}, f32[1,64]{1,0:T(1,128)S(1)}, u32[]{:S(2)}, u32[]{:S(2)}) collective-permute-start(f32[1,64]{1,0:T(1,128)S(1)} %get-tuple-element.260), channel_id=1, source_target_pairs={{0,16},{16,32},{32,48},{48,64},{64,80},{80,96},{96,112},{112,128},... | collective-permute-start | bytes 776 | tf_op jit(solution)/shard_map/ppermute | solution.py:29
  17.5 107.4 %collective-permute-start.11 = (f32[1,36,384]{2,0,1:T(1,128)S(1)}, f32[1,36,384]{2,0,1:T(1,128)S(1)}, u32[]{:S(2)}, u32[]{:S(2)}) collective-permute-start(f32[1,36,384]{2,0,1:T(1,128)S(1)} %get-tuple-element.235), channel_id=1, source_target_pairs={{16,0},{32,16},{48,32},{64,48},{80,64},{96,80},{112,96},{128,112},... | collective-permute-start | bytes 165896 | tf_op jit(solution)/shard_map/ppermute | solution.py:29
  22.0 102.9 %collective-permute-start.10 = (f32[1,36,384]{2,0,1:T(1,128)S(1)}, f32[1,36,384]{2,0,1:T(1,128)S(1)}, u32[]{:S(2)}, u32[]{:S(2)}) collective-permute-start(f32[1,36,384]{2,0,1:T(1,128)S(1)} %get-tuple-element.234), channel_id=1, source_target_pairs={{0,15},{1,0},{2,1},{3,2},{4,3},{5,4},{6,5},{7,6},{8,7},{9,8},{10,9... | collective-permute-start | bytes 165896 | tf_op jit(solution)/shard_map/ppermute | solution.py:23
  76.1 6.0 %collective-permute-start.2 = (f32[1,32,384]{2,1,0:T(8,128)S(1)}, f32[1,32,384]{2,1,0:T(8,128)}, u32[]{:S(2)}, u32[]{:S(2)}) collective-permute-start(f32[1,32,384]{2,1,0:T(8,128)S(1)} %get-tuple-element.242), channel_id=1, source_target_pairs={{0,15},{1,0},{2,1},{3,2},{4,3},{5,4},{6,5},{7,6},{8,7},{9,8},{10,9... | collective-permute-start | bytes 147464 | tf_op jit(solution)/shard_map/ppermute | solution.py:23
  117.4 108.0 %collective-permute-start.4 = (f32[1,32,384]{2,1,0:T(8,128)}, f32[1,32,384]{2,1,0:T(8,128)}, u32[]{:S(2)}, u32[]{:S(2)}) collective-permute-start(f32[1,32,384]{2,1,0:T(8,128)} %copy.276), channel_id=1, source_target_pairs={{0,1},{1,2},{2,3},{3,4},{4,5},{5,6},{6,7},{7,8},{8,9},{9,10},{10,1... | collective-permute-start | bytes 147464 | tf_op jit(solution)/shard_map/ppermute | solution.py:23
  122.7 104.0 %collective-permute-start.5 = (f32[1,32,384]{2,1,0:T(8,128)}, f32[1,32,384]{2,1,0:T(8,128)}, u32[]{:S(2)}, u32[]{:S(2)}) collective-permute-start(f32[1,32,384]{2,1,0:T(8,128)} %copy.278), channel_id=1, source_target_pairs={{0,16},{16,32},{32,48},{48,64},{64,80},{80,96},{96,112},{112,128},... | collective-permute-start | bytes 147464 | tf_op jit(solution)/shard_map/ppermute | solution.py:29
  190.0 7.4 %collective-permute-start.12 = (f32[1,36,36]{1,2,0:T(8,128)}, f32[1,36,36]{1,2,0:T(8,128)}, u32[]{:S(2)}, u32[]{:S(2)}) collective-permute-start(f32[1,36,36]{1,2,0:T(8,128)} %copy.363), channel_id=1, source_target_pairs={{0,1},{1,2},{2,3},{3,4},{4,5},{5,6},{6,7},{7,8},{8,9},{9,10},{10,1... | collective-permute-start | bytes 15560 | tf_op jit(solution)/shard_map/ppermute | solution.py:23
  192.9 6.0 %collective-permute-start.13 = (f32[1,36,36]{1,2,0:T(8,128)S(1)}, f32[1,36,36]{1,2,0:T(8,128)S(1)}, u32[]{:S(2)}, u32[]{:S(2)}) collective-permute-start(f32[1,36,36]{1,2,0:T(8,128)S(1)} %copy.364), channel_id=1, source_target_pairs={{0,16},{16,32},{32,48},{48,64},{64,80},{80,96},{96,112},{112,128},... | collective-permute-start | bytes 15560 | tf_op jit(solution)/shard_map/ppermute | solution.py:29
  229.2 5.5 %collective-permute-start.7 = (f32[1,32,384]{2,1,0:T(8,128)S(1)}, f32[1,32,384]{2,1,0:T(8,128)S(1)}, u32[]{:S(2)}, u32[]{:S(2)}) collective-permute-start(f32[1,32,384]{2,1,0:T(8,128)S(1)} %get-tuple-element.241), channel_id=1, source_target_pairs={{16,0},{32,16},{48,32},{64,48},{80,64},{96,80},{112,96},{128,112},... | collective-permute-start | bytes 147464 | tf_op jit(solution)/shard_map/ppermute | solution.py:29
  231.8 5.7 %collective-permute-start.6 = (f32[1,32,384]{2,1,0:T(8,128)S(1)}, f32[1,32,384]{2,1,0:T(8,128)S(1)}, u32[]{:S(2)}, u32[]{:S(2)}) collective-permute-start(f32[1,32,384]{2,1,0:T(8,128)S(1)} %get-tuple-element.240), channel_id=1, source_target_pairs={{0,15},{1,0},{2,1},{3,2},{4,3},{5,4},{6,5},{7,6},{8,7},{9,8},{10,9... | collective-permute-start | bytes 147464 | tf_op jit(solution)/shard_map/ppermute | solution.py:23
  276.2 12.9 %collective-permute-start.8 = (f32[1,32,384]{2,1,0:T(8,128)}, f32[1,32,384]{2,1,0:T(8,128)}, u32[]{:S(2)}, u32[]{:S(2)}) collective-permute-start(f32[1,32,384]{2,1,0:T(8,128)} %copy.288), channel_id=1, source_target_pairs={{0,1},{1,2},{2,3},{3,4},{4,5},{5,6},{6,7},{7,8},{8,9},{9,10},{10,1... | collective-permute-start | bytes 147464 | tf_op jit(solution)/shard_map/ppermute | solution.py:23
  287.2 6.5 %collective-permute-start.9 = (f32[1,32,384]{2,1,0:T(8,128)}, f32[1,32,384]{2,1,0:T(8,128)S(1)}, u32[]{:S(2)}, u32[]{:S(2)}) collective-permute-start(f32[1,32,384]{2,1,0:T(8,128)} %copy.290), channel_id=1, source_target_pairs={{0,16},{16,32},{32,48},{48,64},{64,80},{80,96},{96,112},{112,128},... | collective-permute-start | bytes 147464 | tf_op jit(solution)/shard_map/ppermute | solution.py:29
  297.6 12.8 %collective-permute-start.15 = (f32[1,32,36]{2,1,0:T(8,128)}, f32[1,32,36]{2,1,0:T(8,128)S(1)}, u32[]{:S(2)}, u32[]{:S(2)}) collective-permute-start(f32[1,32,36]{2,1,0:T(8,128)} %get-tuple-element.257), channel_id=1, source_target_pairs={{16,0},{32,16},{48,32},{64,48},{80,64},{96,80},{112,96},{128,112},... | collective-permute-start | bytes 13832 | tf_op jit(solution)/shard_map/ppermute | solution.py:29
  299.5 10.9 %collective-permute-start.14 = (f32[1,32,36]{2,1,0:T(8,128)}, f32[1,32,36]{2,1,0:T(8,128)}, u32[]{:S(2)}, u32[]{:S(2)}) collective-permute-start(f32[1,32,36]{2,1,0:T(8,128)} %get-tuple-element.256), channel_id=1, source_target_pairs={{0,15},{1,0},{2,1},{3,2},{4,3},{5,4},{6,5},{7,6},{8,7},{9,8},{10,9... | collective-permute-start | bytes 13832 | tf_op jit(solution)/shard_map/ppermute | solution.py:23
  305.0 12.1 %collective-permute-start.16 = (f32[1,32,36]{2,1,0:T(8,128)}, f32[1,32,36]{2,1,0:T(8,128)}, u32[]{:S(2)}, u32[]{:S(2)}) collective-permute-start(f32[1,32,36]{2,1,0:T(8,128)} %get-tuple-element.251), channel_id=1, source_target_pairs={{0,1},{1,2},{2,3},{3,4},{4,5},{5,6},{6,7},{7,8},{8,9},{9,10},{10,1... | collective-permute-start | bytes 13832 | tf_op jit(solution)/shard_map/ppermute | solution.py:23
  308.5 9.3 %collective-permute-start.17 = (f32[1,32,36]{2,1,0:T(8,128)}, f32[1,32,36]{2,1,0:T(8,128)}, u32[]{:S(2)}, u32[]{:S(2)}) collective-permute-start(f32[1,32,36]{2,1,0:T(8,128)} %get-tuple-element.250), channel_id=1, source_target_pairs={{0,16},{16,32},{32,48},{48,64},{64,80},{80,96},{96,112},{112,128},... | collective-permute-start | bytes 13832 | tf_op jit(solution)/shard_map/ppermute | solution.py:29
  321.7 14.1 %collective-permute-start.19 = (f32[1,32,36]{2,1,0:T(8,128)}, f32[1,32,36]{2,1,0:T(8,128)S(1)}, u32[]{:S(2)}, u32[]{:S(2)}) collective-permute-start(f32[1,32,36]{2,1,0:T(8,128)} %get-tuple-element.255), channel_id=1, source_target_pairs={{16,0},{32,16},{48,32},{64,48},{80,64},{96,80},{112,96},{128,112},... | collective-permute-start | bytes 13832 | tf_op jit(solution)/shard_map/ppermute | solution.py:29
  326.3 9.5 %collective-permute-start.18 = (f32[1,32,36]{2,1,0:T(8,128)}, f32[1,32,36]{2,1,0:T(8,128)}, u32[]{:S(2)}, u32[]{:S(2)}) collective-permute-start(f32[1,32,36]{2,1,0:T(8,128)} %get-tuple-element.254), channel_id=1, source_target_pairs={{0,15},{1,0},{2,1},{3,2},{4,3},{5,4},{6,5},{7,6},{8,7},{9,8},{10,9... | collective-permute-start | bytes 13832 | tf_op jit(solution)/shard_map/ppermute | solution.py:23
  331.3 11.2 %collective-permute-start.20 = (f32[1,32,36]{2,1,0:T(8,128)}, f32[1,32,36]{2,1,0:T(8,128)}, u32[]{:S(2)}, u32[]{:S(2)}) collective-permute-start(f32[1,32,36]{2,1,0:T(8,128)} %get-tuple-element.249), channel_id=1, source_target_pairs={{0,1},{1,2},{2,3},{3,4},{4,5},{5,6},{6,7},{7,8},{8,9},{9,10},{10,1... | collective-permute-start | bytes 13832 | tf_op jit(solution)/shard_map/ppermute | solution.py:23
  333.9 9.3 %collective-permute-start.21 = (f32[1,32,36]{2,1,0:T(8,128)}, f32[1,32,36]{2,1,0:T(8,128)}, u32[]{:S(2)}, u32[]{:S(2)}) collective-permute-start(f32[1,32,36]{2,1,0:T(8,128)} %get-tuple-element.248), channel_id=1, source_target_pairs={{0,16},{16,32},{32,48},{48,64},{64,80},{80,96},{96,112},{112,128},... | collective-permute-start | bytes 13832 | tf_op jit(solution)/shard_map/ppermute | solution.py:29
  347.1 15.8 %collective-permute-start.23 = (f32[1,32,36]{2,1,0:T(8,128)}, f32[1,32,36]{2,1,0:T(8,128)}, u32[]{:S(2)}, u32[]{:S(2)}) collective-permute-start(f32[1,32,36]{2,1,0:T(8,128)} %get-tuple-element.253), channel_id=1, source_target_pairs={{16,0},{32,16},{48,32},{64,48},{80,64},{96,80},{112,96},{128,112},... | collective-permute-start | bytes 13832 | tf_op jit(solution)/shard_map/ppermute | solution.py:29
  351.6 11.3 %collective-permute-start.22 = (f32[1,32,36]{2,1,0:T(8,128)}, f32[1,32,36]{2,1,0:T(8,128)}, u32[]{:S(2)}, u32[]{:S(2)}) collective-permute-start(f32[1,32,36]{2,1,0:T(8,128)} %get-tuple-element.252), channel_id=1, source_target_pairs={{0,15},{1,0},{2,1},{3,2},{4,3},{5,4},{6,5},{7,6},{8,7},{9,8},{10,9... | collective-permute-start | bytes 13832 | tf_op jit(solution)/shard_map/ppermute | solution.py:23
  357.6 12.1 %collective-permute-start.24 = (f32[1,32,36]{2,1,0:T(8,128)}, f32[1,32,36]{2,1,0:T(8,128)}, u32[]{:S(2)}, u32[]{:S(2)}) collective-permute-start(f32[1,32,36]{2,1,0:T(8,128)} %get-tuple-element.247), channel_id=1, source_target_pairs={{0,1},{1,2},{2,3},{3,4},{4,5},{5,6},{6,7},{7,8},{8,9},{9,10},{10,1... | collective-permute-start | bytes 13832 | tf_op jit(solution)/shard_map/ppermute | solution.py:23
  361.0 9.4 %collective-permute-start.25 = (f32[1,32,36]{2,1,0:T(8,128)}, f32[1,32,36]{2,1,0:T(8,128)S(1)}, u32[]{:S(2)}, u32[]{:S(2)}) collective-permute-start(f32[1,32,36]{2,1,0:T(8,128)} %get-tuple-element.246), channel_id=1, source_target_pairs={{0,16},{16,32},{32,48},{48,64},{64,80},{80,96},{96,112},{112,128},... | collective-permute-start | bytes 13832 | tf_op jit(solution)/shard_map/ppermute | solution.py:29
  372.7 6.3 %collective-permute-start.27 = (f32[1,32,384]{2,1,0:T(8,128)S(1)}, f32[1,32,384]{2,1,0:T(8,128)S(1)}, u32[]{:S(2)}, u32[]{:S(2)}) collective-permute-start(f32[1,32,384]{2,1,0:T(8,128)S(1)} %get-tuple-element.239), channel_id=1, source_target_pairs={{16,0},{32,16},{48,32},{64,48},{80,64},{96,80},{112,96},{128,112},... | collective-permute-start | bytes 147464 | tf_op jit(solution)/shard_map/ppermute | solution.py:29
  377.2 8.2 %collective-permute-start.26 = (f32[1,32,384]{2,1,0:T(8,128)S(1)}, f32[1,32,384]{2,1,0:T(8,128)S(1)}, u32[]{:S(2)}, u32[]{:S(2)}) collective-permute-start(f32[1,32,384]{2,1,0:T(8,128)S(1)} %get-tuple-element.238), channel_id=1, source_target_pairs={{0,15},{1,0},{2,1},{3,2},{4,3},{5,4},{6,5},{7,6},{8,7},{9,8},{10,9... | collective-permute-start | bytes 147464 | tf_op jit(solution)/shard_map/ppermute | solution.py:23
  414.0 8.8 %collective-permute-start.28 = (f32[1,32,384]{2,1,0:T(8,128)S(1)}, f32[1,32,384]{2,1,0:T(8,128)S(1)}, u32[]{:S(2)}, u32[]{:S(2)}) collective-permute-start(f32[1,32,384]{2,1,0:T(8,128)S(1)} %copy.327), channel_id=1, source_target_pairs={{0,1},{1,2},{2,3},{3,4},{4,5},{5,6},{6,7},{7,8},{8,9},{9,10},{10,1... | collective-permute-start | bytes 147464 | tf_op jit(solution)/shard_map/ppermute | solution.py:23
  420.9 6.6 %collective-permute-start.29 = (f32[1,32,384]{2,1,0:T(8,128)S(1)}, f32[1,32,384]{2,1,0:T(8,128)S(1)}, u32[]{:S(2)}, u32[]{:S(2)}) collective-permute-start(f32[1,32,384]{2,1,0:T(8,128)S(1)} %copy.329), channel_id=1, source_target_pairs={{0,16},{16,32},{32,48},{48,64},{64,80},{80,96},{96,112},{112,128},... | collective-permute-start | bytes 147464 | tf_op jit(solution)/shard_map/ppermute | solution.py:29
  429.5 6.0 %collective-permute-start.30 = (f32[1,32,384]{2,1,0:T(8,128)S(1)}, f32[1,32,384]{2,1,0:T(8,128)S(1)}, u32[]{:S(2)}, u32[]{:S(2)}) collective-permute-start(f32[1,32,384]{2,1,0:T(8,128)S(1)} %get-tuple-element.236), channel_id=1, source_target_pairs={{0,15},{1,0},{2,1},{3,2},{4,3},{5,4},{6,5},{7,6},{8,7},{9,8},{10,9... | collective-permute-start | bytes 147464 | tf_op jit(solution)/shard_map/ppermute | solution.py:23
  467.2 6.6 %collective-permute-start.32 = (f32[1,32,384]{2,1,0:T(8,128)S(1)}, f32[1,32,384]{2,1,0:T(8,128)S(1)}, u32[]{:S(2)}, u32[]{:S(2)}) collective-permute-start(f32[1,32,384]{2,1,0:T(8,128)S(1)} %copy.339), channel_id=1, source_target_pairs={{0,1},{1,2},{2,3},{3,4},{4,5},{5,6},{6,7},{7,8},{8,9},{9,10},{10,1... | collective-permute-start | bytes 147464 | tf_op jit(solution)/shard_map/ppermute | solution.py:23
  470.9 6.3 %collective-permute-start.33 = (f32[1,32,384]{2,1,0:T(8,128)S(1)}, f32[1,32,384]{2,1,0:T(8,128)S(1)}, u32[]{:S(2)}, u32[]{:S(2)}) collective-permute-start(f32[1,32,384]{2,1,0:T(8,128)S(1)} %copy.341), channel_id=1, source_target_pairs={{0,16},{16,32},{32,48},{48,64},{64,80},{80,96},{96,112},{112,128},... | collective-permute-start | bytes 147464 | tf_op jit(solution)/shard_map/ppermute | solution.py:29
  (33 other events, 881.5 us)
where the time goes:
time: 488 us; the launch traced here: 478 us
  local copies, waits for them, and re-layouts  185 us (38%)
  other arithmetic  117 us (24%)
  starting transfers between devices  87.5 us (18%)
  matrix products  56 us (11%)
  waiting for transfers between devices  31.3 us (6%)
    ppermute x17, starting transfers between devices, passed_along(): return lax.ppermute(block, axis, route)  45.2 us
    ppermute x17, starting transfers between devices, shifted(): lax.ppermute(x, axis, [(i, (i + by) % length) for i in range(length)])  42.4 us
    unnamed x64, local copies, waits for them, and re-layouts  38.5 us
    scatter-add x4, other arithmetic, pair_springs(): jax.ops.segment_sum(jnp.concatenate([forces, -forces]), jnp.concatenate([...  29.3 us
    gather x8, local copies, waits for them, and re-layouts, pair_springs(): forces = weight[:, None] * (rows_all[near_rows] - rows_all[far_rows])  17.8 us
    slice x12, local copies, waits for them, and re-layouts, fine_product(): result = bending + springs[:aggregates]  17.5 us
    ppermute x17, waiting for transfers between devices, shifted(): lax.ppermute(x, axis, [(i, (i + by) % length) for i in range(length)])  17.4 us
    transpose x5, local copies, waits for them, and re-layouts, block_rows(): return source.reshape(amount, breadth, BLOCKS, 6).transpose(0, 2, 1, 3).r...  14.1 us
  transfers between devices with their start and end apart: 34, of which 11 were waited for; matrix products, arithmetic and copies ran while one was open for 48% of the time, Pallas kernels for 0%

commit v1 on v0

v1 whole, which is shorter than its diff:
```python
import jax
import jax.numpy as jnp
from jax import lax
from jax.experimental import pallas as pl
from jax.experimental.pallas import tpu as pltpu
from jax.sharding import PartitionSpec as P

COLS = 32
BLOCKS = 64
DOF = 384
MODES = 36
SLOTS = 8
PAIRS = 128
AGG = 4
LANES = 128
PAIRED = 3
MROWS = 40

fine_damping = 0.6
coarse_damping = 0.7
f32 = jnp.float32
bf16 = jnp.bfloat16

NN = (((1,), (0,)), ((), ()))
NT = (((1,), (1,)), ((), ()))


def dot(a, b, dims=NN):
    return lax.dot_general(a, b, dims, preferred_element_type=f32)


def exact(a, b, dims=NN):
    return lax.dot_general(
        a, b, dims, precision=lax.Precision.HIGHEST, preferred_element_type=f32
    )


def split2(x):
    hi = x.astype(bf16)
    lo = (x - hi.astype(f32)).astype(bf16)
    return hi, lo


def split3(x):
    hi = x.astype(bf16)
    rest = x - hi.astype(f32)
    mid = rest.astype(bf16)
    lo = (rest - mid.astype(f32)).astype(bf16)
    return hi, mid, lo


def mm3(x, whi, wlo, dims=NN):
    rows = x.shape[0]
    hi, lo = split2(x)
    first = dot(jnp.concatenate([hi, lo], axis=0), whi, dims)
    return first[:rows] + first[rows:] + dot(hi, wlo, dims)


def mm2(x, w, dims=NN):
    rows = x.shape[0]
    hi, lo = split2(x)
    both = dot(jnp.concatenate([hi, lo], axis=0), w, dims)
    return both[:rows] + both[rows:]


def mm_exact(x, w, dims=NN):
    rows = x.shape[0]
    parts = dot(jnp.concatenate(split3(x), axis=0), w, dims)
    return parts[:rows] + parts[rows : 2 * rows] + parts[2 * rows :]


def iota(shape, axis):
    return lax.broadcasted_iota(jnp.int32, shape, axis)


def permutation():
    i = iota((DOF, DOF), 0)
    j = iota((DOF, DOF), 1)
    return (i == 6 * (j & 63) + (j >> 6)).astype(f32).astype(bf16)


def permutation_back():
    i = iota((DOF, DOF), 0)
    j = iota((DOF, DOF), 1)
    return (j == 6 * (i & 63) + (i >> 6)).astype(f32).astype(bf16)


def hot_twice(index):
    k = iota((LANES, PAIRS), 0) & 63
    return (k == index.astype(jnp.int32)).astype(f32).astype(bf16)


def hot_paired(index):
    r = iota((LANES, 2 * PAIRS), 0)
    doubled = jnp.concatenate([index.astype(jnp.int32)] * 2, axis=1)
    want = doubled + 64 * (iota((1, 2 * PAIRS), 1) >> 7)
    return (r == want).astype(f32).astype(bf16)


def wide(t):
    return jnp.concatenate([t] * PAIRED, axis=1)


def stack_fields(v):
    rows = []
    for m in range(PAIRED):
        rows.append(jnp.concatenate([x[:, m * LANES : (m + 1) * LANES] for x in v], axis=1))
    return jnp.concatenate(rows, axis=0)


def unstack_fields(y, count):
    out = []
    for a in range(count):
        parts = [
            y[m * COLS : (m + 1) * COLS, a * LANES : (a + 1) * LANES] for m in range(PAIRED)
        ]
        out.append(jnp.concatenate(parts, axis=1))
    return out


def rows_of(x):
    return jnp.concatenate([x[:, m * LANES : (m + 1) * LANES] for m in range(PAIRED)], axis=0)


def lanes_of(x):
    r = x.shape[0] // PAIRED
    return jnp.concatenate([x[m * r : (m + 1) * r] for m in range(PAIRED)], axis=1)


def local_product(v, khi, klo, ghi, glo, cross):
    springs = unstack_fields(mm3(stack_fields(v), ghi, glo), AGG)
    return [
        mm3(v[a], khi[a], klo[a]) + (springs[a] + v[a] * cross[a]) for a in range(AGG)
    ]


def to_own(vh, xhi, xlo):
    return lanes_of(mm3(rows_of(vh), xhi, xlo, NT))


def to_halo(v, xhi, xlo):
    return lanes_of(mm3(rows_of(v), xhi, xlo))


def pick(flag, a, b):
    return jnp.where(flag, a, b)


def send(parity, message, blk1, blk0, band1, band0):
    odd_s = parity[0] == 1
    odd_b = parity[1] == 1
    blk1[...] = pick(odd_s, message[2], message[0])
    blk0[...] = pick(odd_s, message[0], message[2])
    band1[...] = pick(odd_b, message[3], message[1])
    band0[...] = pick(odd_b, message[1], message[3])


def receive(parity, blk1, blk0, band1, band0):
    odd_s = parity[0] == 1
    odd_b = parity[1] == 1
    blk1, blk0, band1, band0 = blk1[...], blk0[...], band1[...], band0[...]
    return [
        pick(odd_s, blk0, blk1),
        pick(odd_b, band0, band1),
        pick(odd_s, blk1, blk0),
        pick(odd_b, band1, band0),
    ]


def first_kernel(
    parity, b, k, q, nb, valid, left, right, penalty,
    blk1, blk0, band1, band0, khi, klo, bp, qp, gal, dsum, dloc, tab,
):
    expand = (iota((SLOTS, PAIRS), 0) == (iota((SLOTS, PAIRS), 1) >> 4)).astype(f32)
    slot = dot(nb[...].astype(f32), expand)
    weight = penalty[...] * dot(valid[...].astype(f32), expand)
    crossing = slot > 3.5
    lf = left[...].astype(f32)
    rf = right[...].astype(f32)
    far = slot * 64.0 + rf
    wloc = jnp.where(crossing, 0.0, weight)
    tab[0:4] = lf
    tab[4:8] = rf
    tab[8:12] = far
    tab[12:16] = wloc
    tab[16:20] = jnp.where(crossing, weight, 0.0)

    near = []
    arrive = jnp.zeros((1, AGG * LANES), f32)
    rr = iota((AGG * LANES, PAIRS), 0)
    row = (rr >> 7) * 64 + (rr & 63)
    for a in range(AGG):
        w3 = jnp.concatenate(split3(wloc[a : a + 1]), axis=0)
        near.append(jnp.sum(dot(w3, hot_twice(lf[a : a + 1]), NT), axis=0, keepdims=True))
        hot = (row == far[a : a + 1].astype(jnp.int32)).astype(f32).astype(bf16)
        arrive = arrive + jnp.sum(dot(w3, hot, NT), axis=0, keepdims=True)
    totals = []
    for a in range(AGG):
        total = near[a] + arrive[:, a * LANES : (a + 1) * LANES]
        tab[20 + a : 21 + a] = total
        totals.append(wide(total))

    perm = permutation()
    eye = iota((LANES, LANES), 0) == iota((LANES, LANES), 1)
    diagonals = []
    for a in range(AGG):
        cuts = []
        for m in range(PAIRED):
            tile = k[a, m * LANES : (m + 1) * LANES, m * LANES : (m + 1) * LANES]
            cuts.append(jnp.sum(jnp.where(eye, tile, 0.0), axis=0, keepdims=True))
        diagonals.append(jnp.concatenate(cuts, axis=1))
    stacked = jnp.concatenate([b[a] for a in range(AGG)] + diagonals + [jnp.zeros((4, DOF), f32)], axis=0)
    turned = mm_exact(stacked, perm)
    messages = []
    pad = jnp.zeros((MROWS - MODES, DOF), f32)
    for a in range(AGG):
        load = turned[a * COLS : (a + 1) * COLS]
        bp[a] = load
        diagonal = turned[AGG * COLS + a : AGG * COLS + a + 1] + totals[a]
        dloc[a : a + 1] = diagonal
        modes = jnp.concatenate([q[a].astype(f32), pad], axis=0).astype(bf16)
        turned_modes = dot(modes, perm)
        qp[a, 0:MROWS] = turned_modes.astype(bf16)
        qp[a, MROWS:LANES] = jnp.zeros((LANES - MROWS, DOF), bf16)
        hi, lo = split2(k[a])
        khi[a] = hi
        klo[a] = lo
        projected = dot(modes, hi) + dot(modes, lo)
        wide_modes = jnp.concatenate([modes, jnp.zeros((LANES - MROWS, DOF), bf16)], axis=0)
        galerkin = mm2(projected, wide_modes, NT)
        gal[a] = galerkin
        springs = mm2(turned_modes * totals[a], qp[a], NT)
        table = jnp.concatenate(
            [lf[a : a + 1], rf[a : a + 1], jnp.where(crossing, weight, 0.0)[a : a + 1]], axis=1
        )
        fine = jnp.concatenate([load, turned_modes], axis=0)
        extra = jnp.concatenate([diagonal, table, jnp.zeros((6, DOF), f32)], axis=0)
        body = jnp.concatenate([fine, extra], axis=0)
        dsum[a] = galerkin + springs
        side = jnp.concatenate([galerkin + springs, jnp.zeros((80 - MROWS, LANES), f32)], axis=0)
        messages.append(jnp.concatenate([body, side], axis=1))
    send(parity, messages, blk1, blk0, band1, band0)


def local_kernel(khi, klo, qp, gal, tab, pkhi, pklo, ghi, glo, big):
    perm = permutation()
    back = permutation_back()
    for a in range(AGG):
        pkhi[a] = dot(back, dot(khi[a], perm).astype(bf16)).astype(bf16)
        pklo[a] = dot(back, dot(klo[a], perm).astype(bf16)).astype(bf16)
    r = iota((AGG * LANES, 2 * PAIRS), 0)
    shift = 64 * (iota((1, 2 * PAIRS), 1) >> 7)
    big[...] = jnp.zeros((AGG * LANES, AGG * LANES), f32)
    for a in range(AGG):
        l2 = jnp.concatenate([tab[a : a + 1]] * 2, axis=1).astype(jnp.int32) + shift + a * LANES
        fi = tab[8 + a : 9 + a].astype(jnp.int32)
        fi = (fi >> 6) * LANES + (fi & 63)
        f2 = jnp.concatenate([fi] * 2, axis=1) + shift
        w2 = jnp.concatenate([tab[12 + a : 13 + a]] * 2, axis=1)
        far = (r == f2).astype(f32)
        hi, mid, lo = split3(w2)
        near = (r[0:LANES] + a * LANES == l2).astype(f32)
        nb = near.astype(bf16)
        farb = far.astype(bf16)
        parts = jnp.concatenate([nb * hi, nb * mid, nb * lo], axis=0)
        m = dot(parts, farb, NT)
        m = m[0:LANES] + m[LANES : 2 * LANES] + m[2 * LANES :]
        big[a * LANES : (a + 1) * LANES, :] += m
    mm = big[...]
    adj = mm + mm.T
    eye = iota((AGG * LANES, AGG * LANES), 0) == iota((AGG * LANES, AGG * LANES), 1)
    total = jnp.concatenate([tab[20 + a : 21 + a] for a in range(AGG)], axis=1)
    lap = jnp.where(eye, total, 0.0) - adj
    gh, gl = split2(lap)
    ghi[...] = gh
    glo[...] = gl
    big[...] = jnp.zeros((AGG * LANES, AGG * LANES), f32)
    ys = []
    for a in range(AGG):
        rows = rows_of(qp[a, 0:MROWS])
        y = dot(rows, gh[a * LANES : (a + 1) * LANES]) + dot(rows, gl[a * LANES : (a + 1) * LANES])
        ys.append(y)
    for a in range(AGG):
        stacked = jnp.concatenate(
            [lanes_of(y[:, a * LANES : (a + 1) * LANES]) for y in ys], axis=0
        )
        block = mm2(stacked, qp[a], NT)
        for c in range(AGG):
            part = block[c * MROWS : (c + 1) * MROWS]
            if c == a:
                part = part + gal[a]
            big[c * LANES : c * LANES + MROWS, a * LANES : (a + 1) * LANES] = part


def crossing_kernel_values(received, tab, j):
    if j < 2:
        table = received[73:74]
        halo = table[:, 0:PAIRS]
        own = table[:, PAIRS : 2 * PAIRS]
        w = table[:, 2 * PAIRS : 3 * PAIRS]
    else:
        own = tab[j : j + 1]
        halo = tab[4 + j : 5 + j]
        w = tab[16 + j : 17 + j]
    return own, halo, w


def second_kernel(
    parity, blk1, blk0, band1, band0, bp, qp, dloc, tab, khi, klo, ghi, glo,
    oblk1, oblk0, oband1, oband0, xhi, xlo, rec, rech, qh, cdh, tco, tch, x2o, r1o, dlt, pr, pgo,
):
    halo = receive(parity, blk1, blk0, band1, band0)
    cross, crossh, xs, xh = [], [], [], []
    for j in range(AGG):
        own, far, w = crossing_kernel_values(halo[j], tab, j)
        w3 = jnp.concatenate(split3(w), axis=0)
        cross.append(wide(jnp.sum(dot(w3, hot_twice(own), NT), axis=0, keepdims=True)))
        crossh.append(wide(jnp.sum(dot(w3, hot_twice(far), NT), axis=0, keepdims=True)))
        near = hot_paired(own)
        hi, mid, lo = split3(jnp.concatenate([w, w], axis=1))
        m = dot(jnp.concatenate([near * hi, near * mid, near * lo], axis=0), hot_paired(far), NT)
        m = m[0:LANES] + m[LANES : 2 * LANES] + m[2 * LANES :]
        hi, lo = split2(m)
        xhi[j] = hi
        xlo[j] = lo
        tco[j : j + 1] = cross[j]
        tch[j : j + 1] = crossh[j]
        inverse = 1.0 / (dloc[j : j + 1] + cross[j])
        inverseh = 1.0 / (halo[j][72:73, 0:DOF] + crossh[j])
        rec[j : j + 1] = inverse
        rech[j : j + 1] = inverseh
        qh[j, 0:MROWS] = halo[j][32:72, 0:DOF].astype(bf16)
        qh[j, MROWS:LANES] = jnp.zeros((LANES - MROWS, DOF), bf16)
        cdh[j] = halo[j][0:MROWS, DOF : DOF + LANES]
        xs.append(fine_damping * inverse * bp[j])
        xh.append(fine_damping * inverseh * halo[j][0:COLS, 0:DOF])
    kh = [khi[a] for a in range(AGG)]
    kl = [klo[a] for a in range(AGG)]
    gh, gl = ghi[...], glo[...]
    y = local_product(xs, kh, kl, gh, gl, cross)
    d = []
    for j in range(AGG):
        r1 = bp[j] - y[j] + to_own(xh[j], xhi[j], xlo[j])
        step = fine_damping * rec[j : j + 1] * r1
        d.append(step)
        dlt[j] = step
        x2o[j] = xs[j] + step
        r1o[j] = r1
    y = local_product(d, kh, kl, gh, gl, cross)
    messages = []
    for j in range(AGG):
        part = r1o[j] - y[j]
        pr[j] = part
        pg = mm2(part, qp[j], NT)
        pgo[j] = pg
        messages.append(jnp.concatenate([d[j], pg], axis=1))
    send(parity, messages, oblk1, oblk0, oband1, oband0)


def inverse_kernel(
    qp, qh, dsum, cdh, tco, tch, xhi, xlo, big, inv, invh, cxhi, cxlo, chi, clo, work
):
    whole = big[...]
    ch, cl = split2(whole)
    chi[...] = ch
    clo[...] = cl
    for j in range(AGG):
        own = mm2(qp[j, 0:MROWS].astype(f32) * tco[j : j + 1], qp[j], NT)
        corner = big[j * LANES : j * LANES + MROWS, j * LANES : (j + 1) * LANES] + own
        hi, lo = split2(corner)
        chi[j * LANES : j * LANES + MROWS, j * LANES : (j + 1) * LANES] = hi
        clo[j * LANES : j * LANES + MROWS, j * LANES : (j + 1) * LANES] = lo
        other = mm2(qh[j, 0:MROWS].astype(f32) * tch[j : j + 1], qh[j], NT)
        work[:, j, :] = dsum[j] + own
        work[:, AGG + j, :] = cdh[j] + other
        rows = rows_of(qp[j, 0:MROWS])
        y = lanes_of(dot(rows, xhi[j]) + dot(rows, xlo[j]))
        hi, lo = split2(-mm2(y, qh[j], NT))
        cxhi[j, 0:MROWS] = hi
        cxlo[j, 0:MROWS] = lo
        cxhi[j, MROWS:LANES] = jnp.zeros((LANES - MROWS, LANES), bf16)
        cxlo[j, MROWS:LANES] = jnp.zeros((LANES - MROWS, LANES), bf16)
    lane = iota((8, LANES), 1)
    rows = [work[i] + jnp.where(lane == 64 + i, 1.0, 0.0) for i in range(MODES)]
    for s in range(MODES):
        pivot = jnp.broadcast_to(rows[s][:, s : s + 1], (8, LANES))
        scaled = rows[s] / pivot
        for i in range(MODES):
            if i != s:
                rows[i] = rows[i] - jnp.broadcast_to(rows[i][:, s : s + 1], (8, LANES)) * scaled
        rows[s] = scaled
    for i in range(MODES):
        work[i] = jnp.where(lane < 64, pltpu.roll(rows[i], 64, 1), 0.0)
    for i in range(MODES, MROWS):
        work[i] = jnp.zeros((8, LANES), f32)
    for j in range(AGG):
        inv[j, 0:MROWS] = work[:, j, :]
        invh[j, 0:MROWS] = work[:, AGG + j, :]
        inv[j, MROWS:LANES] = jnp.zeros((LANES - MROWS, LANES), f32)
        invh[j, MROWS:LANES] = jnp.zeros((LANES - MROWS, LANES), f32)


def coarse_local(e, chi, clo):
    y = mm3(jnp.concatenate(e, axis=1), chi, clo)
    return [y[:, a * LANES : (a + 1) * LANES] for a in range(AGG)]


def third_kernel(
    parity, blk1, blk0, band1, band0, pr, pg, dlt, qp, qh, xhi, xlo, inv, invh, chi, clo, cxhi, cxlo,
    oblk1, oblk0, oband1, oband0, r2o, e1o, d1o, pm2o,
):
    halo = receive(parity, blk1, blk0, band1, band0)
    e0, e0h, g = [], [], []
    for j in range(AGG):
        change = to_own(halo[j][:, 0:DOF], xhi[j], xlo[j])
        r2o[j] = pr[j] + change
        g.append(pg[j] + mm2(change, qp[j], NT))
        changeh = to_halo(dlt[j], xhi[j], xlo[j])
        gh = halo[j][:, DOF : DOF + LANES] + mm2(changeh, qh[j], NT)
        e0.append(coarse_damping * exact(g[j], inv[j]))
        e0h.append(coarse_damping * exact(gh, invh[j]))
    ch, cl = chi[...], clo[...]
    applied = coarse_local(e0, ch, cl)
    d1, m1 = [], []
    for j in range(AGG):
        m = g[j] - applied[j] - mm3(e0h[j], cxhi[j], cxlo[j], NT)
        m1.append(m)
        d1.append(coarse_damping * exact(m, inv[j]))
    applied = coarse_local(d1, ch, cl)
    messages = []
    for j in range(AGG):
        part = m1[j] - applied[j]
        pm2o[j] = part
        d1o[j] = d1[j]
        e1o[j] = e0[j] + d1[j]
        messages.append(jnp.concatenate([d1[j], part], axis=1))
    send(parity, messages, oblk1, oblk0, oband1, oband0)


def fourth_kernel(
    parity, blk1, blk0, band1, band0, pm2, d1, e1, inv, invh, chi, clo, cxhi, cxlo,
    x2, r2, qp, khi, klo, ghi, glo, tco,
    oblk1, oblk0, oband1, oband0, x3o, f3o, pr3o,
):
    halo = receive(parity, blk1, blk0, band1, band0)
    d2, d2h, m2 = [], [], []
    for j in range(AGG):
        m = pm2[j] - mm3(halo[j][:, 0:LANES], cxhi[j], cxlo[j], NT)
        mh = halo[j][:, LANES : 2 * LANES] - mm3(d1[j], cxhi[j], cxlo[j])
        m2.append(m)
        d2.append(coarse_damping * exact(m, inv[j]))
        d2h.append(coarse_damping * exact(mh, invh[j]))
    applied = coarse_local(d2, chi[...], clo[...])
    e, f = [], []
    for j in range(AGG):
        m = m2[j] - applied[j] - mm3(d2h[j], cxhi[j], cxlo[j], NT)
        e.append(e1[j] + d2[j] + coarse_damping * exact(m, inv[j]))
        f.append(mm2(e[j], qp[j]))
        f3o[j] = f[j]
        x3o[j] = x2[j] + f[j]
    cross = [tco[j : j + 1] for j in range(AGG)]
    y = local_product(
        f, [khi[a] for a in range(AGG)], [klo[a] for a in range(AGG)], ghi[...], glo[...], cross
    )
    messages = []
    for j in range(AGG):
        part = r2[j] - y[j]
        pr3o[j] = part
        messages.append(jnp.concatenate([part, e[j]], axis=1))
    send(parity, messages, oblk1, oblk0, oband1, oband0)


def last_kernel(
    parity, blk1, blk0, band1, band0, x3, f3, pr3, qh, rec, rech, khi, klo, ghi, glo, tco, xhi, xlo,
    field, residual,
):
    halo = receive(parity, blk1, blk0, band1, band0)
    d4, d4h, r3 = [], [], []
    for j in range(AGG):
        fh = mm2(halo[j][:, DOF : DOF + LANES], qh[j])
        r = pr3[j] + to_own(fh, xhi[j], xlo[j])
        rh = halo[j][:, 0:DOF] + to_halo(f3[j], xhi[j], xlo[j])
        r3.append(r)
        d4.append(fine_damping * rec[j : j + 1] * r)
        d4h.append(fine_damping * rech[j : j + 1] * rh)
    cross = [tco[j : j + 1] for j in range(AGG)]
    y = local_product(
        d4, [khi[a] for a in range(AGG)], [klo[a] for a in range(AGG)], ghi[...], glo[...], cross
    )
    out = []
    for j in range(AGG):
        out.append(x3[j] + d4[j])
    for j in range(AGG):
        out.append(r3[j] - y[j] + to_own(d4h[j], xhi[j], xlo[j]))
    turned = mm_exact(jnp.concatenate(out, axis=0), permutation_back())
    for j in range(AGG):
        field[j] = turned[j * COLS : (j + 1) * COLS]
        residual[j] = turned[(AGG + j) * COLS : (AGG + j + 1) * COLS]


VM = pl.BlockSpec(memory_space=pltpu.VMEM)
SM = pl.BlockSpec(memory_space=pltpu.SMEM)


def run(kernel, outs, *args, scalars=0, scratch=()):
    return pl.pallas_call(
        kernel,
        out_shape=[jax.ShapeDtypeStruct(shape, kind) for shape, kind in outs],
        in_specs=[SM] * scalars + [VM] * (len(args) - scalars),
        out_specs=[VM] * len(outs),
        scratch_shapes=list(scratch),
        compiler_params=pltpu.CompilerParams(vmem_limit_bytes=24 * 2**20),
    )(*args)


def swapped(x, axis, odd):
    length = lax.axis_size(axis)
    route = []
    for i in range(odd, length + odd, 2):
        near, far = i % length, (i + 1) % length
        route += [(near, far), (far, near)]
    return lax.ppermute(x, axis, route)


def exchange(messages):
    blk1, blk0, band1, band0 = messages
    in0 = swapped(band0, "band", 0)
    in1 = swapped(band1, "band", 1)
    in2 = swapped(blk0, "blk", 0)
    in3 = swapped(blk1, "blk", 1)
    return in3, in2, in1, in0


def shards(
    load_columns, stiffness, rigid_modes, neighbours, slot_valid, pair_left, pair_right, penalty
):
    parity = jnp.stack([lax.axis_index("blk") % 2, lax.axis_index("band") % 2]).astype(jnp.int32)
    fields = ((AGG, COLS, DOF), f32)
    modes = ((AGG, LANES, DOF), bf16)
    square = ((AGG, DOF, DOF), bf16)
    local = ((AGG * LANES, AGG * LANES), bf16)
    small = ((AGG, MROWS, LANES), f32)
    tile = ((AGG, LANES, LANES), bf16)
    tile32 = ((AGG, LANES, LANES), f32)
    rows = ((AGG, DOF), f32)
    coarse = ((AGG, COLS, LANES), f32)

    def message(height, width):
        return [((height, width), f32)] * 4

    *out, khi, klo, bp, qp, gal, dsum, dloc, tab = run(
        first_kernel,
        message(80, DOF + LANES)
        + [square, square, fields, modes, small, small, rows, ((24, PAIRS), f32)],
        parity,
        load_columns[0, 0],
        stiffness[0, 0],
        rigid_modes[0, 0],
        neighbours[0, 0],
        slot_valid[0, 0],
        pair_left[0, 0],
        pair_right[0, 0],
        penalty[0, 0],
        scalars=1,
    )
    got = exchange(out)
    pkhi, pklo, ghi, glo, big = run(
        local_kernel,
        [square, square, local, local, ((AGG * LANES, AGG * LANES), f32)],
        khi, klo, qp, gal, tab,
    )
    *out, xhi, xlo, rec, rech, qh, cdh, tco, tch, x2, r1, dlt, pr, pg = run(
        second_kernel,
        message(COLS, DOF + LANES)
        + [tile, tile, rows, rows, modes, small, rows, rows, fields, fields, fields, fields, coarse],
        parity, *got, bp, qp, dloc, tab, pkhi, pklo, ghi, glo,
        scalars=1,
    )
    got = exchange(out)
    inv, invh, cxhi, cxlo, chi, clo = run(
        inverse_kernel,
        [tile32, tile32, tile, tile, local, local],
        qp, qh, dsum, cdh, tco, tch, xhi, xlo, big,
        scratch=[pltpu.VMEM((MROWS, 2 * AGG, LANES), f32)],
    )
    *out, r2, e1, d1, pm2 = run(
        third_kernel,
        message(COLS, 2 * LANES) + [fields, coarse, coarse, coarse],
        parity, *got, pr, pg, dlt, qp, qh, xhi, xlo, inv, invh, chi, clo, cxhi, cxlo,
        scalars=1,
    )
    got = exchange(out)
    *out, x3, f3, pr3 = run(
        fourth_kernel,
        message(COLS, DOF + LANES) + [fields, fields, fields],
        parity, *got, pm2, d1, e1, inv, invh, chi, clo, cxhi, cxlo,
        x2, r2, qp, pkhi, pklo, ghi, glo, tco,
        scalars=1,
    )
    got = exchange(out)
    field, residual = run(
        last_kernel,
        [fields, fields],
        parity, *got, x3, f3, pr3, qh, rec, rech, pkhi, pklo, ghi, glo, tco, xhi, xlo,
        scalars=1,
    )
    return (field[None, None], residual[None, None])


def solution(mesh):
    in_specs = (
        P("band", "blk", None, None, None),
        P("band", "blk", None, None, None),
        P("band", "blk", None, None, None),
        P("band", "blk", None, None),
        P("band", "blk", None, None),
        P("band", "blk", None, None),
        P("band", "blk", None, None),
        P("band", "blk", None, None),
    )
    out_specs = (P("band", "blk", None, None, None), P("band", "blk", None, None, None))
    return jax.shard_map(shards, mesh=mesh, in_specs=in_specs, out_specs=out_specs, check_vma=False)
```

time: 488 us -> 75.8 us (0.16)
  the two profiles are of different devices: /device:TPU:104 before, /device:TPU:32 now
where the time goes in v1:
time: 75.8 us; the launch traced here: 75.5 us
  starting transfers between devices  26.7 us (35%)
  Pallas kernels  26 us (34%)
  waiting for transfers between devices  15 us (20%)
  local copies, waits for them, and re-layouts  6.91 us (9%)
    ppermute x16, starting transfers between devices, swapped(): return lax.ppermute(x, axis, route)  26.7 us
    pallas_call x7, Pallas kernels, run(): pl.pallas_call(kernel, out_shape=[jax.ShapeDtypeStruct(shape, kind) for s...  26 us
    ppermute x16, waiting for transfers between devices, swapped(): return lax.ppermute(x, axis, route)  15 us
    unnamed x15, local copies, waits for them, and re-layouts  6.91 us
  transfers between devices with their start and end apart: 16, of which 8 were waited for; matrix products, arithmetic and copies ran while one was open for 0% of the time, Pallas kernels for 12%

profile of v1, /device:TPU:32, one launch (start us, length us, event | category | flops | bytes accessed | tf_op | source)
XLA Modules:
  0.0 75.5 jit_solution(5875160032992512257)
XLA Ops:
  0.6 0.9 %copy.12 = bf16[1,1,4,36,384]{4,3,2,1,0:T(8,128)(2,1)S(1)} copy(bf16[1,1,4,36,384]{4,2,3,1,0:T(4,128)(2,1)} %param.10) | data formatting | bytes 221184 | tf_op args[2]
  1.6 1.7 %copy-done = f32[1,1,4,384,384]{4,3,2,1,0:T(8,128)S(1)} copy-done((f32[1,1,4,384,384]{4,3,2,1,0:T(8,128)S(1)}, f32[1,1,4,384,384]{4,3,2,1,0:T(8,128)}, u32[]{:S(2)}) %copy-start) | copy-done | bytes 2359320
  3.3 0.9 %copy-done.1 = f32[1,1,4,32,384]{4,3,2,1,0:T(8,128)S(1)} copy-done((f32[1,1,4,32,384]{4,3,2,1,0:T(8,128)S(1)}, f32[1,1,4,32,384]{4,3,2,1,0:T(8,128)}, u32[]{:S(2)}) %copy-start.1) | copy-done | bytes 196632
  4.2 0.7 copy-done.2
  4.9 0.7 copy-done.3
  5.6 0.7 copy-done.4
  6.3 0.7 copy-done.5
  7.0 0.7 copy-done.6
  7.7 2.6 %shard_map.95 = (f32[80,512]{1,0:T(8,128)S(1)}, f32[80,512]{1,0:T(8,128)S(1)}, f32[80,512]{1,0:T(8,128)S(1)}, f32[80,512]{1,0:T(8,128)S(1)}, bf16[4,384,384]{2,1...) custom-call(s32[2]{0:T(128)S(1)} %pad_add_fusion.parity, ...), custom_call_target="tpu_custom_call" | custom-call | tf_op jit(solution)/shard_map/pallas_call | solution.py:506
  10.2 2.7 %collective-permute-start = (f32[80,512]{1,0:T(8,128)S(1)}, f32[80,512]{1,0:T(8,128)S(1)}, u32[]{:S(2)}, u32[]{:S(2)}) collective-permute-start(f32[80,512]{1,0:T(8,128)S(1)} %get-tuple-element.58), channel_id=1, source_target_pairs={{1,2},{2,1},{3,4},{4,3},{5,6},{6,5},{7,8},{8,7},{9,10},{10,9},{11,... | collective-permute-start | bytes 491528 | tf_op jit(solution)/shard_map/ppermute | solution.py:522
  12.9 2.3 %collective-permute-start.1 = (f32[80,512]{1,0:T(8,128)S(1)}, f32[80,512]{1,0:T(8,128)S(1)}, u32[]{:S(2)}, u32[]{:S(2)}) collective-permute-start(f32[80,512]{1,0:T(8,128)S(1)} %get-tuple-element.59), channel_id=1, source_target_pairs={{0,1},{1,0},{2,3},{3,2},{4,5},{5,4},{6,7},{7,6},{8,9},{9,8},{10,11... | collective-permute-start | bytes 491528 | tf_op jit(solution)/shard_map/ppermute | solution.py:522
  15.2 2.8 %collective-permute-start.2 = (f32[80,512]{1,0:T(8,128)S(1)}, f32[80,512]{1,0:T(8,128)S(1)}, u32[]{:S(2)}, u32[]{:S(2)}) collective-permute-start(f32[80,512]{1,0:T(8,128)S(1)} %get-tuple-element.60), channel_id=1, source_target_pairs={{16,32},{32,16},{48,64},{64,48},{80,96},{96,80},{112,128},{128,112... | collective-permute-start | bytes 491528 | tf_op jit(solution)/shard_map/ppermute | solution.py:522
  18.0 5.0 %shard_map.96 = (bf16[4,384,384]{2,1,0:T(8,128)(2,1)S(1)}, bf16[4,384,384]{2,1,0:T(8,128)(2,1)S(1)}, bf16[512,512]{1,0:T(8,128)(2,1)S(1)}, bf16[512,512]{1,0:T(8,128)(2,1)S(1)}, f32[512,512]{1,0:T(8,128)S(1)}) custom-call(bf16[4,384,384]{2,1,0:T(8,128)(2,1)S(1)} %get-tuple-element.66.khi, bf16[4,384,384]{2,1,0:T(8,128)(2,1)S(1)} %get-tuple-element.67.klo, ...), custom_call_target="tpu_custom_call" | custom-call | tf_op jit(solution)/shard_map/pallas_call | solution.py:506
  23.1 5.0 %collective-permute-done.2.band1 = f32[80,512]{1,0:T(8,128)S(1)} collective-permute-done((f32[80,512]{1,0:T(8,128)S(1)}, f32[80,512]{1,0:T(8,128)S(1)}, u32[]{:S(2)}, u32[]{:S(2)}) %collective-permute-start.2) | collective-permute-done | bytes 163872 | tf_op jit(solution)/shard_map/ppermute | solution.py:522
  28.1 3.1 %shard_map.97 = (f32[32,512]{1,0:T(8,128)S(1)}, f32[32,512]{1,0:T(8,128)S(1)}, f32[32,512]{1,0:T(8,128)S(1)}, f32[32,512]{1,0:T(8,128)S(1)}, bf16[4,128,128]{2,1...) custom-call(s32[2]{0:T(128)S(1)} %pad_add_fusion.parity, ...), custom_call_target="tpu_custom_call" | custom-call | tf_op jit(solution)/shard_map/pallas_call | solution.py:506
  31.2 4.0 %collective-permute-start.4 = (f32[32,512]{1,0:T(8,128)S(1)}, f32[32,512]{1,0:T(8,128)S(1)}, u32[]{:S(2)}, u32[]{:S(2)}) collective-permute-start(f32[32,512]{1,0:T(8,128)S(1)} %get-tuple-element.73), channel_id=1, source_target_pairs={{1,2},{2,1},{3,4},{4,3},{5,6},{6,5},{7,8},{8,7},{9,10},{10,9},{11,... | collective-permute-start | bytes 196616 | tf_op jit(solution)/shard_map/ppermute | solution.py:522
  35.3 0.9 %collective-permute-start.5 = (f32[32,512]{1,0:T(8,128)S(1)}, f32[32,512]{1,0:T(8,128)S(1)}, u32[]{:S(2)}, u32[]{:S(2)}) collective-permute-start(f32[32,512]{1,0:T(8,128)S(1)} %get-tuple-element.74), channel_id=1, source_target_pairs={{0,1},{1,0},{2,3},{3,2},{4,5},{5,4},{6,7},{7,6},{8,9},{9,8},{10,11... | collective-permute-start | bytes 196616 | tf_op jit(solution)/shard_map/ppermute | solution.py:522
  36.2 4.1 %shard_map.98 = (f32[4,128,128]{2,1,0:T(8,128)S(1)}, f32[4,128,128]{2,1,0:T(8,128)S(1)}, bf16[4,128,128]{2,1,0:T(8,128)(2,1)S(1)}, bf16[4,128,128]{2,1,0:T(8,128...) custom-call(bf16[4,128,384]{2,1,0:T(8,128)(2,1)S(1)} %get-tuple-element.63.qp, ...), custom_call_target="tpu_custom_call" | custom-call | tf_op jit(solution)/shard_map/pallas_call | solution.py:506
  40.3 0.7 collective-permute-done.5.blk0
  41.0 0.9 %collective-permute-done.6.band1 = f32[32,512]{1,0:T(8,128)S(1)} collective-permute-done((f32[32,512]{1,0:T(8,128)S(1)}, f32[32,512]{1,0:T(8,128)S(1)}, u32[]{:S(2)}, u32[]{:S(2)}) %collective-permute-start.6) | collective-permute-done | bytes 65568 | tf_op jit(solution)/shard_map/ppermute | solution.py:522
  41.9 3.7 %shard_map.99 = (f32[32,256]{1,0:T(8,128)S(1)}, f32[32,256]{1,0:T(8,128)S(1)}, f32[32,256]{1,0:T(8,128)S(1)}, f32[32,256]{1,0:T(8,128)S(1)}, f32[4,32,384]{2,1,0...) custom-call(s32[2]{0:T(128)S(1)} %pad_add_fusion.parity, ...), custom_call_target="tpu_custom_call" | custom-call | tf_op jit(solution)/shard_map/pallas_call | solution.py:506
  45.7 5.6 %collective-permute-start.8 = (f32[32,256]{1,0:T(8,128)S(1)}, f32[32,256]{1,0:T(8,128)S(1)}, u32[]{:S(2)}, u32[]{:S(2)}) collective-permute-start(f32[32,256]{1,0:T(8,128)S(1)} %get-tuple-element.94), channel_id=1, source_target_pairs={{1,2},{2,1},{3,4},{4,3},{5,6},{6,5},{7,8},{8,7},{9,10},{10,9},{11,... | collective-permute-start | bytes 98312 | tf_op jit(solution)/shard_map/ppermute | solution.py:522
  51.8 1.7 %collective-permute-start.10 = (f32[32,256]{1,0:T(8,128)S(1)}, f32[32,256]{1,0:T(8,128)S(1)}, u32[]{:S(2)}, u32[]{:S(2)}) collective-permute-start(f32[32,256]{1,0:T(8,128)S(1)} %get-tuple-element.96), channel_id=1, source_target_pairs={{16,32},{32,16},{48,64},{64,48},{80,96},{96,80},{112,128},{128,112... | collective-permute-start | bytes 98312 | tf_op jit(solution)/shard_map/ppermute | solution.py:522
  53.5 3.1 %collective-permute-done.9.blk0 = f32[32,256]{1,0:T(8,128)S(1)} collective-permute-done((f32[32,256]{1,0:T(8,128)S(1)}, f32[32,256]{1,0:T(8,128)S(1)}, u32[]{:S(2)}, u32[]{:S(2)}) %collective-permute-start.9) | collective-permute-done | bytes 32800 | tf_op jit(solution)/shard_map/ppermute | solution.py:522
  57.3 4.2 %shard_map.100 = (f32[32,512]{1,0:T(8,128)S(1)}, f32[32,512]{1,0:T(8,128)S(1)}, f32[32,512]{1,0:T(8,128)S(1)}, f32[32,512]{1,0:T(8,128)S(1)}, f32[4,32,384]{2,1,...) custom-call(s32[2]{0:T(128)S(1)} %pad_add_fusion.parity, ...), custom_call_target="tpu_custom_call" | custom-call | tf_op jit(solution)/shard_map/pallas_call | solution.py:506
  61.5 3.5 %collective-permute-start.12 = (f32[32,512]{1,0:T(8,128)S(1)}, f32[32,512]{1,0:T(8,128)S(1)}, u32[]{:S(2)}, u32[]{:S(2)}) collective-permute-start(f32[32,512]{1,0:T(8,128)S(1)} %get-tuple-element.103), channel_id=1, source_target_pairs={{1,2},{2,1},{3,4},{4,3},{5,6},{6,5},{7,8},{8,7},{9,10},{10,9},{11,... | collective-permute-start | bytes 196616 | tf_op jit(solution)/shard_map/ppermute | solution.py:522
  65.0 1.5 %collective-permute-start.13 = (f32[32,512]{1,0:T(8,128)S(1)}, f32[32,512]{1,0:T(8,128)S(1)}, u32[]{:S(2)}, u32[]{:S(2)}) collective-permute-start(f32[32,512]{1,0:T(8,128)S(1)} %get-tuple-element.104), channel_id=1, source_target_pairs={{0,1},{1,0},{2,3},{3,2},{4,5},{5,4},{6,7},{7,6},{8,9},{9,8},{10,11... | collective-permute-start | bytes 196616 | tf_op jit(solution)/shard_map/ppermute | solution.py:522
  66.5 1.1 %collective-permute-start.14 = (f32[32,512]{1,0:T(8,128)S(1)}, f32[32,512]{1,0:T(8,128)S(1)}, u32[]{:S(2)}, u32[]{:S(2)}) collective-permute-start(f32[32,512]{1,0:T(8,128)S(1)} %get-tuple-element.105), channel_id=1, source_target_pairs={{16,32},{32,16},{48,64},{64,48},{80,96},{96,80},{112,128},{128,112... | collective-permute-start | bytes 196616 | tf_op jit(solution)/shard_map/ppermute | solution.py:522
  67.6 0.7 collective-permute-done.12.blk1
  68.4 2.4 %collective-permute-done.13.blk0 = f32[32,512]{1,0:T(8,128)S(1)} collective-permute-done((f32[32,512]{1,0:T(8,128)S(1)}, f32[32,512]{1,0:T(8,128)S(1)}, u32[]{:S(2)}, u32[]{:S(2)}) %collective-permute-start.13) | collective-permute-done | bytes 65568 | tf_op jit(solution)/shard_map/ppermute | solution.py:522
  70.7 1.5 %collective-permute-done.14.band1 = f32[32,512]{1,0:T(8,128)S(1)} collective-permute-done((f32[32,512]{1,0:T(8,128)S(1)}, f32[32,512]{1,0:T(8,128)S(1)}, u32[]{:S(2)}, u32[]{:S(2)}) %collective-permute-start.14) | collective-permute-done | bytes 65568 | tf_op jit(solution)/shard_map/ppermute | solution.py:522
  72.3 3.2 %shard_map.101 = (f32[4,32,384]{2,1,0:T(8,128)}, f32[4,32,384]{2,1,0:T(8,128)}) custom-call(s32[2]{0:T(128)S(1)} %pad_add_fusion.parity, f32[32,512]{1,0:T(8,128)S(1)} %collective-permute-done.12.blk1, f32[32,512]{1,0:T(8,128)S(1)} %collective-permute-done.13.blk0, f32[32,512]{1,0:T(8,128)S(1)} %collective-permute-done.14.band1, ...), custom_call_target="tpu_custom_call" | custom-call | tf_op jit(solution)/shard_map/pallas_call | solution.py:506
  (23 shorter events, 1.4 us)
Async XLA Ops:
  1.6 1.7 %copy-start = (f32[1,1,4,384,384]{4,3,2,1,0:T(8,128)S(1)}, f32[1,1,4,384,384]{4,3,2,1,0:T(8,128)}, u32[]{:S(2)}) copy-start(f32[1,1,4,384,384]{4,3,2,1,0:T(8,128)} %param.9) | copy-start | bytes 7077892
  3.3 0.9 %copy-start.1 = (f32[1,1,4,32,384]{4,3,2,1,0:T(8,128)S(1)}, f32[1,1,4,32,384]{4,3,2,1,0:T(8,128)}, u32[]{:S(2)}) copy-start(f32[1,1,4,32,384]{4,3,2,1,0:T(8,128)} %param.8) | copy-start | bytes 589828
  4.2 0.7 copy-start.2
  4.9 0.7 copy-start.3
  5.6 0.7 copy-start.4
  6.3 0.7 copy-start.5
  7.0 0.7 copy-start.6
  10.2 12.8 %collective-permute-start = (f32[80,512]{1,0:T(8,128)S(1)}, f32[80,512]{1,0:T(8,128)S(1)}, u32[]{:S(2)}, u32[]{:S(2)}) collective-permute-start(f32[80,512]{1,0:T(8,128)S(1)} %get-tuple-element.58), channel_id=1, source_target_pairs={{1,2},{2,1},{3,4},{4,3},{5,6},{6,5},{7,8},{8,7},{9,10},{10,9},{11,... | collective-permute-start | bytes 491528 | tf_op jit(solution)/shard_map/ppermute | solution.py:522
  12.9 10.2 %collective-permute-start.1 = (f32[80,512]{1,0:T(8,128)S(1)}, f32[80,512]{1,0:T(8,128)S(1)}, u32[]{:S(2)}, u32[]{:S(2)}) collective-permute-start(f32[80,512]{1,0:T(8,128)S(1)} %get-tuple-element.59), channel_id=1, source_target_pairs={{0,1},{1,0},{2,3},{3,2},{4,5},{5,4},{6,7},{7,6},{8,9},{9,8},{10,11... | collective-permute-start | bytes 491528 | tf_op jit(solution)/shard_map/ppermute | solution.py:522
  15.2 12.9 %collective-permute-start.2 = (f32[80,512]{1,0:T(8,128)S(1)}, f32[80,512]{1,0:T(8,128)S(1)}, u32[]{:S(2)}, u32[]{:S(2)}) collective-permute-start(f32[80,512]{1,0:T(8,128)S(1)} %get-tuple-element.60), channel_id=1, source_target_pairs={{16,32},{32,16},{48,64},{64,48},{80,96},{96,80},{112,128},{128,112... | collective-permute-start | bytes 491528 | tf_op jit(solution)/shard_map/ppermute | solution.py:522
  18.0 10.1 %collective-permute-start.3 = (f32[80,512]{1,0:T(8,128)S(1)}, f32[80,512]{1,0:T(8,128)S(1)}, u32[]{:S(2)}, u32[]{:S(2)}) collective-permute-start(f32[80,512]{1,0:T(8,128)S(1)} %get-tuple-element.61), channel_id=1, source_target_pairs={{0,16},{16,0},{32,48},{48,32},{64,80},{80,64},{96,112},{112,96},{1... | collective-permute-start | bytes 491528 | tf_op jit(solution)/shard_map/ppermute | solution.py:522
  31.2 9.1 %collective-permute-start.4 = (f32[32,512]{1,0:T(8,128)S(1)}, f32[32,512]{1,0:T(8,128)S(1)}, u32[]{:S(2)}, u32[]{:S(2)}) collective-permute-start(f32[32,512]{1,0:T(8,128)S(1)} %get-tuple-element.73), channel_id=1, source_target_pairs={{1,2},{2,1},{3,4},{4,3},{5,6},{6,5},{7,8},{8,7},{9,10},{10,9},{11,... | collective-permute-start | bytes 196616 | tf_op jit(solution)/shard_map/ppermute | solution.py:522
  35.3 5.8 %collective-permute-start.5 = (f32[32,512]{1,0:T(8,128)S(1)}, f32[32,512]{1,0:T(8,128)S(1)}, u32[]{:S(2)}, u32[]{:S(2)}) collective-permute-start(f32[32,512]{1,0:T(8,128)S(1)} %get-tuple-element.74), channel_id=1, source_target_pairs={{0,1},{1,0},{2,3},{3,2},{4,5},{5,4},{6,7},{7,6},{8,9},{9,8},{10,11... | collective-permute-start | bytes 196616 | tf_op jit(solution)/shard_map/ppermute | solution.py:522
  36.1 5.8 %collective-permute-start.6 = (f32[32,512]{1,0:T(8,128)S(1)}, f32[32,512]{1,0:T(8,128)S(1)}, u32[]{:S(2)}, u32[]{:S(2)}) collective-permute-start(f32[32,512]{1,0:T(8,128)S(1)} %get-tuple-element.75), channel_id=1, source_target_pairs={{16,32},{32,16},{48,64},{64,48},{80,96},{96,80},{112,128},{128,112... | collective-permute-start | bytes 196616 | tf_op jit(solution)/shard_map/ppermute | solution.py:522
  36.2 5.7 %collective-permute-start.7 = (f32[32,512]{1,0:T(8,128)S(1)}, f32[32,512]{1,0:T(8,128)S(1)}, u32[]{:S(2)}, u32[]{:S(2)}) collective-permute-start(f32[32,512]{1,0:T(8,128)S(1)} %get-tuple-element.76), channel_id=1, source_target_pairs={{0,16},{16,0},{32,48},{48,32},{64,80},{80,64},{96,112},{112,96},{1... | collective-permute-start | bytes 196616 | tf_op jit(solution)/shard_map/ppermute | solution.py:522
  45.7 7.9 %collective-permute-start.8 = (f32[32,256]{1,0:T(8,128)S(1)}, f32[32,256]{1,0:T(8,128)S(1)}, u32[]{:S(2)}, u32[]{:S(2)}) collective-permute-start(f32[32,256]{1,0:T(8,128)S(1)} %get-tuple-element.94), channel_id=1, source_target_pairs={{1,2},{2,1},{3,4},{4,3},{5,6},{6,5},{7,8},{8,7},{9,10},{10,9},{11,... | collective-permute-start | bytes 98312 | tf_op jit(solution)/shard_map/ppermute | solution.py:522
  51.2 5.4 %collective-permute-start.9 = (f32[32,256]{1,0:T(8,128)S(1)}, f32[32,256]{1,0:T(8,128)S(1)}, u32[]{:S(2)}, u32[]{:S(2)}) collective-permute-start(f32[32,256]{1,0:T(8,128)S(1)} %get-tuple-element.95), channel_id=1, source_target_pairs={{0,1},{1,0},{2,3},{3,2},{4,5},{5,4},{6,7},{7,6},{8,9},{9,8},{10,11... | collective-permute-start | bytes 98312 | tf_op jit(solution)/shard_map/ppermute | solution.py:522
  51.8 5.4 %collective-permute-start.10 = (f32[32,256]{1,0:T(8,128)S(1)}, f32[32,256]{1,0:T(8,128)S(1)}, u32[]{:S(2)}, u32[]{:S(2)}) collective-permute-start(f32[32,256]{1,0:T(8,128)S(1)} %get-tuple-element.96), channel_id=1, source_target_pairs={{16,32},{32,16},{48,64},{64,48},{80,96},{96,80},{112,128},{128,112... | collective-permute-start | bytes 98312 | tf_op jit(solution)/shard_map/ppermute | solution.py:522
  53.5 3.8 %collective-permute-start.11 = (f32[32,256]{1,0:T(8,128)S(1)}, f32[32,256]{1,0:T(8,128)S(1)}, u32[]{:S(2)}, u32[]{:S(2)}) collective-permute-start(f32[32,256]{1,0:T(8,128)S(1)} %get-tuple-element.97), channel_id=1, source_target_pairs={{0,16},{16,0},{32,48},{48,32},{64,80},{80,64},{96,112},{112,96},{1... | collective-permute-start | bytes 98312 | tf_op jit(solution)/shard_map/ppermute | solution.py:522
  61.5 6.9 %collective-permute-start.12 = (f32[32,512]{1,0:T(8,128)S(1)}, f32[32,512]{1,0:T(8,128)S(1)}, u32[]{:S(2)}, u32[]{:S(2)}) collective-permute-start(f32[32,512]{1,0:T(8,128)S(1)} %get-tuple-element.103), channel_id=1, source_target_pairs={{1,2},{2,1},{3,4},{4,3},{5,6},{6,5},{7,8},{8,7},{9,10},{10,9},{11,... | collective-permute-start | bytes 196616 | tf_op jit(solution)/shard_map/ppermute | solution.py:522
  65.0 5.8 %collective-permute-start.13 = (f32[32,512]{1,0:T(8,128)S(1)}, f32[32,512]{1,0:T(8,128)S(1)}, u32[]{:S(2)}, u32[]{:S(2)}) collective-permute-start(f32[32,512]{1,0:T(8,128)S(1)} %get-tuple-element.104), channel_id=1, source_target_pairs={{0,1},{1,0},{2,3},{3,2},{4,5},{5,4},{6,7},{7,6},{8,9},{9,8},{10,11... | collective-permute-start | bytes 196616 | tf_op jit(solution)/shard_map/ppermute | solution.py:522
  66.5 5.8 %collective-permute-start.14 = (f32[32,512]{1,0:T(8,128)S(1)}, f32[32,512]{1,0:T(8,128)S(1)}, u32[]{:S(2)}, u32[]{:S(2)}) collective-permute-start(f32[32,512]{1,0:T(8,128)S(1)} %get-tuple-element.105), channel_id=1, source_target_pairs={{16,32},{32,16},{48,64},{64,48},{80,96},{96,80},{112,128},{128,112... | collective-permute-start | bytes 196616 | tf_op jit(solution)/shard_map/ppermute | solution.py:522
  67.6 4.7 %collective-permute-start.15 = (f32[32,512]{1,0:T(8,128)S(1)}, f32[32,512]{1,0:T(8,128)S(1)}, u32[]{:S(2)}, u32[]{:S(2)}) collective-permute-start(f32[32,512]{1,0:T(8,128)S(1)} %get-tuple-element.106), channel_id=1, source_target_pairs={{0,16},{16,0},{32,48},{48,32},{64,80},{80,64},{96,112},{112,96},{1... | collective-permute-start | bytes 196616 | tf_op jit(solution)/shard_map/ppermute | solution.py:522

commit v2 on v1

v2 whole, which is shorter than its diff:
```python
import jax
import jax.numpy as jnp
from jax import lax
from jax.experimental import pallas as pl
from jax.experimental.pallas import tpu as pltpu
from jax.sharding import PartitionSpec as P

COLS = 32
BLOCKS = 64
DOF = 384
MODES = 36
SLOTS = 8
PAIRS = 128
AGG = 4
LANES = 128
PAIRED = 3
STRIDE = 64
WIDTH = AGG * STRIDE

fine_damping = 0.6
coarse_damping = 0.7
f32 = jnp.float32
bf16 = jnp.bfloat16

NN = (((1,), (0,)), ((), ()))
NT = (((1,), (1,)), ((), ()))


def dot(a, b, dims=NN):
    return lax.dot_general(a, b, dims, preferred_element_type=f32)


def split2(x):
    hi = x.astype(bf16)
    lo = (x - hi.astype(f32)).astype(bf16)
    return hi, lo


def split3(x):
    hi = x.astype(bf16)
    rest = x - hi.astype(f32)
    mid = rest.astype(bf16)
    lo = (rest - mid.astype(f32)).astype(bf16)
    return hi, mid, lo


def mm3(x, whi, wlo, dims=NN):
    rows = x.shape[0]
    hi, lo = split2(x)
    first = dot(jnp.concatenate([hi, lo], axis=0), whi, dims)
    return first[:rows] + first[rows:] + dot(hi, wlo, dims)


def mm2(x, w, dims=NN):
    rows = x.shape[0]
    hi, lo = split2(x)
    both = dot(jnp.concatenate([hi, lo], axis=0), w, dims)
    return both[:rows] + both[rows:]


def mm_exact(x, w, dims=NN):
    rows = x.shape[0]
    parts = dot(jnp.concatenate(split3(x), axis=0), w, dims)
    return parts[:rows] + parts[rows : 2 * rows] + parts[2 * rows :]


def iota(shape, axis):
    return lax.broadcasted_iota(jnp.int32, shape, axis)


def permutation():
    i = iota((DOF, DOF), 0)
    j = iota((DOF, DOF), 1)
    return (i == 6 * (j & 63) + (j >> 6)).astype(f32).astype(bf16)


def permutation_back():
    i = iota((DOF, DOF), 0)
    j = iota((DOF, DOF), 1)
    return (j == 6 * (i & 63) + (i >> 6)).astype(f32).astype(bf16)


def hot_twice(index):
    k = iota((LANES, PAIRS), 0) & 63
    return (k == index.astype(jnp.int32)).astype(f32).astype(bf16)


def hot_paired(index):
    r = iota((LANES, 2 * PAIRS), 0)
    doubled = jnp.concatenate([index.astype(jnp.int32)] * 2, axis=1)
    want = doubled + 64 * (iota((1, 2 * PAIRS), 1) >> 7)
    return (r == want).astype(f32).astype(bf16)


def wide(t):
    return jnp.concatenate([t] * PAIRED, axis=1)


def stack_fields(v):
    rows = []
    for m in range(PAIRED):
        rows.append(jnp.concatenate([x[:, m * LANES : (m + 1) * LANES] for x in v], axis=1))
    return jnp.concatenate(rows, axis=0)


def unstack_fields(y, count):
    out = []
    for a in range(count):
        parts = [
            y[m * COLS : (m + 1) * COLS, a * LANES : (a + 1) * LANES] for m in range(PAIRED)
        ]
        out.append(jnp.concatenate(parts, axis=1))
    return out


def rows_of(x):
    return jnp.concatenate([x[:, m * LANES : (m + 1) * LANES] for m in range(PAIRED)], axis=0)


def lanes_of(x):
    r = x.shape[0] // PAIRED
    return jnp.concatenate([x[m * r : (m + 1) * r] for m in range(PAIRED)], axis=1)


def local_product(v, khi, klo, ghi, glo, cross):
    springs = unstack_fields(mm3(stack_fields(v), ghi, glo), AGG)
    return [
        mm3(v[a], khi[a], klo[a]) + (springs[a] + v[a] * cross[a]) for a in range(AGG)
    ]


def to_own(vh, xhi, xlo):
    return lanes_of(mm3(rows_of(vh), xhi, xlo, NT))


def to_halo(v, xhi, xlo):
    return lanes_of(mm3(rows_of(v), xhi, xlo))


def pick(flag, a, b):
    return jnp.where(flag, a, b)


def send(parity, message, blk1, blk0, band1, band0):
    odd_s = parity[0] == 1
    odd_b = parity[1] == 1
    blk1[...] = pick(odd_s, message[2], message[0])
    blk0[...] = pick(odd_s, message[0], message[2])
    band1[...] = pick(odd_b, message[3], message[1])
    band0[...] = pick(odd_b, message[1], message[3])


def receive(parity, blk1, blk0, band1, band0):
    odd_s = parity[0] == 1
    odd_b = parity[1] == 1
    blk1, blk0, band1, band0 = blk1[...], blk0[...], band1[...], band0[...]
    return [
        pick(odd_s, blk0, blk1),
        pick(odd_b, band0, band1),
        pick(odd_s, blk1, blk0),
        pick(odd_b, band1, band0),
    ]


def block_diagonal(blocks):
    rows = []
    for j in range(AGG):
        parts = []
        if j > 0:
            parts.append(jnp.zeros((STRIDE, j * STRIDE), f32))
        parts.append(blocks[j])
        if j < AGG - 1:
            parts.append(jnp.zeros((STRIDE, (AGG - 1 - j) * STRIDE), f32))
        rows.append(jnp.concatenate(parts, axis=1))
    return jnp.concatenate(rows, axis=0)


def store2(hi_ref, lo_ref, x):
    hi, lo = split2(x)
    hi_ref[...] = hi
    lo_ref[...] = lo


def sent_modes(sent):
    pad = jnp.zeros((STRIDE - MODES, DOF), f32)
    return jnp.concatenate([sent[32:68], pad], axis=0).astype(bf16)


def sent_diagonal(sent):
    tail = sent[72:80]
    return jnp.concatenate([tail[:, t * STRIDE : (t + 1) * STRIDE] for t in range(5)], axis=0)


def pair_weights(own, far, w, xhi, xlo, j):
    w3 = jnp.concatenate(split3(w), axis=0)
    total = wide(jnp.sum(dot(w3, hot_twice(own), NT), axis=0, keepdims=True))
    total_far = wide(jnp.sum(dot(w3, hot_twice(far), NT), axis=0, keepdims=True))
    near = hot_paired(own)
    hi, mid, lo = split3(jnp.concatenate([w, w], axis=1))
    m = dot(jnp.concatenate([near * hi, near * mid, near * lo], axis=0), hot_paired(far), NT)
    m = m[0:LANES] + m[LANES : 2 * LANES] + m[2 * LANES :]
    hi, lo = split2(m)
    xhi[j] = hi
    xlo[j] = lo
    return total, total_far


def first_kernel(
    parity, b_in, k_in, q_in, nb_in, valid_in, left_in, right_in, penalty_in,
    blk1, blk0, band1, band0, tab,
    b, k, q, nb, valid, left, right, penalty, sem,
):
    small = [
        pltpu.make_async_copy(src, dst, sem.at[n])
        for n, (src, dst) in enumerate(
            [
                (nb_in, nb),
                (valid_in, valid),
                (left_in, left),
                (right_in, right),
                (penalty_in, penalty),
                (q_in, q),
                (b_in, b),
            ]
        )
    ]
    large = [pltpu.make_async_copy(k_in.at[a], k.at[a], sem.at[8 + a]) for a in range(AGG)]
    for copy in small + large:
        copy.start()
    perm = permutation()
    for copy in small:
        copy.wait()

    expand = (iota((SLOTS, PAIRS), 0) == (iota((SLOTS, PAIRS), 1) >> 4)).astype(f32)
    slot = dot(nb[...].astype(f32), expand)
    weight = penalty[...] * dot(valid[...].astype(f32), expand)
    crossing = slot > 3.5
    lf = left[...].astype(f32)
    rf = right[...].astype(f32)
    far = slot * 64.0 + rf
    wloc = jnp.where(crossing, 0.0, weight)
    wcross = jnp.where(crossing, weight, 0.0)
    tab[0:4] = lf
    tab[4:8] = rf
    tab[8:12] = far
    tab[12:16] = wloc
    tab[16:20] = wcross

    near = []
    arrive = jnp.zeros((1, AGG * LANES), f32)
    rr = iota((AGG * LANES, PAIRS), 0)
    row = (rr >> 7) * 64 + (rr & 63)
    for a in range(AGG):
        w3 = jnp.concatenate(split3(wloc[a : a + 1]), axis=0)
        near.append(jnp.sum(dot(w3, hot_twice(lf[a : a + 1]), NT), axis=0, keepdims=True))
        hot = (row == far[a : a + 1].astype(jnp.int32)).astype(f32).astype(bf16)
        arrive = arrive + jnp.sum(dot(w3, hot, NT), axis=0, keepdims=True)
    totals = []
    for a in range(AGG):
        total = near[a] + arrive[:, a * LANES : (a + 1) * LANES]
        tab[20 + a : 21 + a] = total
        totals.append(wide(total))

    pad = jnp.zeros((STRIDE - MODES, DOF), f32)
    q_all = q[...].astype(f32)
    modes = [jnp.concatenate([q_all[:, a, :], pad], axis=0).astype(bf16) for a in range(AGG)]
    turned_modes = dot(jnp.concatenate(modes, axis=0), perm)
    turned_modes = [turned_modes[a * STRIDE : (a + 1) * STRIDE] for a in range(AGG)]
    eye = iota((LANES, LANES), 0) == iota((LANES, LANES), 1)
    diagonals = []
    for a in range(AGG):
        large[a].wait()
        cuts = []
        for m in range(PAIRED):
            tile = k[a, m * LANES : (m + 1) * LANES, m * LANES : (m + 1) * LANES]
            cuts.append(jnp.sum(jnp.where(eye, tile, 0.0), axis=0, keepdims=True))
        diagonals.append(jnp.concatenate(cuts, axis=1))
    stacked = jnp.concatenate(
        [b[a] for a in range(AGG)] + diagonals + [jnp.zeros((4, DOF), f32)], axis=0
    )
    turned = mm_exact(stacked, perm)
    messages = []
    for a in range(AGG):
        load = turned[a * COLS : (a + 1) * COLS]
        diagonal = turned[AGG * COLS + a : AGG * COLS + a + 1] + totals[a]
        hi, lo = split2(k[a])
        projected = dot(modes[a], hi) + dot(modes[a], lo)
        galerkin = mm2(projected, modes[a], NT)
        whole = galerkin + mm2(turned_modes[a] * totals[a], turned_modes[a].astype(bf16), NT)
        table = jnp.concatenate([lf[a : a + 1], rf[a : a + 1], wcross[a : a + 1]], axis=1)
        side = [whole[8 * t : 8 * t + 8] for t in range(5)] + [jnp.zeros((8, STRIDE), f32)]
        messages.append(
            jnp.concatenate(
                [
                    load,
                    turned_modes[a][0:32],
                    jnp.concatenate([turned_modes[a][32:36], diagonal, table], axis=0),
                    jnp.zeros((2, DOF), f32),
                    jnp.concatenate(side, axis=1),
                ],
                axis=0,
            )
        )
    send(parity, messages, blk1, blk0, band1, band0)


def local_kernel(
    parity, blk1, blk0, band1, band0, k, tab,
    pkhi, pklo, ghi, glo, aqhi, aqlo, big, xhi, xlo, tco, tch, bp, qp, dsum, dloc, work,
):
    for a, sent in enumerate(receive(parity, blk1, blk0, band1, band0)):
        bp[a] = sent[0:COLS]
        qp[a] = sent_modes(sent)
        dsum[a] = sent_diagonal(sent)
        dloc[a : a + 1] = sent[68:69]
    perm = permutation()
    back = permutation_back()
    for a in range(AGG):
        hi, lo = split2(k[a])
        pkhi[a] = dot(back, dot(hi, perm).astype(bf16)).astype(bf16)
        pklo[a] = dot(back, dot(lo, perm).astype(bf16)).astype(bf16)
    r = iota((AGG * LANES, 2 * PAIRS), 0)
    shift = 64 * (iota((1, 2 * PAIRS), 1) >> 7)
    rows = []
    for a in range(AGG):
        fi = tab[8 + a : 9 + a].astype(jnp.int32)
        fi = (fi >> 6) * LANES + (fi & 63)
        f2 = jnp.concatenate([fi] * 2, axis=1) + shift
        w2 = jnp.concatenate([tab[12 + a : 13 + a]] * 2, axis=1)
        far = (r == f2).astype(f32).astype(bf16)
        hi, mid, lo = split3(w2)
        near = hot_paired(tab[a : a + 1])
        parts = jnp.concatenate([near * hi, near * mid, near * lo], axis=0)
        m = dot(parts, far, NT)
        rows.append(m[0:LANES] + m[LANES : 2 * LANES] + m[2 * LANES :])
    mm = jnp.concatenate(rows, axis=0)
    work[...] = mm + mm.T
    eye = iota((AGG * LANES, AGG * LANES), 0) == iota((AGG * LANES, AGG * LANES), 1)
    total = jnp.concatenate([tab[20 + a : 21 + a] for a in range(AGG)], axis=1)
    gh, gl = split2(jnp.where(eye, total, 0.0) - work[...])
    ghi[...] = gh
    glo[...] = gl
    lines = []
    for a in range(AGG):
        rows = rows_of(qp[a].astype(f32)).astype(bf16)
        y = dot(rows, gh[a * LANES : (a + 1) * LANES]) + dot(rows, gl[a * LANES : (a + 1) * LANES])
        turned = dot(qp[a], pkhi[a]) + dot(qp[a], pklo[a])
        parts = []
        for c in range(AGG):
            part = lanes_of(y[:, c * LANES : (c + 1) * LANES])
            parts.append(part + turned if c == a else part)
        lines.append(jnp.concatenate(parts, axis=1))
    aq = jnp.concatenate(lines, axis=0)
    ah, al = split2(aq)
    aqhi[...] = ah
    aqlo[...] = al
    columns = []
    for a in range(AGG):
        both = jnp.concatenate([ah, al], axis=0)[:, a * DOF : (a + 1) * DOF]
        block = dot(both, qp[a], NT)
        columns.append(block[:WIDTH] + block[WIDTH:])
    big[...] = jnp.concatenate(columns, axis=1)
    for j in range(2, AGG):
        tco[j : j + 1], tch[j : j + 1] = pair_weights(
            tab[j : j + 1], tab[4 + j : 5 + j], tab[16 + j : 17 + j], xhi, xlo, j - 2
        )
    tco[0:2] = jnp.zeros((2, DOF), f32)
    tch[0:2] = jnp.zeros((2, DOF), f32)


def second_kernel(
    parity, blk1, blk0, band1, band0, bp, qp, dloc, khi, klo, ghi, glo, aqhi, aqlo, x2hi, x2lo, t2o, t2h,
    oblk1, oblk0, oband1, oband0, xhi, xlo, rec, rech, qh, cdh, tco, tch, x2o, r1o, dlt, pgo,
):
    halo = receive(parity, blk1, blk0, band1, band0)
    cross, xs, xh = [], [], []
    for j in range(AGG):
        if j < 2:
            table = halo[j][69:70]
            total, total_far = pair_weights(
                table[:, PAIRS : 2 * PAIRS], table[:, 0:PAIRS], table[:, 2 * PAIRS :], xhi, xlo, j
            )
        else:
            xhi[j] = x2hi[j - 2]
            xlo[j] = x2lo[j - 2]
            total, total_far = t2o[j : j + 1], t2h[j : j + 1]
        cross.append(total)
        tco[j : j + 1] = total
        tch[j : j + 1] = total_far
        inverse = fine_damping / (dloc[j : j + 1] + total)
        inverseh = fine_damping / (halo[j][68:69] + total_far)
        rec[j : j + 1] = inverse
        rech[j : j + 1] = inverseh
        qh[j] = sent_modes(halo[j])
        cdh[j] = sent_diagonal(halo[j])
        xs.append(inverse * bp[j])
        xh.append(inverseh * halo[j][0:COLS])
    kh = [khi[a] for a in range(AGG)]
    kl = [klo[a] for a in range(AGG)]
    y = local_product(xs, kh, kl, ghi[...], glo[...], cross)
    d, pg = [], []
    for j in range(AGG):
        r1 = bp[j] - y[j] + to_own(xh[j], xhi[j], xlo[j])
        step = rec[j : j + 1] * r1
        d.append(step)
        dlt[j] = step
        x2o[j] = xs[j] + step
        r1o[j] = r1
        pg.append(mm2(r1 - step * cross[j], qp[j], NT))
    pg = jnp.concatenate(pg, axis=1) - mm3(jnp.concatenate(d, axis=1), aqhi[...], aqlo[...], NT)
    pgo[...] = pg
    messages = []
    for j in range(AGG):
        part = pg[:, j * STRIDE : (j + 1) * STRIDE]
        messages.append(jnp.concatenate([d[j], part, jnp.zeros((COLS, STRIDE), f32)], axis=1))
    send(parity, messages, oblk1, oblk0, oband1, oband0)


def inverse_kernel(
    dlt, r1, khi, klo, ghi, glo, qp, qh, dsum, cdh, tco, tch, xhi, xlo, big,
    pr, yhi, ylo, zhi, zlo, ghp, hhi, hlo, hhhi, hhlo, gchi, gclo, gxhi, gxlo, gohi, golo, work,
):
    d = [dlt[j] for j in range(AGG)]
    cross = [tco[j : j + 1] for j in range(AGG)]
    y = local_product(
        d, [khi[a] for a in range(AGG)], [klo[a] for a in range(AGG)], ghi[...], glo[...], cross
    )
    for j in range(AGG):
        pr[j] = r1[j] - y[j]
    corner, couple, part = [], [], []
    for j in range(AGG):
        mine = qp[j].astype(f32)
        other = qh[j].astype(f32)
        rows = rows_of(mine).astype(bf16)
        y = lanes_of(dot(rows, xhi[j]) + dot(rows, xlo[j]))
        hi, lo = split2(y)
        yhi[j] = hi
        ylo[j] = lo
        couple.append(-(dot(hi, qh[j], NT) + dot(lo, qh[j], NT)))
        rows = rows_of(other).astype(bf16)
        z = lanes_of(dot(rows, xhi[j], NT) + dot(rows, xlo[j], NT))
        hi, lo = split2(z)
        zhi[j] = hi
        zlo[j] = lo
        part.append(mm3(d[j], hi, lo, NT))
        own = mm2(mine * tco[j : j + 1], qp[j], NT)
        corner.append(own)
        blank = jnp.zeros((MODES, LANES - STRIDE), f32)
        work[:, j, :] = jnp.concatenate([dsum[j][0:MODES] + own[0:MODES], blank], axis=1)
        far = mm2(other * tch[j : j + 1], qh[j], NT)
        work[:, AGG + j, :] = jnp.concatenate([cdh[j][0:MODES] + far[0:MODES], blank], axis=1)
    ghp[...] = jnp.concatenate(part, axis=1)
    lane = iota((8, LANES), 1)
    rows = [work[i] + jnp.where(lane == STRIDE + i, 1.0, 0.0) for i in range(MODES)]
    for s in range(MODES):
        pivot = jnp.broadcast_to(rows[s][:, s : s + 1], (8, LANES))
        scaled = rows[s] / pivot
        for i in range(MODES):
            if i != s:
                rows[i] = rows[i] - jnp.broadcast_to(rows[i][:, s : s + 1], (8, LANES)) * scaled
        rows[s] = scaled
    for i in range(MODES):
        work[i] = rows[i] * coarse_damping
    below = jnp.zeros((STRIDE - MODES, STRIDE), f32)
    blocks = [
        jnp.concatenate([work[:, m, :][:, STRIDE:], below], axis=0) for m in range(2 * AGG)
    ]
    hh, hl = split2(block_diagonal(blocks[:AGG]))
    hhi[...] = hh
    hlo[...] = hl
    fh, fl = split2(block_diagonal(blocks[AGG:]))
    hhhi[...] = fh
    hhlo[...] = fl
    eye = iota((WIDTH, WIDTH), 0) == iota((WIDTH, WIDTH), 1)
    whole = big[...] + block_diagonal(corner)
    store2(gchi, gclo, jnp.where(eye, 1.0, 0.0) - mm3(whole, hh, hl))
    store2(gxhi, gxlo, -mm3(block_diagonal([c.T for c in couple]), hh, hl))
    store2(gohi, golo, -mm3(block_diagonal(couple), fh, fl))


def halo_modes(halo, at):
    return jnp.concatenate([h[:, at : at + STRIDE] for h in halo], axis=1)


def third_kernel(
    parity, blk1, blk0, band1, band0, pg, ghp, yhi, ylo, hhi, hlo, hhhi, hhlo, gchi, gclo, gxhi, gxlo,
    oblk1, oblk0, oband1, oband0, e1o, d1o, p2o, dh,
):
    halo = receive(parity, blk1, blk0, band1, band0)
    parts = []
    for j in range(AGG):
        value = halo[j][:, 0:DOF]
        dh[j] = value
        parts.append(mm3(value, yhi[j], ylo[j], NT))
    g = pg[...] + jnp.concatenate(parts, axis=1)
    gh = halo_modes(halo, DOF) + ghp[...]
    e0 = mm3(g, hhi[...], hlo[...])
    e0h = mm3(gh, hhhi[...], hhlo[...])
    gch, gcl = gchi[...], gclo[...]
    d1 = mm3(e0, gch, gcl) + mm3(e0h, gxhi[...], gxlo[...])
    p2 = mm3(d1, gch, gcl)
    e1o[...] = e0 + d1
    d1o[...] = d1
    p2o[...] = p2
    messages = []
    for j in range(AGG):
        cut = slice(j * STRIDE, (j + 1) * STRIDE)
        messages.append(jnp.concatenate([d1[:, cut], p2[:, cut]], axis=1))
    send(parity, messages, oblk1, oblk0, oband1, oband0)


def beside_third_kernel(dh, pr, xhi, xlo, d1, gohi, golo, r2o, w2o):
    w2o[...] = mm3(d1[...], gohi[...], golo[...])
    for j in range(AGG):
        r2o[j] = pr[j] + to_own(dh[j], xhi[j], xlo[j])


def fourth_kernel(
    parity, blk1, blk0, band1, band0, p2, w2, e1, gchi, gclo, gxhi, gxlo, r2, qp, aqhi, aqlo, tco,
    oblk1, oblk0, oband1, oband0, eo, f3o, pr3o,
):
    halo = receive(parity, blk1, blk0, band1, band0)
    gxh, gxl = gxhi[...], gxlo[...]
    d2 = p2[...] + mm3(halo_modes(halo, 0), gxh, gxl)
    d2h = halo_modes(halo, STRIDE) + w2[...]
    d3 = mm3(d2, gchi[...], gclo[...]) + mm3(d2h, gxh, gxl)
    e = e1[...] + d2 + d3
    eo[...] = e
    y = mm3(e, aqhi[...], aqlo[...])
    messages = []
    for j in range(AGG):
        mine = e[:, j * STRIDE : (j + 1) * STRIDE]
        f = mm2(mine, qp[j])
        f3o[j] = f
        part = r2[j] - y[:, j * DOF : (j + 1) * DOF] - f * tco[j : j + 1]
        pr3o[j] = part
        messages.append(jnp.concatenate([part, mine, jnp.zeros((COLS, STRIDE), f32)], axis=1))
    send(parity, messages, oblk1, oblk0, oband1, oband0)


def beside_fourth_kernel(e, x2, f3, yhi, ylo, x3o, rho):
    for j in range(AGG):
        x3o[j] = x2[j] + f3[j]
        rho[j] = mm3(e[:, j * STRIDE : (j + 1) * STRIDE], yhi[j], ylo[j])


def last_kernel(
    parity, blk1, blk0, band1, band0, x3, pr3, rh3, zhi, zlo, rec, rech, khi, klo, ghi, glo, tco, xhi, xlo,
    field, residual,
):
    halo = receive(parity, blk1, blk0, band1, band0)
    d4, d4h, r3 = [], [], []
    for j in range(AGG):
        r = pr3[j] + mm3(halo[j][:, DOF : DOF + STRIDE], zhi[j], zlo[j])
        rh = halo[j][:, 0:DOF] + rh3[j]
        r3.append(r)
        d4.append(rec[j : j + 1] * r)
        d4h.append(rech[j : j + 1] * rh)
    cross = [tco[j : j + 1] for j in range(AGG)]
    y = local_product(
        d4, [khi[a] for a in range(AGG)], [klo[a] for a in range(AGG)], ghi[...], glo[...], cross
    )
    out = []
    for j in range(AGG):
        out.append(x3[j] + d4[j])
    for j in range(AGG):
        out.append(r3[j] - y[j] + to_own(d4h[j], xhi[j], xlo[j]))
    turned = mm_exact(jnp.concatenate(out, axis=0), permutation_back())
    for j in range(AGG):
        field[j] = turned[j * COLS : (j + 1) * COLS]
        residual[j] = turned[(AGG + j) * COLS : (AGG + j + 1) * COLS]


VM = pl.BlockSpec(memory_space=pltpu.VMEM)
SM = pl.BlockSpec(memory_space=pltpu.SMEM)
HB = pl.BlockSpec(memory_space=pltpu.HBM)


def run(kernel, outs, *args, scalars=0, scratch=(), place=VM, limit=24):
    if place is HB:
        args = args[:scalars] + tuple(
            pltpu.with_memory_space_constraint(x, pltpu.HBM) for x in args[scalars:]
        )
    return pl.pallas_call(
        kernel,
        out_shape=[jax.ShapeDtypeStruct(shape, kind) for shape, kind in outs],
        in_specs=[SM] * scalars + [place] * (len(args) - scalars),
        out_specs=[VM] * len(outs),
        scratch_shapes=list(scratch),
        compiler_params=pltpu.CompilerParams(vmem_limit_bytes=int(limit * 2**20)),
    )(*args)


def swapped(x, axis, odd):
    length = lax.axis_size(axis)
    route = []
    for i in range(odd, length + odd, 2):
        near, far = i % length, (i + 1) % length
        route += [(near, far), (far, near)]
    return lax.ppermute(x, axis, route)


def exchange(messages):
    blk1, blk0, band1, band0 = messages
    in0 = swapped(band0, "band", 0)
    in1 = swapped(band1, "band", 1)
    in2 = swapped(blk0, "blk", 0)
    in3 = swapped(blk1, "blk", 1)
    return in3, in2, in1, in0


def shards(
    load_columns, stiffness, rigid_modes, neighbours, slot_valid, pair_left, pair_right, penalty
):
    parity = jnp.stack([lax.axis_index("blk") % 2, lax.axis_index("band") % 2]).astype(jnp.int32)
    fields = ((AGG, COLS, DOF), f32)
    modes = ((AGG, STRIDE, DOF), bf16)
    square = ((AGG, DOF, DOF), bf16)
    local = ((AGG * LANES, AGG * LANES), bf16)
    small = ((AGG, 40, STRIDE), f32)
    tile = ((AGG, LANES, LANES), bf16)
    rows = ((AGG, DOF), f32)
    coarse = ((COLS, WIDTH), f32)
    broad = ((WIDTH, AGG * DOF), bf16)
    dense = ((WIDTH, WIDTH), bf16)

    def message(height, width):
        return [((height, width), f32)] * 4

    *out, tab = run(
        first_kernel,
        message(80, DOF) + [((24, PAIRS), f32)],
        parity,
        load_columns[0, 0],
        stiffness[0, 0],
        jnp.transpose(rigid_modes[0, 0], (1, 0, 2)),
        neighbours[0, 0],
        slot_valid[0, 0],
        pair_left[0, 0],
        pair_right[0, 0],
        penalty[0, 0],
        scalars=1,
        place=HB,
        scratch=[
            pltpu.VMEM((AGG, COLS, DOF), f32),
            pltpu.VMEM((AGG, DOF, DOF), f32),
            pltpu.VMEM((MODES, AGG, DOF), bf16),
            pltpu.VMEM((AGG, SLOTS), jnp.int32),
            pltpu.VMEM((AGG, SLOTS), jnp.int32),
            pltpu.VMEM((AGG, PAIRS), jnp.int32),
            pltpu.VMEM((AGG, PAIRS), jnp.int32),
            pltpu.VMEM((AGG, PAIRS), f32),
            pltpu.SemaphoreType.DMA((12,)),
        ],
    )
    got = exchange(out)
    pair_tile = ((2, LANES, LANES), bf16)
    pkhi, pklo, ghi, glo, aqhi, aqlo, big, x2hi, x2lo, t2o, t2h, bp, qp, dsum, dloc = run(
        local_kernel,
        [square, square, local, local, broad, broad, ((WIDTH, WIDTH), f32), pair_tile, pair_tile, rows, rows]
        + [fields, modes, small, rows],
        parity, *out, stiffness[0, 0], tab,
        scalars=1,
        scratch=[pltpu.VMEM((AGG * LANES, AGG * LANES), f32)],
    )
    *out, xhi, xlo, rec, rech, qh, cdh, tco, tch, x2, r1, dlt, pg = run(
        second_kernel,
        message(COLS, DOF + LANES)
        + [tile, tile, rows, rows, modes, small, rows, rows, fields, fields, fields, coarse],
        parity, *got, bp, qp, dloc, pkhi, pklo, ghi, glo, aqhi, aqlo, x2hi, x2lo, t2o, t2h,
        scalars=1,
    )
    got = exchange(out)
    pr, yhi, ylo, zhi, zlo, ghp, hhi, hlo, hhhi, hhlo, gchi, gclo, gxhi, gxlo, gohi, golo = run(
        inverse_kernel,
        [fields, modes, modes, modes, modes, coarse] + [dense] * 10,
        dlt, r1, pkhi, pklo, ghi, glo, qp, qh, dsum, cdh, tco, tch, xhi, xlo, big,
        scratch=[pltpu.VMEM((MODES, 2 * AGG, LANES), f32)],
    )
    *out, e1, d1, p2, dh = run(
        third_kernel,
        message(COLS, LANES) + [coarse, coarse, coarse, fields],
        parity, *got, pg, ghp, yhi, ylo, hhi, hlo, hhhi, hhlo, gchi, gclo, gxhi, gxlo,
        scalars=1,
    )
    got = exchange(out)
    r2, w2 = run(beside_third_kernel, [fields, coarse], dh, pr, xhi, xlo, d1, gohi, golo)
    *out, e, f3, pr3 = run(
        fourth_kernel,
        message(COLS, DOF + LANES) + [coarse, fields, fields],
        parity, *got, p2, w2, e1, gchi, gclo, gxhi, gxlo, r2, qp, aqhi, aqlo, tco,
        scalars=1,
    )
    got = exchange(out)
    x3, rh3 = run(beside_fourth_kernel, [fields, fields], e, x2, f3, yhi, ylo)
    field, residual = run(
        last_kernel,
        [fields, fields],
        parity, *got, x3, pr3, rh3, zhi, zlo, rec, rech, pkhi, pklo, ghi, glo, tco, xhi, xlo,
        scalars=1,
    )
    return (field[None, None], residual[None, None])


def solution(mesh):
    in_specs = (
        P("band", "blk", None, None, None),
        P("band", "blk", None, None, None),
        P("band", "blk", None, None, None),
        P("band", "blk", None, None),
        P("band", "blk", None, None),
        P("band", "blk", None, None),
        P("band", "blk", None, None),
        P("band", "blk", None, None),
    )
    out_specs = (P("band", "blk", None, None, None), P("band", "blk", None, None, None))
    return jax.shard_map(shards, mesh=mesh, in_specs=in_specs, out_specs=out_specs, check_vma=False)
```

time: 75.8 us -> 63.6 us (0.84)
  waiting for transfers between devices: 15 us -> 6.05 us
  local copies, waits for them, and re-layouts: 6.91 us -> 0.01 us
  starting transfers between devices: 26.7 us -> 29.9 us
    ppermute x16, waiting for transfers between devices: 15 us -> 6.05 us  [swapped(): return lax.ppermute(x, axis, route)]
    unnamed x15 -> x2, local copies, waits for them, and re-layouts: 6.91 us -> 0.01 us
    ppermute x16, starting transfers between devices: 26.7 us -> 29.9 us  [swapped(): return lax.ppermute(x, axis, route)]
    pallas_call x7 -> x9, Pallas kernels: 26 us -> 25.9 us  [run(): pl.pallas_call(kernel, out_shape=[jax.ShapeDtypeStruct(shape, kind) for s...]
  transfers between devices with their start and end apart: 16 -> 16, of which waited for: 8 -> 5; matrix products, arithmetic and copies ran while one was open for 0% -> 0% of each run, Pallas kernels for 12% -> 21%
where the time goes in v2:
time: 63.6 us; the launch traced here: 62.7 us
  starting transfers between devices  29.9 us (47%)
  Pallas kernels  25.9 us (41%)
  waiting for transfers between devices  6.05 us (10%)
  between operations  0.77 us (1%)
    ppermute x16, starting transfers between devices, swapped(): return lax.ppermute(x, axis, route)  29.9 us
    pallas_call x9, Pallas kernels, run(): pl.pallas_call(kernel, out_shape=[jax.ShapeDtypeStruct(shape, kind) for s...  25.9 us
    ppermute x16, waiting for transfers between devices, swapped(): return lax.ppermute(x, axis, route)  6.05 us
  transfers between devices with their start and end apart: 16, of which 5 were waited for; matrix products, arithmetic and copies ran while one was open for 0% of the time, Pallas kernels for 21%

profile of v2, /device:TPU:32, one launch (start us, length us, event | category | flops | bytes accessed | tf_op | source)
XLA Modules:
  0.0 62.7 jit_solution(2673461108696178480)
XLA Ops:
  0.6 0.1 pad_add_fusion.parity
  0.7 4.0 %shard_map.95 = (f32[80,384]{1,0:T(8,128)S(1)}, f32[80,384]{1,0:T(8,128)S(1)}, f32[80,384]{1,0:T(8,128)S(1)}, f32[80,384]{1,0:T(8,128)S(1)}, f32[24,128]{1,0:T(8,128)S(1)}) custom-call(s32[2]{0:T(128)S(1)} %pad_add_fusion.parity, f32[4,32,384]{2,1,0:T(8,128)} %bitcast.16, f32[4,384,384]{2,1,0:T(8,128)} %bitcast.14, bf16[36,4,384]{2,1,0:T(4,128)(2,1)} %bitcast.17, ...), custom_call_target="tpu_custom_call" | custom-call | tf_op jit(solution)/shard_map/pallas_call | solution.py:584
  4.7 2.7 %collective-permute-start = (f32[80,384]{1,0:T(8,128)S(1)}, f32[80,384]{1,0:T(8,128)S(1)}, u32[]{:S(2)}, u32[]{:S(2)}) collective-permute-start(f32[80,384]{1,0:T(8,128)S(1)} %get-tuple-element.75.blk1), channel_id=1, source_target_pairs={{1,2},{2,1},{3,4},{4,3},{5,6},{6,5},{7,8},{8,7},{9,10},{10,9},{11,... | collective-permute-start | bytes 368648 | tf_op jit(solution)/shard_map/ppermute | solution.py:600
  7.4 2.3 %collective-permute-start.1 = (f32[80,384]{1,0:T(8,128)S(1)}, f32[80,384]{1,0:T(8,128)S(1)}, u32[]{:S(2)}, u32[]{:S(2)}) collective-permute-start(f32[80,384]{1,0:T(8,128)S(1)} %get-tuple-element.76.blk0), channel_id=1, source_target_pairs={{0,1},{1,0},{2,3},{3,2},{4,5},{5,4},{6,7},{7,6},{8,9},{9,8},{10,11... | collective-permute-start | bytes 368648 | tf_op jit(solution)/shard_map/ppermute | solution.py:600
  9.7 2.8 %collective-permute-start.2 = (f32[80,384]{1,0:T(8,128)S(1)}, f32[80,384]{1,0:T(8,128)S(1)}, u32[]{:S(2)}, u32[]{:S(2)}) collective-permute-start(f32[80,384]{1,0:T(8,128)S(1)} %get-tuple-element.77.band1), channel_id=1, source_target_pairs={{16,32},{32,16},{48,64},{64,48},{80,96},{96,80},{112,128},{128,112... | collective-permute-start | bytes 368648 | tf_op jit(solution)/shard_map/ppermute | solution.py:600
  12.5 6.6 %shard_map.96 = (bf16[4,384,384]{2,1,0:T(8,128)(2,1)S(1)}, bf16[4,384,384]{2,1,0:T(8,128)(2,1)S(1)}, bf16[512,512]{1,0:T(8,128)(2,1)S(1)}, bf16[512,512]{1,0:T(8...) custom-call(s32[2]{0:T(128)S(1)} %pad_add_fusion.parity, ...), custom_call_target="tpu_custom_call" | custom-call | tf_op jit(solution)/shard_map/pallas_call | solution.py:584
  19.1 0.0 collective-permute-done.blk1
  19.1 0.0 collective-permute-done.1.blk0
  19.1 0.5 collective-permute-done.2.band1
  19.7 3.0 %shard_map.97 = (f32[32,512]{1,0:T(8,128)S(1)}, f32[32,512]{1,0:T(8,128)S(1)}, f32[32,512]{1,0:T(8,128)S(1)}, f32[32,512]{1,0:T(8,128)S(1)}, bf16[4,128,128]{2,1...) custom-call(s32[2]{0:T(128)S(1)} %pad_add_fusion.parity, ...), custom_call_target="tpu_custom_call" | custom-call | tf_op jit(solution)/shard_map/pallas_call | solution.py:584
  22.7 5.8 %collective-permute-start.4 = (f32[32,512]{1,0:T(8,128)S(1)}, f32[32,512]{1,0:T(8,128)S(1)}, u32[]{:S(2)}, u32[]{:S(2)}) collective-permute-start(f32[32,512]{1,0:T(8,128)S(1)} %get-tuple-element.93), channel_id=1, source_target_pairs={{1,2},{2,1},{3,4},{4,3},{5,6},{6,5},{7,8},{8,7},{9,10},{10,9},{11,... | collective-permute-start | bytes 196616 | tf_op jit(solution)/shard_map/ppermute | solution.py:600
  28.5 0.0 collective-permute-start.5
  28.5 0.4 collective-permute-start.6
  29.0 0.0 collective-permute-start.7
  29.0 6.1 %shard_map.98 = (f32[4,32,384]{2,1,0:T(8,128)S(1)}, bf16[4,64,384]{2,1,0:T(8,128)(2,1)S(1)}, bf16[4,64,384]{2,1,0:T(8,128)(2,1)S(1)}, bf16[4,64,384]{2,1,0:T(8,1...) custom-call(f32[4,32,384]{2,1,0:T(8,128)S(1)} %get-tuple-element.98., ...), custom_call_target="tpu_custom_call" | custom-call | tf_op jit(solution)/shard_map/pallas_call | solution.py:584
  35.1 0.0 collective-permute-done.5.blk0
  35.1 1.5 %shard_map.99 = (f32[32,128]{1,0:T(8,128)S(1)}, f32[32,128]{1,0:T(8,128)S(1)}, f32[32,128]{1,0:T(8,128)S(1)}, f32[32,128]{1,0:T(8,128)S(1)}, f32[32,256]{1,0:T(8...) custom-call(s32[2]{0:T(128)S(1)} %pad_add_fusion.parity, ...), custom_call_target="tpu_custom_call" | custom-call | tf_op jit(solution)/shard_map/pallas_call | solution.py:584
  36.6 4.5 %collective-permute-start.8 = (f32[32,128]{1,0:T(8,128)S(1)}, f32[32,128]{1,0:T(8,128)S(1)}, u32[]{:S(2)}, u32[]{:S(2)}) collective-permute-start(f32[32,128]{1,0:T(8,128)S(1)} %get-tuple-element.119), channel_id=1, source_target_pairs={{1,2},{2,1},{3,4},{4,3},{5,6},{6,5},{7,8},{8,7},{9,10},{10,9},{11,... | collective-permute-start | bytes 49160 | tf_op jit(solution)/shard_map/ppermute | solution.py:600
  41.1 0.7 %collective-permute-start.9 = (f32[32,128]{1,0:T(8,128)S(1)}, f32[32,128]{1,0:T(8,128)S(1)}, u32[]{:S(2)}, u32[]{:S(2)}) collective-permute-start(f32[32,128]{1,0:T(8,128)S(1)} %get-tuple-element.120), channel_id=1, source_target_pairs={{0,1},{1,0},{2,3},{3,2},{4,5},{5,4},{6,7},{7,6},{8,9},{9,8},{10,11... | collective-permute-start | bytes 49160 | tf_op jit(solution)/shard_map/ppermute | solution.py:600
  41.8 2.9 %collective-permute-start.10 = (f32[32,128]{1,0:T(8,128)S(1)}, f32[32,128]{1,0:T(8,128)S(1)}, u32[]{:S(2)}, u32[]{:S(2)}) collective-permute-start(f32[32,128]{1,0:T(8,128)S(1)} %get-tuple-element.121), channel_id=1, source_target_pairs={{16,32},{32,16},{48,64},{64,48},{80,96},{96,80},{112,128},{128,112... | collective-permute-start | bytes 49160 | tf_op jit(solution)/shard_map/ppermute | solution.py:600
  44.8 0.0 collective-permute-start.11
  44.8 0.3 shard_map.100
  45.1 1.2 %collective-permute-done.9.blk0 = f32[32,128]{1,0:T(8,128)S(1)} collective-permute-done((f32[32,128]{1,0:T(8,128)S(1)}, f32[32,128]{1,0:T(8,128)S(1)}, u32[]{:S(2)}, u32[]{:S(2)}) %collective-permute-start.9) | collective-permute-done | bytes 16416 | tf_op jit(solution)/shard_map/ppermute | solution.py:600
  46.4 0.8 %collective-permute-done.10.band1 = f32[32,128]{1,0:T(8,128)S(1)} collective-permute-done((f32[32,128]{1,0:T(8,128)S(1)}, f32[32,128]{1,0:T(8,128)S(1)}, u32[]{:S(2)}, u32[]{:S(2)}) %collective-permute-start.10) | collective-permute-done | bytes 16416 | tf_op jit(solution)/shard_map/ppermute | solution.py:600
  47.1 1.4 %shard_map.101 = (f32[32,512]{1,0:T(8,128)S(1)}, f32[32,512]{1,0:T(8,128)S(1)}, f32[32,512]{1,0:T(8,128)S(1)}, f32[32,512]{1,0:T(8,128)S(1)}, f32[32,256]{1,0:T(...) custom-call(s32[2]{0:T(128)S(1)} %pad_add_fusion.parity, f32[32,128]{1,0:T(8,128)S(1)} %collective-permute-done.8.blk1, ...), custom_call_target="tpu_custom_call" | custom-call | tf_op jit(solution)/shard_map/pallas_call | solution.py:584
  48.5 3.3 %collective-permute-start.12 = (f32[32,512]{1,0:T(8,128)S(1)}, f32[32,512]{1,0:T(8,128)S(1)}, u32[]{:S(2)}, u32[]{:S(2)}) collective-permute-start(f32[32,512]{1,0:T(8,128)S(1)} %get-tuple-element.132), channel_id=1, source_target_pairs={{1,2},{2,1},{3,4},{4,3},{5,6},{6,5},{7,8},{8,7},{9,10},{10,9},{11,... | collective-permute-start | bytes 196616 | tf_op jit(solution)/shard_map/ppermute | solution.py:600
  51.9 1.6 %collective-permute-start.13 = (f32[32,512]{1,0:T(8,128)S(1)}, f32[32,512]{1,0:T(8,128)S(1)}, u32[]{:S(2)}, u32[]{:S(2)}) collective-permute-start(f32[32,512]{1,0:T(8,128)S(1)} %get-tuple-element.133), channel_id=1, source_target_pairs={{0,1},{1,0},{2,3},{3,2},{4,5},{5,4},{6,7},{7,6},{8,9},{9,8},{10,11... | collective-permute-start | bytes 196616 | tf_op jit(solution)/shard_map/ppermute | solution.py:600
  53.5 2.7 %collective-permute-start.14 = (f32[32,512]{1,0:T(8,128)S(1)}, f32[32,512]{1,0:T(8,128)S(1)}, u32[]{:S(2)}, u32[]{:S(2)}) collective-permute-start(f32[32,512]{1,0:T(8,128)S(1)} %get-tuple-element.134), channel_id=1, source_target_pairs={{16,32},{32,16},{48,64},{64,48},{80,96},{96,80},{112,128},{128,112... | collective-permute-start | bytes 196616 | tf_op jit(solution)/shard_map/ppermute | solution.py:600
  56.2 0.3 shard_map.102
  56.5 1.2 %collective-permute-done.13.blk0 = f32[32,512]{1,0:T(8,128)S(1)} collective-permute-done((f32[32,512]{1,0:T(8,128)S(1)}, f32[32,512]{1,0:T(8,128)S(1)}, u32[]{:S(2)}, u32[]{:S(2)}) %collective-permute-start.13) | collective-permute-done | bytes 65568 | tf_op jit(solution)/shard_map/ppermute | solution.py:600
  57.6 2.3 %collective-permute-done.14.band1 = f32[32,512]{1,0:T(8,128)S(1)} collective-permute-done((f32[32,512]{1,0:T(8,128)S(1)}, f32[32,512]{1,0:T(8,128)S(1)}, u32[]{:S(2)}, u32[]{:S(2)}) %collective-permute-start.14) | collective-permute-done | bytes 65568 | tf_op jit(solution)/shard_map/ppermute | solution.py:600
  60.0 2.8 %shard_map.103 = (f32[4,32,384]{2,1,0:T(8,128)}, f32[4,32,384]{2,1,0:T(8,128)}) custom-call(s32[2]{0:T(128)S(1)} %pad_add_fusion.parity, f32[32,512]{1,0:T(8,128)S(1)} %collective-permute-done.12.blk1, f32[32,512]{1,0:T(8,128)S(1)} %collective-permute-done.13.blk0, f32[32,512]{1,0:T(8,128)S(1)} %collective-permute-done.14.band1, ...), custom_call_target="tpu_custom_call" | custom-call | tf_op jit(solution)/shard_map/pallas_call | solution.py:584
  (12 shorter events, 0.0 us)
Async XLA Ops:
  0.7 11.8 %copy-start = (f32[1,1,4,384,384]{4,3,2,1,0:T(8,128)S(1)}, f32[1,1,4,384,384]{4,3,2,1,0:T(8,128)}, u32[]{:S(2)}) copy-start(f32[1,1,4,384,384]{4,3,2,1,0:T(8,128)} %param.9) | copy-start | bytes 7077892
  4.7 14.4 %collective-permute-start = (f32[80,384]{1,0:T(8,128)S(1)}, f32[80,384]{1,0:T(8,128)S(1)}, u32[]{:S(2)}, u32[]{:S(2)}) collective-permute-start(f32[80,384]{1,0:T(8,128)S(1)} %get-tuple-element.75.blk1), channel_id=1, source_target_pairs={{1,2},{2,1},{3,4},{4,3},{5,6},{6,5},{7,8},{8,7},{9,10},{10,9},{11,... | collective-permute-start | bytes 368648 | tf_op jit(solution)/shard_map/ppermute | solution.py:600
  7.4 11.7 %collective-permute-start.1 = (f32[80,384]{1,0:T(8,128)S(1)}, f32[80,384]{1,0:T(8,128)S(1)}, u32[]{:S(2)}, u32[]{:S(2)}) collective-permute-start(f32[80,384]{1,0:T(8,128)S(1)} %get-tuple-element.76.blk0), channel_id=1, source_target_pairs={{0,1},{1,0},{2,3},{3,2},{4,5},{5,4},{6,7},{7,6},{8,9},{9,8},{10,11... | collective-permute-start | bytes 368648 | tf_op jit(solution)/shard_map/ppermute | solution.py:600
  9.7 9.9 %collective-permute-start.2 = (f32[80,384]{1,0:T(8,128)S(1)}, f32[80,384]{1,0:T(8,128)S(1)}, u32[]{:S(2)}, u32[]{:S(2)}) collective-permute-start(f32[80,384]{1,0:T(8,128)S(1)} %get-tuple-element.77.band1), channel_id=1, source_target_pairs={{16,32},{32,16},{48,64},{64,48},{80,96},{96,80},{112,128},{128,112... | collective-permute-start | bytes 368648 | tf_op jit(solution)/shard_map/ppermute | solution.py:600
  12.5 7.1 %collective-permute-start.3 = (f32[80,384]{1,0:T(8,128)S(1)}, f32[80,384]{1,0:T(8,128)S(1)}, u32[]{:S(2)}, u32[]{:S(2)}) collective-permute-start(f32[80,384]{1,0:T(8,128)S(1)} %get-tuple-element.78.band0), channel_id=1, source_target_pairs={{0,16},{16,0},{32,48},{48,32},{64,80},{80,64},{96,112},{112,96},{1... | collective-permute-start | bytes 368648 | tf_op jit(solution)/shard_map/ppermute | solution.py:600
  22.7 12.4 %collective-permute-start.4 = (f32[32,512]{1,0:T(8,128)S(1)}, f32[32,512]{1,0:T(8,128)S(1)}, u32[]{:S(2)}, u32[]{:S(2)}) collective-permute-start(f32[32,512]{1,0:T(8,128)S(1)} %get-tuple-element.93), channel_id=1, source_target_pairs={{1,2},{2,1},{3,4},{4,3},{5,6},{6,5},{7,8},{8,7},{9,10},{10,9},{11,... | collective-permute-start | bytes 196616 | tf_op jit(solution)/shard_map/ppermute | solution.py:600
  28.5 6.5 %collective-permute-start.5 = (f32[32,512]{1,0:T(8,128)S(1)}, f32[32,512]{1,0:T(8,128)S(1)}, u32[]{:S(2)}, u32[]{:S(2)}) collective-permute-start(f32[32,512]{1,0:T(8,128)S(1)} %get-tuple-element.94), channel_id=1, source_target_pairs={{0,1},{1,0},{2,3},{3,2},{4,5},{5,4},{6,7},{7,6},{8,9},{9,8},{10,11... | collective-permute-start | bytes 196616 | tf_op jit(solution)/shard_map/ppermute | solution.py:600
  28.5 6.6 %collective-permute-start.6 = (f32[32,512]{1,0:T(8,128)S(1)}, f32[32,512]{1,0:T(8,128)S(1)}, u32[]{:S(2)}, u32[]{:S(2)}) collective-permute-start(f32[32,512]{1,0:T(8,128)S(1)} %get-tuple-element.95), channel_id=1, source_target_pairs={{16,32},{32,16},{48,64},{64,48},{80,96},{96,80},{112,128},{128,112... | collective-permute-start | bytes 196616 | tf_op jit(solution)/shard_map/ppermute | solution.py:600
  29.0 6.1 %collective-permute-start.7 = (f32[32,512]{1,0:T(8,128)S(1)}, f32[32,512]{1,0:T(8,128)S(1)}, u32[]{:S(2)}, u32[]{:S(2)}) collective-permute-start(f32[32,512]{1,0:T(8,128)S(1)} %get-tuple-element.96), channel_id=1, source_target_pairs={{0,16},{16,0},{32,48},{48,32},{64,80},{80,64},{96,112},{112,96},{1... | collective-permute-start | bytes 196616 | tf_op jit(solution)/shard_map/ppermute | solution.py:600
  36.6 8.5 %collective-permute-start.8 = (f32[32,128]{1,0:T(8,128)S(1)}, f32[32,128]{1,0:T(8,128)S(1)}, u32[]{:S(2)}, u32[]{:S(2)}) collective-permute-start(f32[32,128]{1,0:T(8,128)S(1)} %get-tuple-element.119), channel_id=1, source_target_pairs={{1,2},{2,1},{3,4},{4,3},{5,6},{6,5},{7,8},{8,7},{9,10},{10,9},{11,... | collective-permute-start | bytes 49160 | tf_op jit(solution)/shard_map/ppermute | solution.py:600
  41.1 5.2 %collective-permute-start.9 = (f32[32,128]{1,0:T(8,128)S(1)}, f32[32,128]{1,0:T(8,128)S(1)}, u32[]{:S(2)}, u32[]{:S(2)}) collective-permute-start(f32[32,128]{1,0:T(8,128)S(1)} %get-tuple-element.120), channel_id=1, source_target_pairs={{0,1},{1,0},{2,3},{3,2},{4,5},{5,4},{6,7},{7,6},{8,9},{9,8},{10,11... | collective-permute-start | bytes 49160 | tf_op jit(solution)/shard_map/ppermute | solution.py:600
  41.8 5.3 %collective-permute-start.10 = (f32[32,128]{1,0:T(8,128)S(1)}, f32[32,128]{1,0:T(8,128)S(1)}, u32[]{:S(2)}, u32[]{:S(2)}) collective-permute-start(f32[32,128]{1,0:T(8,128)S(1)} %get-tuple-element.121), channel_id=1, source_target_pairs={{16,32},{32,16},{48,64},{64,48},{80,96},{96,80},{112,128},{128,112... | collective-permute-start | bytes 49160 | tf_op jit(solution)/shard_map/ppermute | solution.py:600
  44.8 2.4 %collective-permute-start.11 = (f32[32,128]{1,0:T(8,128)S(1)}, f32[32,128]{1,0:T(8,128)S(1)}, u32[]{:S(2)}, u32[]{:S(2)}) collective-permute-start(f32[32,128]{1,0:T(8,128)S(1)} %get-tuple-element.122), channel_id=1, source_target_pairs={{0,16},{16,0},{32,48},{48,32},{64,80},{80,64},{96,112},{112,96},{1... | collective-permute-start | bytes 49160 | tf_op jit(solution)/shard_map/ppermute | solution.py:600
  48.5 7.9 %collective-permute-start.12 = (f32[32,512]{1,0:T(8,128)S(1)}, f32[32,512]{1,0:T(8,128)S(1)}, u32[]{:S(2)}, u32[]{:S(2)}) collective-permute-start(f32[32,512]{1,0:T(8,128)S(1)} %get-tuple-element.132), channel_id=1, source_target_pairs={{1,2},{2,1},{3,4},{4,3},{5,6},{6,5},{7,8},{8,7},{9,10},{10,9},{11,... | collective-permute-start | bytes 196616 | tf_op jit(solution)/shard_map/ppermute | solution.py:600
  51.9 5.8 %collective-permute-start.13 = (f32[32,512]{1,0:T(8,128)S(1)}, f32[32,512]{1,0:T(8,128)S(1)}, u32[]{:S(2)}, u32[]{:S(2)}) collective-permute-start(f32[32,512]{1,0:T(8,128)S(1)} %get-tuple-element.133), channel_id=1, source_target_pairs={{0,1},{1,0},{2,3},{3,2},{4,5},{5,4},{6,7},{7,6},{8,9},{9,8},{10,11... | collective-permute-start | bytes 196616 | tf_op jit(solution)/shard_map/ppermute | solution.py:600
  53.5 6.5 %collective-permute-start.14 = (f32[32,512]{1,0:T(8,128)S(1)}, f32[32,512]{1,0:T(8,128)S(1)}, u32[]{:S(2)}, u32[]{:S(2)}) collective-permute-start(f32[32,512]{1,0:T(8,128)S(1)} %get-tuple-element.134), channel_id=1, source_target_pairs={{16,32},{32,16},{48,64},{64,48},{80,96},{96,80},{112,128},{128,112... | collective-permute-start | bytes 196616 | tf_op jit(solution)/shard_map/ppermute | solution.py:600
  56.2 3.7 %collective-permute-start.15 = (f32[32,512]{1,0:T(8,128)S(1)}, f32[32,512]{1,0:T(8,128)S(1)}, u32[]{:S(2)}, u32[]{:S(2)}) collective-permute-start(f32[32,512]{1,0:T(8,128)S(1)} %get-tuple-element.135), channel_id=1, source_target_pairs={{0,16},{16,0},{32,48},{48,32},{64,80},{80,64},{96,112},{112,96},{1... | collective-permute-start | bytes 196616 | tf_op jit(solution)/shard_map/ppermute | solution.py:600

commit v3 on v2

--- a/solution.py
+++ b/solution.py
@@ -189,6 +189,16 @@
 def sent_diagonal(sent):
     tail = sent[72:80]
     return jnp.concatenate([tail[:, t * STRIDE : (t + 1) * STRIDE] for t in range(5)], axis=0)
+
+
+def with_modes(field, part):
+    side = [part[8 * t : 8 * t + 8] for t in range(4)] + [jnp.zeros((8, LANES), f32)]
+    return jnp.concatenate([field, jnp.concatenate(side, axis=1)], axis=0)
+
+
+def modes_below(sent):
+    tail = sent[COLS : COLS + 8]
+    return jnp.concatenate([tail[:, t * STRIDE : (t + 1) * STRIDE] for t in range(4)], axis=0)
 
 
 def pair_weights(own, far, w, xhi, xlo, j):
@@ -228,12 +238,14 @@
     for copy in small + large:
         copy.start()
     perm = permutation()
+    expand = (iota((SLOTS, PAIRS), 0) == (iota((SLOTS, PAIRS), 1) >> 4)).astype(f32).astype(bf16)
     for copy in small:
         copy.wait()
 
-    expand = (iota((SLOTS, PAIRS), 0) == (iota((SLOTS, PAIRS), 1) >> 4)).astype(f32)
-    slot = dot(nb[...].astype(f32), expand)
-    weight = penalty[...] * dot(valid[...].astype(f32), expand)
+    listed = jnp.concatenate([nb[...], valid[...]], axis=0).astype(f32).astype(bf16)
+    listed = dot(listed, expand)
+    slot = listed[0:AGG]
+    weight = penalty[...] * listed[AGG:]
     crossing = slot > 3.5
     lf = left[...].astype(f32)
     rf = right[...].astype(f32)
@@ -246,47 +258,49 @@
     tab[12:16] = wloc
     tab[16:20] = wcross
 
-    near = []
-    arrive = jnp.zeros((1, AGG * LANES), f32)
     rr = iota((AGG * LANES, PAIRS), 0)
     row = (rr >> 7) * 64 + (rr & 63)
+    lefts = lf.astype(jnp.int32)
+    fars = far.astype(jnp.int32)
+    hits = []
     for a in range(AGG):
-        w3 = jnp.concatenate(split3(wloc[a : a + 1]), axis=0)
-        near.append(jnp.sum(dot(w3, hot_twice(lf[a : a + 1]), NT), axis=0, keepdims=True))
-        hot = (row == far[a : a + 1].astype(jnp.int32)).astype(f32).astype(bf16)
-        arrive = arrive + jnp.sum(dot(w3, hot, NT), axis=0, keepdims=True)
+        near = jnp.where(row == lefts[a : a + 1] + a * BLOCKS, 1.0, 0.0)
+        hits.append((near + jnp.where(row == fars[a : a + 1], 1.0, 0.0)).astype(bf16))
+    flat = jnp.concatenate([wloc[a : a + 1] for a in range(AGG)], axis=1)
+    total = dot(jnp.concatenate(split3(flat), axis=0), jnp.concatenate(hits, axis=1), NT)
+    total = jnp.sum(total, axis=0, keepdims=True)
     totals = []
     for a in range(AGG):
-        total = near[a] + arrive[:, a * LANES : (a + 1) * LANES]
-        tab[20 + a : 21 + a] = total
-        totals.append(wide(total))
+        tab[20 + a : 21 + a] = total[:, a * LANES : (a + 1) * LANES]
+        totals.append(wide(total[:, a * LANES : (a + 1) * LANES]))
 
     pad = jnp.zeros((STRIDE - MODES, DOF), f32)
     q_all = q[...].astype(f32)
     modes = [jnp.concatenate([q_all[:, a, :], pad], axis=0).astype(bf16) for a in range(AGG)]
     turned_modes = dot(jnp.concatenate(modes, axis=0), perm)
     turned_modes = [turned_modes[a * STRIDE : (a + 1) * STRIDE] for a in range(AGG)]
+    turned = mm_exact(jnp.concatenate([b[a] for a in range(AGG)], axis=0), perm)
     eye = iota((LANES, LANES), 0) == iota((LANES, LANES), 1)
-    diagonals = []
+    turned16 = [turned_modes[a].astype(bf16) for a in range(AGG)]
+    springs = [mm2(turned_modes[a] * totals[a], turned16[a], NT) for a in range(AGG)]
+    diagonals, wholes = [], []
+    for copy in large:
+        copy.wait()
     for a in range(AGG):
-        large[a].wait()
         cuts = []
         for m in range(PAIRED):
             tile = k[a, m * LANES : (m + 1) * LANES, m * LANES : (m + 1) * LANES]
             cuts.append(jnp.sum(jnp.where(eye, tile, 0.0), axis=0, keepdims=True))
         diagonals.append(jnp.concatenate(cuts, axis=1))
-    stacked = jnp.concatenate(
-        [b[a] for a in range(AGG)] + diagonals + [jnp.zeros((4, DOF), f32)], axis=0
-    )
-    turned = mm_exact(stacked, perm)
+        hi, lo = split2(k[a])
+        projected = dot(modes[a], hi) + dot(modes[a], lo)
+        wholes.append(mm2(projected, modes[a], NT) + springs[a])
+    diagonals = mm_exact(jnp.concatenate(diagonals + [jnp.zeros((4, DOF), f32)], axis=0), perm)
     messages = []
     for a in range(AGG):
         load = turned[a * COLS : (a + 1) * COLS]
-        diagonal = turned[AGG * COLS + a : AGG * COLS + a + 1] + totals[a]
-        hi, lo = split2(k[a])
-        projected = dot(modes[a], hi) + dot(modes[a], lo)
-        galerkin = mm2(projected, modes[a], NT)
-        whole = galerkin + mm2(turned_modes[a] * totals[a], turned_modes[a].astype(bf16), NT)
+        diagonal = diagonals[a : a + 1] + totals[a]
+        whole = wholes[a]
         table = jnp.concatenate([lf[a : a + 1], rf[a : a + 1], wcross[a : a + 1]], axis=1)
         side = [whole[8 * t : 8 * t + 8] for t in range(5)] + [jnp.zeros((8, STRIDE), f32)]
         messages.append(
@@ -305,20 +319,34 @@
 
 
 def local_kernel(
-    parity, blk1, blk0, band1, band0, k, tab,
-    pkhi, pklo, ghi, glo, aqhi, aqlo, big, xhi, xlo, tco, tch, bp, qp, dsum, dloc, work,
+    parity, blk1, blk0, band1, band0, tab, k_in,
+    pkhi, pklo, ghi, glo, aqhi, aqlo, big, xhi, xlo, tco, tch, bp, qp, dsum, dloc, work, k, sem,
 ):
+    copies = [
+        pltpu.make_async_copy(
+            k_in.at[a, :, pl.ds(m * LANES, LANES)], k.at[a, m], sem.at[a * PAIRED + m]
+        )
+        for a in range(AGG)
+        for m in range(PAIRED)
+    ]
+    for copy in copies:
+        copy.start()
     for a, sent in enumerate(receive(parity, blk1, blk0, band1, band0)):
         bp[a] = sent[0:COLS]
         qp[a] = sent_modes(sent)
         dsum[a] = sent_diagonal(sent)
         dloc[a : a + 1] = sent[68:69]
     perm = permutation()
-    back = permutation_back()
     for a in range(AGG):
-        hi, lo = split2(k[a])
-        pkhi[a] = dot(back, dot(hi, perm).astype(bf16)).astype(bf16)
-        pklo[a] = dot(back, dot(lo, perm).astype(bf16)).astype(bf16)
+        tiles = []
+        for m in range(PAIRED):
+            copies[a * PAIRED + m].wait()
+            picked = [k[a, m, pl.ds(c, BLOCKS, stride=6), :] for c in range(6)]
+            tiles.append(jnp.concatenate(picked, axis=0))
+        hi, lo = split2(jnp.concatenate(tiles, axis=1))
+        both = dot(jnp.concatenate([hi, lo], axis=0), perm).astype(bf16)
+        pkhi[a] = both[0:DOF]
+        pklo[a] = both[DOF:]
     r = iota((AGG * LANES, 2 * PAIRS), 0)
     shift = 64 * (iota((1, 2 * PAIRS), 1) >> 7)
     rows = []
@@ -412,7 +440,7 @@
     messages = []
     for j in range(AGG):
         part = pg[:, j * STRIDE : (j + 1) * STRIDE]
-        messages.append(jnp.concatenate([d[j], part, jnp.zeros((COLS, STRIDE), f32)], axis=1))
+        messages.append(with_modes(d[j], part))
     send(parity, messages, oblk1, oblk0, oband1, oband0)
 
 
@@ -421,44 +449,66 @@
     pr, yhi, ylo, zhi, zlo, ghp, hhi, hlo, hhhi, hhlo, gchi, gclo, gxhi, gxlo, gohi, golo, work,
 ):
     d = [dlt[j] for j in range(AGG)]
-    cross = [tco[j : j + 1] for j in range(AGG)]
-    y = local_product(
-        d, [khi[a] for a in range(AGG)], [klo[a] for a in range(AGG)], ghi[...], glo[...], cross
-    )
-    for j in range(AGG):
-        pr[j] = r1[j] - y[j]
     corner, couple, part = [], [], []
     for j in range(AGG):
         mine = qp[j].astype(f32)
         other = qh[j].astype(f32)
-        rows = rows_of(mine).astype(bf16)
-        y = lanes_of(dot(rows, xhi[j]) + dot(rows, xlo[j]))
-        hi, lo = split2(y)
-        yhi[j] = hi
-        ylo[j] = lo
-        couple.append(-(dot(hi, qh[j], NT) + dot(lo, qh[j], NT)))
-        rows = rows_of(other).astype(bf16)
-        z = lanes_of(dot(rows, xhi[j], NT) + dot(rows, xlo[j], NT))
-        hi, lo = split2(z)
-        zhi[j] = hi
-        zlo[j] = lo
-        part.append(mm3(d[j], hi, lo, NT))
         own = mm2(mine * tco[j : j + 1], qp[j], NT)
         corner.append(own)
         blank = jnp.zeros((MODES, LANES - STRIDE), f32)
         work[:, j, :] = jnp.concatenate([dsum[j][0:MODES] + own[0:MODES], blank], axis=1)
         far = mm2(other * tch[j : j + 1], qh[j], NT)
         work[:, AGG + j, :] = jnp.concatenate([cdh[j][0:MODES] + far[0:MODES], blank], axis=1)
-    ghp[...] = jnp.concatenate(part, axis=1)
+
+    def own_side(j):
+        rows = rows_of(qp[j].astype(f32)).astype(bf16)
+        y = lanes_of(dot(rows, xhi[j]) + dot(rows, xlo[j]))
+        hi, lo = split2(y)
+        yhi[j] = hi
+        ylo[j] = lo
+        couple.append(-(dot(hi, qh[j], NT) + dot(lo, qh[j], NT)))
+
+    def far_side(j):
+        rows = rows_of(qh[j].astype(f32)).astype(bf16)
+        z = lanes_of(dot(rows, xhi[j], NT) + dot(rows, xlo[j], NT))
+        hi, lo = split2(z)
+        zhi[j] = hi
+        zlo[j] = lo
+        part.append(mm3(d[j], hi, lo, NT))
+
+    springs = []
+
+    def spring_side(j):
+        if j == 0:
+            springs.extend(unstack_fields(mm3(stack_fields(d), ghi[...], glo[...]), AGG))
+
+    def bend_side(j):
+        bend = mm3(d[j], khi[j], klo[j])
+        pr[j] = r1[j] - (bend + (springs[j] + d[j] * tco[j : j + 1]))
+
+    tasks = [(f, j) for f in (own_side, far_side, spring_side, bend_side) for j in range(AGG)]
     lane = iota((8, LANES), 1)
     rows = [work[i] + jnp.where(lane == STRIDE + i, 1.0, 0.0) for i in range(MODES)]
-    for s in range(MODES):
-        pivot = jnp.broadcast_to(rows[s][:, s : s + 1], (8, LANES))
-        scaled = rows[s] / pivot
+
+    def column(i, s):
+        return jnp.broadcast_to(rows[i][:, s : s + 1], (8, LANES))
+
+    for s in range(0, MODES, 2):
+        p, q = s, s + 1
+        pp, pq, qq, qp_ = column(p, p), column(p, q), column(q, q), column(q, p)
+        scale = 1.0 / (pp * qq - pq * qp_)
+        first = (qq * scale) * rows[p] - (pq * scale) * rows[q]
+        second = (pp * scale) * rows[q] - (qp_ * scale) * rows[p]
         for i in range(MODES):
-            if i != s:
-                rows[i] = rows[i] - jnp.broadcast_to(rows[i][:, s : s + 1], (8, LANES)) * scaled
-        rows[s] = scaled
+            if i != p and i != q:
+                rows[i] = rows[i] - column(i, p) * first - column(i, q) * second
+        rows[p], rows[q] = first, second
+        if tasks:
+            task, at = tasks.pop(0)
+            task(at)
+    for task, at in tasks:
+        task(at)
+    ghp[...] = jnp.concatenate(part, axis=1)
     for i in range(MODES):
         work[i] = rows[i] * coarse_damping
     below = jnp.zeros((STRIDE - MODES, STRIDE), f32)
@@ -489,11 +539,11 @@
     halo = receive(parity, blk1, blk0, band1, band0)
     parts = []
     for j in range(AGG):
-        value = halo[j][:, 0:DOF]
+        value = halo[j][0:COLS]
         dh[j] = value
         parts.append(mm3(value, yhi[j], ylo[j], NT))
     g = pg[...] + jnp.concatenate(parts, axis=1)
-    gh = halo_modes(halo, DOF) + ghp[...]
+    gh = jnp.concatenate([modes_below(h) for h in halo], axis=1) + ghp[...]
     e0 = mm3(g, hhi[...], hlo[...])
     e0h = mm3(gh, hhhi[...], hhlo[...])
     gch, gcl = gchi[...], gclo[...]
@@ -534,7 +584,7 @@
         f3o[j] = f
         part = r2[j] - y[:, j * DOF : (j + 1) * DOF] - f * tco[j : j + 1]
         pr3o[j] = part
-        messages.append(jnp.concatenate([part, mine, jnp.zeros((COLS, STRIDE), f32)], axis=1))
+        messages.append(with_modes(part, mine))
     send(parity, messages, oblk1, oblk0, oband1, oband0)
 
 
@@ -551,8 +601,8 @@
     halo = receive(parity, blk1, blk0, band1, band0)
     d4, d4h, r3 = [], [], []
     for j in range(AGG):
-        r = pr3[j] + mm3(halo[j][:, DOF : DOF + STRIDE], zhi[j], zlo[j])
-        rh = halo[j][:, 0:DOF] + rh3[j]
+        r = pr3[j] + mm3(modes_below(halo[j]), zhi[j], zlo[j])
+        rh = halo[j][0:COLS] + rh3[j]
         r3.append(r)
         d4.append(rec[j : j + 1] * r)
         d4h.append(rech[j : j + 1] * rh)
@@ -576,18 +626,18 @@
 HB = pl.BlockSpec(memory_space=pltpu.HBM)
 
 
-def run(kernel, outs, *args, scalars=0, scratch=(), place=VM, limit=24):
-    if place is HB:
-        args = args[:scalars] + tuple(
-            pltpu.with_memory_space_constraint(x, pltpu.HBM) for x in args[scalars:]
-        )
+def run(kernel, outs, *args, scalars=0, far=0, scratch=()):
+    near = len(args) - far
+    args = args[:near] + tuple(
+        pltpu.with_memory_space_constraint(x, pltpu.HBM) for x in args[near:]
+    )
     return pl.pallas_call(
         kernel,
         out_shape=[jax.ShapeDtypeStruct(shape, kind) for shape, kind in outs],
-        in_specs=[SM] * scalars + [place] * (len(args) - scalars),
+        in_specs=[SM] * scalars + [VM] * (near - scalars) + [HB] * far,
         out_specs=[VM] * len(outs),
         scratch_shapes=list(scratch),
-        compiler_params=pltpu.CompilerParams(vmem_limit_bytes=int(limit * 2**20)),
+        compiler_params=pltpu.CompilerParams(vmem_limit_bytes=24 * 2**20),
     )(*args)
 
 
@@ -640,7 +690,7 @@
         pair_right[0, 0],
         penalty[0, 0],
         scalars=1,
-        place=HB,
+        far=8,
         scratch=[
             pltpu.VMEM((AGG, COLS, DOF), f32),
             pltpu.VMEM((AGG, DOF, DOF), f32),
@@ -659,13 +709,18 @@
         local_kernel,
         [square, square, local, local, broad, broad, ((WIDTH, WIDTH), f32), pair_tile, pair_tile, rows, rows]
         + [fields, modes, small, rows],
-        parity, *out, stiffness[0, 0], tab,
+        parity, *out, tab, stiffness[0, 0],
         scalars=1,
-        scratch=[pltpu.VMEM((AGG * LANES, AGG * LANES), f32)],
+        far=1,
+        scratch=[
+            pltpu.VMEM((AGG * LANES, AGG * LANES), f32),
+            pltpu.VMEM((AGG, PAIRED, DOF, LANES), f32),
+            pltpu.SemaphoreType.DMA((AGG * PAIRED,)),
+        ],
     )
     *out, xhi, xlo, rec, rech, qh, cdh, tco, tch, x2, r1, dlt, pg = run(
         second_kernel,
-        message(COLS, DOF + LANES)
+        message(COLS + 8, DOF)
         + [tile, tile, rows, rows, modes, small, rows, rows, fields, fields, fields, coarse],
         parity, *got, bp, qp, dloc, pkhi, pklo, ghi, glo, aqhi, aqlo, x2hi, x2lo, t2o, t2h,
         scalars=1,
@@ -687,7 +742,7 @@
     r2, w2 = run(beside_third_kernel, [fields, coarse], dh, pr, xhi, xlo, d1, gohi, golo)
     *out, e, f3, pr3 = run(
         fourth_kernel,
-        message(COLS, DOF + LANES) + [coarse, fields, fields],
+        message(COLS + 8, DOF) + [coarse, fields, fields],
         parity, *got, p2, w2, e1, gchi, gclo, gxhi, gxlo, r2, qp, aqhi, aqlo, tco,
         scalars=1,
     )

time: 63.6 us -> 61.7 us (0.970); the launches traced: 62.7 us -> 61.5 us
  waiting for transfers between devices: 6.05 us -> 12.2 us
  starting transfers between devices: 29.9 us -> 25.7 us
  Pallas kernels: 25.9 us -> 22.9 us
    ppermute x16, waiting for transfers between devices: 6.05 us -> 12.2 us  [swapped(): return lax.ppermute(x, axis, route)]
    ppermute x16, starting transfers between devices: 29.9 us -> 25.7 us  [swapped(): return lax.ppermute(x, axis, route)]
    pallas_call x9, Pallas kernels: 25.9 us -> 22.9 us  [run(): pl.pallas_call(kernel, out_shape=[jax.ShapeDtypeStruct(shape, kind) for s...]
  transfers between devices with their start and end apart: 16 -> 16, of which waited for: 5 -> 7; matrix products, arithmetic and copies ran while one was open for 0% -> 0% of each run, Pallas kernels for 21% -> 17%
where the time goes in v3:
time: 61.7 us; the launch traced here: 61.5 us
  starting transfers between devices  25.7 us (42%)
  Pallas kernels  22.9 us (37%)
  waiting for transfers between devices  12.2 us (20%)
  between operations  0.75 us (1%)
    ppermute x16, starting transfers between devices, swapped(): return lax.ppermute(x, axis, route)  25.7 us
    pallas_call x9, Pallas kernels, run(): pl.pallas_call(kernel, out_shape=[jax.ShapeDtypeStruct(shape, kind) for s...  22.9 us
    ppermute x16, waiting for transfers between devices, swapped(): return lax.ppermute(x, axis, route)  12.2 us
  transfers between devices with their start and end apart: 16, of which 7 were waited for; matrix products, arithmetic and copies ran while one was open for 0% of the time, Pallas kernels for 17%

profile of v3, /device:TPU:32, one launch (start us, length us, event | category | flops | bytes accessed | tf_op | source)
XLA Modules:
  0.0 61.5 jit_solution(168371534481887356)
XLA Ops:
  0.6 0.1 pad_add_fusion.parity
  0.7 3.8 %shard_map.95 = (f32[80,384]{1,0:T(8,128)S(1)}, f32[80,384]{1,0:T(8,128)S(1)}, f32[80,384]{1,0:T(8,128)S(1)}, f32[80,384]{1,0:T(8,128)S(1)}, f32[24,128]{1,0:T(8,128)S(1)}) custom-call(s32[2]{0:T(128)S(1)} %pad_add_fusion.parity, f32[4,32,384]{2,1,0:T(8,128)} %bitcast.16, f32[4,384,384]{2,1,0:T(8,128)} %bitcast.14, bf16[36,4,384]{2,1,0:T(4,128)(2,1)} %bitcast.17, ...), custom_call_target="tpu_custom_call" | custom-call | tf_op jit(solution)/shard_map/pallas_call | solution.py:634
  4.5 2.7 %collective-permute-start = (f32[80,384]{1,0:T(8,128)S(1)}, f32[80,384]{1,0:T(8,128)S(1)}, u32[]{:S(2)}, u32[]{:S(2)}) collective-permute-start(f32[80,384]{1,0:T(8,128)S(1)} %get-tuple-element.75.blk1), channel_id=1, source_target_pairs={{1,2},{2,1},{3,4},{4,3},{5,6},{6,5},{7,8},{8,7},{9,10},{10,9},{11,... | collective-permute-start | bytes 368648 | tf_op jit(solution)/shard_map/ppermute | solution.py:650
  7.2 2.3 %collective-permute-start.1 = (f32[80,384]{1,0:T(8,128)S(1)}, f32[80,384]{1,0:T(8,128)S(1)}, u32[]{:S(2)}, u32[]{:S(2)}) collective-permute-start(f32[80,384]{1,0:T(8,128)S(1)} %get-tuple-element.76.blk0), channel_id=1, source_target_pairs={{0,1},{1,0},{2,3},{3,2},{4,5},{5,4},{6,7},{7,6},{8,9},{9,8},{10,11... | collective-permute-start | bytes 368648 | tf_op jit(solution)/shard_map/ppermute | solution.py:650
  9.5 2.8 %collective-permute-start.2 = (f32[80,384]{1,0:T(8,128)S(1)}, f32[80,384]{1,0:T(8,128)S(1)}, u32[]{:S(2)}, u32[]{:S(2)}) collective-permute-start(f32[80,384]{1,0:T(8,128)S(1)} %get-tuple-element.77.band1), channel_id=1, source_target_pairs={{16,32},{32,16},{48,64},{64,48},{80,96},{96,80},{112,128},{128,112... | collective-permute-start | bytes 368648 | tf_op jit(solution)/shard_map/ppermute | solution.py:650
  12.3 0.0 collective-permute-start.3
  12.3 6.2 %shard_map.96 = (bf16[4,384,384]{2,1,0:T(8,128)(2,1)S(1)}, bf16[4,384,384]{2,1,0:T(8,128)(2,1)S(1)}, bf16[512,512]{1,0:T(8,128)(2,1)S(1)}, bf16[512,512]{1,0:T(8...) custom-call(s32[2]{0:T(128)S(1)} %pad_add_fusion.parity, ...), custom_call_target="tpu_custom_call" | custom-call | tf_op jit(solution)/shard_map/pallas_call | solution.py:634
  18.6 0.9 %collective-permute-done.2.band1 = f32[80,384]{1,0:T(8,128)S(1)} collective-permute-done((f32[80,384]{1,0:T(8,128)S(1)}, f32[80,384]{1,0:T(8,128)S(1)}, u32[]{:S(2)}, u32[]{:S(2)}) %collective-permute-start.2) | collective-permute-done | bytes 122912 | tf_op jit(solution)/shard_map/ppermute | solution.py:650
  19.5 0.0 collective-permute-done.3.band0
  19.5 3.0 %shard_map.97 = (f32[40,384]{1,0:T(8,128)S(1)}, f32[40,384]{1,0:T(8,128)S(1)}, f32[40,384]{1,0:T(8,128)S(1)}, f32[40,384]{1,0:T(8,128)S(1)}, bf16[4,128,128]{2,1...) custom-call(s32[2]{0:T(128)S(1)} %pad_add_fusion.parity, ...), custom_call_target="tpu_custom_call" | custom-call | tf_op jit(solution)/shard_map/pallas_call | solution.py:634
  22.5 5.5 %collective-permute-start.4 = (f32[40,384]{1,0:T(8,128)S(1)}, f32[40,384]{1,0:T(8,128)S(1)}, u32[]{:S(2)}, u32[]{:S(2)}) collective-permute-start(f32[40,384]{1,0:T(8,128)S(1)} %get-tuple-element.93), channel_id=1, source_target_pairs={{1,2},{2,1},{3,4},{4,3},{5,6},{6,5},{7,8},{8,7},{9,10},{10,9},{11,... | collective-permute-start | bytes 184328 | tf_op jit(solution)/shard_map/ppermute | solution.py:650
  28.0 0.0 collective-permute-start.5
  28.0 0.4 collective-permute-start.6
  28.4 0.0 collective-permute-start.7
  28.4 3.5 %shard_map.98 = (f32[4,32,384]{2,1,0:T(8,128)S(1)}, bf16[4,64,384]{2,1,0:T(8,128)(2,1)S(1)}, bf16[4,64,384]{2,1,0:T(8,128)(2,1)S(1)}, bf16[4,64,384]{2,1,0:T(8,1...) custom-call(f32[4,32,384]{2,1,0:T(8,128)S(1)} %get-tuple-element.98., ...), custom_call_target="tpu_custom_call" | custom-call | tf_op jit(solution)/shard_map/pallas_call | solution.py:634
  31.9 2.4 %collective-permute-done.5.blk0 = f32[40,384]{1,0:T(8,128)S(1)} collective-permute-done((f32[40,384]{1,0:T(8,128)S(1)}, f32[40,384]{1,0:T(8,128)S(1)}, u32[]{:S(2)}, u32[]{:S(2)}) %collective-permute-start.5) | collective-permute-done | bytes 61472 | tf_op jit(solution)/shard_map/ppermute | solution.py:650
  34.3 1.5 %shard_map.99 = (f32[32,128]{1,0:T(8,128)S(1)}, f32[32,128]{1,0:T(8,128)S(1)}, f32[32,128]{1,0:T(8,128)S(1)}, f32[32,128]{1,0:T(8,128)S(1)}, f32[32,256]{1,0:T(8...) custom-call(s32[2]{0:T(128)S(1)} %pad_add_fusion.parity, ...), custom_call_target="tpu_custom_call" | custom-call | tf_op jit(solution)/shard_map/pallas_call | solution.py:634
  35.8 4.7 %collective-permute-start.8 = (f32[32,128]{1,0:T(8,128)S(1)}, f32[32,128]{1,0:T(8,128)S(1)}, u32[]{:S(2)}, u32[]{:S(2)}) collective-permute-start(f32[32,128]{1,0:T(8,128)S(1)} %get-tuple-element.119), channel_id=1, source_target_pairs={{1,2},{2,1},{3,4},{4,3},{5,6},{6,5},{7,8},{8,7},{9,10},{10,9},{11,... | collective-permute-start | bytes 49160 | tf_op jit(solution)/shard_map/ppermute | solution.py:650
  40.5 0.4 collective-permute-start.9
  40.9 1.1 %collective-permute-start.10 = (f32[32,128]{1,0:T(8,128)S(1)}, f32[32,128]{1,0:T(8,128)S(1)}, u32[]{:S(2)}, u32[]{:S(2)}) collective-permute-start(f32[32,128]{1,0:T(8,128)S(1)} %get-tuple-element.121), channel_id=1, source_target_pairs={{16,32},{32,16},{48,64},{64,48},{80,96},{96,80},{112,128},{128,112... | collective-permute-start | bytes 49160 | tf_op jit(solution)/shard_map/ppermute | solution.py:650
  42.0 0.3 shard_map.100
  42.3 3.5 %collective-permute-done.9.blk0 = f32[32,128]{1,0:T(8,128)S(1)} collective-permute-done((f32[32,128]{1,0:T(8,128)S(1)}, f32[32,128]{1,0:T(8,128)S(1)}, u32[]{:S(2)}, u32[]{:S(2)}) %collective-permute-start.9) | collective-permute-done | bytes 16416 | tf_op jit(solution)/shard_map/ppermute | solution.py:650
  45.8 0.4 collective-permute-done.10.band1
  46.2 1.4 %shard_map.101 = (f32[40,384]{1,0:T(8,128)S(1)}, f32[40,384]{1,0:T(8,128)S(1)}, f32[40,384]{1,0:T(8,128)S(1)}, f32[40,384]{1,0:T(8,128)S(1)}, f32[32,256]{1,0:T(...) custom-call(s32[2]{0:T(128)S(1)} %pad_add_fusion.parity, f32[32,128]{1,0:T(8,128)S(1)} %collective-permute-done.8.blk1, ...), custom_call_target="tpu_custom_call" | custom-call | tf_op jit(solution)/shard_map/pallas_call | solution.py:634
  47.6 3.7 %collective-permute-start.12 = (f32[40,384]{1,0:T(8,128)S(1)}, f32[40,384]{1,0:T(8,128)S(1)}, u32[]{:S(2)}, u32[]{:S(2)}) collective-permute-start(f32[40,384]{1,0:T(8,128)S(1)} %get-tuple-element.132), channel_id=1, source_target_pairs={{1,2},{2,1},{3,4},{4,3},{5,6},{6,5},{7,8},{8,7},{9,10},{10,9},{11,... | collective-permute-start | bytes 184328 | tf_op jit(solution)/shard_map/ppermute | solution.py:650
  51.3 1.6 %collective-permute-start.13 = (f32[40,384]{1,0:T(8,128)S(1)}, f32[40,384]{1,0:T(8,128)S(1)}, u32[]{:S(2)}, u32[]{:S(2)}) collective-permute-start(f32[40,384]{1,0:T(8,128)S(1)} %get-tuple-element.133), channel_id=1, source_target_pairs={{0,1},{1,0},{2,3},{3,2},{4,5},{5,4},{6,7},{7,6},{8,9},{9,8},{10,11... | collective-permute-start | bytes 184328 | tf_op jit(solution)/shard_map/ppermute | solution.py:650
  52.9 0.5 collective-permute-start.14
  53.4 0.3 shard_map.102
  53.7 0.7 %collective-permute-done.12.blk1 = f32[40,384]{1,0:T(8,128)S(1)} collective-permute-done((f32[40,384]{1,0:T(8,128)S(1)}, f32[40,384]{1,0:T(8,128)S(1)}, u32[]{:S(2)}, u32[]{:S(2)}) %collective-permute-start.12) | collective-permute-done | bytes 61472 | tf_op jit(solution)/shard_map/ppermute | solution.py:650
  54.3 2.7 %collective-permute-done.13.blk0 = f32[40,384]{1,0:T(8,128)S(1)} collective-permute-done((f32[40,384]{1,0:T(8,128)S(1)}, f32[40,384]{1,0:T(8,128)S(1)}, u32[]{:S(2)}, u32[]{:S(2)}) %collective-permute-start.13) | collective-permute-done | bytes 61472 | tf_op jit(solution)/shard_map/ppermute | solution.py:650
  57.0 1.6 %collective-permute-done.14.band1 = f32[40,384]{1,0:T(8,128)S(1)} collective-permute-done((f32[40,384]{1,0:T(8,128)S(1)}, f32[40,384]{1,0:T(8,128)S(1)}, u32[]{:S(2)}, u32[]{:S(2)}) %collective-permute-start.14) | collective-permute-done | bytes 61472 | tf_op jit(solution)/shard_map/ppermute | solution.py:650
  58.7 2.9 %shard_map.103 = (f32[4,32,384]{2,1,0:T(8,128)}, f32[4,32,384]{2,1,0:T(8,128)}) custom-call(s32[2]{0:T(128)S(1)} %pad_add_fusion.parity, f32[40,384]{1,0:T(8,128)S(1)} %collective-permute-done.12.blk1, f32[40,384]{1,0:T(8,128)S(1)} %collective-permute-done.13.blk0, f32[40,384]{1,0:T(8,128)S(1)} %collective-permute-done.14.band1, ...), custom_call_target="tpu_custom_call" | custom-call | tf_op jit(solution)/shard_map/pallas_call | solution.py:634
  (10 shorter events, 0.0 us)
Async XLA Ops:
  4.5 14.0 %collective-permute-start = (f32[80,384]{1,0:T(8,128)S(1)}, f32[80,384]{1,0:T(8,128)S(1)}, u32[]{:S(2)}, u32[]{:S(2)}) collective-permute-start(f32[80,384]{1,0:T(8,128)S(1)} %get-tuple-element.75.blk1), channel_id=1, source_target_pairs={{1,2},{2,1},{3,4},{4,3},{5,6},{6,5},{7,8},{8,7},{9,10},{10,9},{11,... | collective-permute-start | bytes 368648 | tf_op jit(solution)/shard_map/ppermute | solution.py:650
  7.2 11.4 %collective-permute-start.1 = (f32[80,384]{1,0:T(8,128)S(1)}, f32[80,384]{1,0:T(8,128)S(1)}, u32[]{:S(2)}, u32[]{:S(2)}) collective-permute-start(f32[80,384]{1,0:T(8,128)S(1)} %get-tuple-element.76.blk0), channel_id=1, source_target_pairs={{0,1},{1,0},{2,3},{3,2},{4,5},{5,4},{6,7},{7,6},{8,9},{9,8},{10,11... | collective-permute-start | bytes 368648 | tf_op jit(solution)/shard_map/ppermute | solution.py:650
  9.5 10.0 %collective-permute-start.2 = (f32[80,384]{1,0:T(8,128)S(1)}, f32[80,384]{1,0:T(8,128)S(1)}, u32[]{:S(2)}, u32[]{:S(2)}) collective-permute-start(f32[80,384]{1,0:T(8,128)S(1)} %get-tuple-element.77.band1), channel_id=1, source_target_pairs={{16,32},{32,16},{48,64},{64,48},{80,96},{96,80},{112,128},{128,112... | collective-permute-start | bytes 368648 | tf_op jit(solution)/shard_map/ppermute | solution.py:650
  12.3 7.1 %collective-permute-start.3 = (f32[80,384]{1,0:T(8,128)S(1)}, f32[80,384]{1,0:T(8,128)S(1)}, u32[]{:S(2)}, u32[]{:S(2)}) collective-permute-start(f32[80,384]{1,0:T(8,128)S(1)} %get-tuple-element.78.band0), channel_id=1, source_target_pairs={{0,16},{16,0},{32,48},{48,32},{64,80},{80,64},{96,112},{112,96},{1... | collective-permute-start | bytes 368648 | tf_op jit(solution)/shard_map/ppermute | solution.py:650
  22.5 9.4 %collective-permute-start.4 = (f32[40,384]{1,0:T(8,128)S(1)}, f32[40,384]{1,0:T(8,128)S(1)}, u32[]{:S(2)}, u32[]{:S(2)}) collective-permute-start(f32[40,384]{1,0:T(8,128)S(1)} %get-tuple-element.93), channel_id=1, source_target_pairs={{1,2},{2,1},{3,4},{4,3},{5,6},{6,5},{7,8},{8,7},{9,10},{10,9},{11,... | collective-permute-start | bytes 184328 | tf_op jit(solution)/shard_map/ppermute | solution.py:650
  28.0 6.3 %collective-permute-start.5 = (f32[40,384]{1,0:T(8,128)S(1)}, f32[40,384]{1,0:T(8,128)S(1)}, u32[]{:S(2)}, u32[]{:S(2)}) collective-permute-start(f32[40,384]{1,0:T(8,128)S(1)} %get-tuple-element.94), channel_id=1, source_target_pairs={{0,1},{1,0},{2,3},{3,2},{4,5},{5,4},{6,7},{7,6},{8,9},{9,8},{10,11... | collective-permute-start | bytes 184328 | tf_op jit(solution)/shard_map/ppermute | solution.py:650
  28.0 6.3 %collective-permute-start.6 = (f32[40,384]{1,0:T(8,128)S(1)}, f32[40,384]{1,0:T(8,128)S(1)}, u32[]{:S(2)}, u32[]{:S(2)}) collective-permute-start(f32[40,384]{1,0:T(8,128)S(1)} %get-tuple-element.95), channel_id=1, source_target_pairs={{16,32},{32,16},{48,64},{64,48},{80,96},{96,80},{112,128},{128,112... | collective-permute-start | bytes 184328 | tf_op jit(solution)/shard_map/ppermute | solution.py:650
  28.4 5.9 %collective-permute-start.7 = (f32[40,384]{1,0:T(8,128)S(1)}, f32[40,384]{1,0:T(8,128)S(1)}, u32[]{:S(2)}, u32[]{:S(2)}) collective-permute-start(f32[40,384]{1,0:T(8,128)S(1)} %get-tuple-element.96), channel_id=1, source_target_pairs={{0,16},{16,0},{32,48},{48,32},{64,80},{80,64},{96,112},{112,96},{1... | collective-permute-start | bytes 184328 | tf_op jit(solution)/shard_map/ppermute | solution.py:650
  35.8 6.5 %collective-permute-start.8 = (f32[32,128]{1,0:T(8,128)S(1)}, f32[32,128]{1,0:T(8,128)S(1)}, u32[]{:S(2)}, u32[]{:S(2)}) collective-permute-start(f32[32,128]{1,0:T(8,128)S(1)} %get-tuple-element.119), channel_id=1, source_target_pairs={{1,2},{2,1},{3,4},{4,3},{5,6},{6,5},{7,8},{8,7},{9,10},{10,9},{11,... | collective-permute-start | bytes 49160 | tf_op jit(solution)/shard_map/ppermute | solution.py:650
  40.5 5.2 %collective-permute-start.9 = (f32[32,128]{1,0:T(8,128)S(1)}, f32[32,128]{1,0:T(8,128)S(1)}, u32[]{:S(2)}, u32[]{:S(2)}) collective-permute-start(f32[32,128]{1,0:T(8,128)S(1)} %get-tuple-element.120), channel_id=1, source_target_pairs={{0,1},{1,0},{2,3},{3,2},{4,5},{5,4},{6,7},{7,6},{8,9},{9,8},{10,11... | collective-permute-start | bytes 49160 | tf_op jit(solution)/shard_map/ppermute | solution.py:650
  40.9 5.3 %collective-permute-start.10 = (f32[32,128]{1,0:T(8,128)S(1)}, f32[32,128]{1,0:T(8,128)S(1)}, u32[]{:S(2)}, u32[]{:S(2)}) collective-permute-start(f32[32,128]{1,0:T(8,128)S(1)} %get-tuple-element.121), channel_id=1, source_target_pairs={{16,32},{32,16},{48,64},{64,48},{80,96},{96,80},{112,128},{128,112... | collective-permute-start | bytes 49160 | tf_op jit(solution)/shard_map/ppermute | solution.py:650
  42.0 4.2 %collective-permute-start.11 = (f32[32,128]{1,0:T(8,128)S(1)}, f32[32,128]{1,0:T(8,128)S(1)}, u32[]{:S(2)}, u32[]{:S(2)}) collective-permute-start(f32[32,128]{1,0:T(8,128)S(1)} %get-tuple-element.122), channel_id=1, source_target_pairs={{0,16},{16,0},{32,48},{48,32},{64,80},{80,64},{96,112},{112,96},{1... | collective-permute-start | bytes 49160 | tf_op jit(solution)/shard_map/ppermute | solution.py:650
  47.6 6.7 %collective-permute-start.12 = (f32[40,384]{1,0:T(8,128)S(1)}, f32[40,384]{1,0:T(8,128)S(1)}, u32[]{:S(2)}, u32[]{:S(2)}) collective-permute-start(f32[40,384]{1,0:T(8,128)S(1)} %get-tuple-element.132), channel_id=1, source_target_pairs={{1,2},{2,1},{3,4},{4,3},{5,6},{6,5},{7,8},{8,7},{9,10},{10,9},{11,... | collective-permute-start | bytes 184328 | tf_op jit(solution)/shard_map/ppermute | solution.py:650
  51.3 5.7 %collective-permute-start.13 = (f32[40,384]{1,0:T(8,128)S(1)}, f32[40,384]{1,0:T(8,128)S(1)}, u32[]{:S(2)}, u32[]{:S(2)}) collective-permute-start(f32[40,384]{1,0:T(8,128)S(1)} %get-tuple-element.133), channel_id=1, source_target_pairs={{0,1},{1,0},{2,3},{3,2},{4,5},{5,4},{6,7},{7,6},{8,9},{9,8},{10,11... | collective-permute-start | bytes 184328 | tf_op jit(solution)/shard_map/ppermute | solution.py:650
  52.9 5.8 %collective-permute-start.14 = (f32[40,384]{1,0:T(8,128)S(1)}, f32[40,384]{1,0:T(8,128)S(1)}, u32[]{:S(2)}, u32[]{:S(2)}) collective-permute-start(f32[40,384]{1,0:T(8,128)S(1)} %get-tuple-element.134), channel_id=1, source_target_pairs={{16,32},{32,16},{48,64},{64,48},{80,96},{96,80},{112,128},{128,112... | collective-permute-start | bytes 184328 | tf_op jit(solution)/shard_map/ppermute | solution.py:650
  53.4 5.3 %collective-permute-start.15 = (f32[40,384]{1,0:T(8,128)S(1)}, f32[40,384]{1,0:T(8,128)S(1)}, u32[]{:S(2)}, u32[]{:S(2)}) collective-permute-start(f32[40,384]{1,0:T(8,128)S(1)} %get-tuple-element.135), channel_id=1, source_target_pairs={{0,16},{16,0},{32,48},{48,32},{64,80},{80,64},{96,112},{112,96},{1... | collective-permute-start | bytes 184328 | tf_op jit(solution)/shard_map/ppermute | solution.py:650

commit v4 on v3

--- a/solution.py
+++ b/solution.py
@@ -217,8 +217,8 @@
 
 def first_kernel(
     parity, b_in, k_in, q_in, nb_in, valid_in, left_in, right_in, penalty_in,
-    blk1, blk0, band1, band0, tab,
-    b, k, q, nb, valid, left, right, penalty, sem,
+    blk1, blk0, band1, band0, tab, k,
+    b, q, nb, valid, left, right, penalty, sem,
 ):
     small = [
         pltpu.make_async_copy(src, dst, sem.at[n])
@@ -234,7 +234,13 @@
             ]
         )
     ]
-    large = [pltpu.make_async_copy(k_in.at[a], k.at[a], sem.at[8 + a]) for a in range(AGG)]
+    large = [
+        pltpu.make_async_copy(
+            k_in.at[a, :, pl.ds(m * LANES, LANES)], k.at[a, m], sem.at[8 + a * PAIRED + m]
+        )
+        for a in range(AGG)
+        for m in range(PAIRED)
+    ]
     for copy in small + large:
         copy.start()
     perm = permutation()
@@ -289,10 +295,10 @@
     for a in range(AGG):
         cuts = []
         for m in range(PAIRED):
-            tile = k[a, m * LANES : (m + 1) * LANES, m * LANES : (m + 1) * LANES]
+            tile = k[a, m, m * LANES : (m + 1) * LANES, :]
             cuts.append(jnp.sum(jnp.where(eye, tile, 0.0), axis=0, keepdims=True))
         diagonals.append(jnp.concatenate(cuts, axis=1))
-        hi, lo = split2(k[a])
+        hi, lo = split2(jnp.concatenate([k[a, m] for m in range(PAIRED)], axis=1))
         projected = dot(modes[a], hi) + dot(modes[a], lo)
         wholes.append(mm2(projected, modes[a], NT) + springs[a])
     diagonals = mm_exact(jnp.concatenate(diagonals + [jnp.zeros((4, DOF), f32)], axis=0), perm)
@@ -319,18 +325,9 @@
 
 
 def local_kernel(
-    parity, blk1, blk0, band1, band0, tab, k_in,
-    pkhi, pklo, ghi, glo, aqhi, aqlo, big, xhi, xlo, tco, tch, bp, qp, dsum, dloc, work, k, sem,
-):
-    copies = [
-        pltpu.make_async_copy(
-            k_in.at[a, :, pl.ds(m * LANES, LANES)], k.at[a, m], sem.at[a * PAIRED + m]
-        )
-        for a in range(AGG)
-        for m in range(PAIRED)
-    ]
-    for copy in copies:
-        copy.start()
+    parity, blk1, blk0, band1, band0, tab, k,
+    pkhi, pklo, ghi, glo, aqhi, aqlo, big, xhi, xlo, tco, tch, bp, qp, dsum, dloc, work,
+):
     for a, sent in enumerate(receive(parity, blk1, blk0, band1, band0)):
         bp[a] = sent[0:COLS]
         qp[a] = sent_modes(sent)
@@ -340,7 +337,6 @@
     for a in range(AGG):
         tiles = []
         for m in range(PAIRED):
-            copies[a * PAIRED + m].wait()
             picked = [k[a, m, pl.ds(c, BLOCKS, stride=6), :] for c in range(6)]
             tiles.append(jnp.concatenate(picked, axis=0))
         hi, lo = split2(jnp.concatenate(tiles, axis=1))
@@ -445,8 +441,8 @@
 
 
 def inverse_kernel(
-    dlt, r1, khi, klo, ghi, glo, qp, qh, dsum, cdh, tco, tch, xhi, xlo, big,
-    pr, yhi, ylo, zhi, zlo, ghp, hhi, hlo, hhhi, hhlo, gchi, gclo, gxhi, gxlo, gohi, golo, work,
+    pg, dlt, r1, khi, klo, ghi, glo, qp, qh, dsum, cdh, tco, tch, xhi, xlo, big,
+    pr, yhi, ylo, zhi, zlo, vhi, vlo, q0, ghp, hhhi, hhlo, gchi, gclo, gxhi, gxlo, gohi, golo, work,
 ):
     d = [dlt[j] for j in range(AGG)]
     corner, couple, part = [], [], []
@@ -516,8 +512,9 @@
         jnp.concatenate([work[:, m, :][:, STRIDE:], below], axis=0) for m in range(2 * AGG)
     ]
     hh, hl = split2(block_diagonal(blocks[:AGG]))
-    hhi[...] = hh
-    hlo[...] = hl
+    q0[...] = mm3(pg[...], hh, hl)
+    for j in range(AGG):
+        store2(vhi.at[j], vlo.at[j], mm3(blocks[j], yhi[j], ylo[j]))
     fh, fl = split2(block_diagonal(blocks[AGG:]))
     hhhi[...] = fh
     hhlo[...] = fl
@@ -533,7 +530,7 @@
 
 
 def third_kernel(
-    parity, blk1, blk0, band1, band0, pg, ghp, yhi, ylo, hhi, hlo, hhhi, hhlo, gchi, gclo, gxhi, gxlo,
+    parity, blk1, blk0, band1, band0, q0, ghp, vhi, vlo, hhhi, hhlo, gchi, gclo, gxhi, gxlo,
     oblk1, oblk0, oband1, oband0, e1o, d1o, p2o, dh,
 ):
     halo = receive(parity, blk1, blk0, band1, band0)
@@ -541,10 +538,9 @@
     for j in range(AGG):
         value = halo[j][0:COLS]
         dh[j] = value
-        parts.append(mm3(value, yhi[j], ylo[j], NT))
-    g = pg[...] + jnp.concatenate(parts, axis=1)
+        parts.append(mm3(value, vhi[j], vlo[j], NT))
+    e0 = q0[...] + jnp.concatenate(parts, axis=1)
     gh = jnp.concatenate([modes_below(h) for h in halo], axis=1) + ghp[...]
-    e0 = mm3(g, hhi[...], hlo[...])
     e0h = mm3(gh, hhhi[...], hhlo[...])
     gch, gcl = gchi[...], gclo[...]
     d1 = mm3(e0, gch, gcl) + mm3(e0h, gxhi[...], gxlo[...])
@@ -559,22 +555,26 @@
     send(parity, messages, oblk1, oblk0, oband1, oband0)
 
 
-def beside_third_kernel(dh, pr, xhi, xlo, d1, gohi, golo, r2o, w2o):
-    w2o[...] = mm3(d1[...], gohi[...], golo[...])
+def beside_third_kernel(
+    dh, pr, xhi, xlo, d1, e1, p2, gchi, gclo, gxhi, gxlo, gohi, golo, r2o, eo, gshi, gslo
+):
+    gch, gcl = gchi[...], gclo[...]
+    gxh, gxl = gxhi[...], gxlo[...]
+    gx = gxh.astype(f32) + gxl.astype(f32)
+    store2(gshi, gslo, gx + mm3(gx, gch, gcl))
+    w2 = mm3(d1[...], gohi[...], golo[...])
+    eo[...] = e1[...] + p2[...] + mm3(p2[...], gch, gcl) + mm3(w2, gxh, gxl)
     for j in range(AGG):
         r2o[j] = pr[j] + to_own(dh[j], xhi[j], xlo[j])
 
 
 def fourth_kernel(
-    parity, blk1, blk0, band1, band0, p2, w2, e1, gchi, gclo, gxhi, gxlo, r2, qp, aqhi, aqlo, tco,
+    parity, blk1, blk0, band1, band0, ep, gshi, gslo, gxhi, gxlo, r2, qp, aqhi, aqlo, tco,
     oblk1, oblk0, oband1, oband0, eo, f3o, pr3o,
 ):
     halo = receive(parity, blk1, blk0, band1, band0)
-    gxh, gxl = gxhi[...], gxlo[...]
-    d2 = p2[...] + mm3(halo_modes(halo, 0), gxh, gxl)
-    d2h = halo_modes(halo, STRIDE) + w2[...]
-    d3 = mm3(d2, gchi[...], gclo[...]) + mm3(d2h, gxh, gxl)
-    e = e1[...] + d2 + d3
+    e = ep[...] + mm3(halo_modes(halo, 0), gshi[...], gslo[...])
+    e = e + mm3(halo_modes(halo, STRIDE), gxhi[...], gxlo[...])
     eo[...] = e
     y = mm3(e, aqhi[...], aqlo[...])
     messages = []
@@ -615,7 +615,7 @@
         out.append(x3[j] + d4[j])
     for j in range(AGG):
         out.append(r3[j] - y[j] + to_own(d4h[j], xhi[j], xlo[j]))
-    turned = mm_exact(jnp.concatenate(out, axis=0), permutation_back())
+    turned = mm2(jnp.concatenate(out, axis=0), permutation_back())
     for j in range(AGG):
         field[j] = turned[j * COLS : (j + 1) * COLS]
         residual[j] = turned[(AGG + j) * COLS : (AGG + j + 1) * COLS]
@@ -677,9 +677,9 @@
     def message(height, width):
         return [((height, width), f32)] * 4
 
-    *out, tab = run(
+    *out, tab, tiles = run(
         first_kernel,
-        message(80, DOF) + [((24, PAIRS), f32)],
+        message(80, DOF) + [((24, PAIRS), f32), ((AGG, PAIRED, DOF, LANES), f32)],
         parity,
         load_columns[0, 0],
         stiffness[0, 0],
@@ -693,14 +693,13 @@
         far=8,
         scratch=[
             pltpu.VMEM((AGG, COLS, DOF), f32),
-            pltpu.VMEM((AGG, DOF, DOF), f32),
             pltpu.VMEM((MODES, AGG, DOF), bf16),
             pltpu.VMEM((AGG, SLOTS), jnp.int32),
             pltpu.VMEM((AGG, SLOTS), jnp.int32),
             pltpu.VMEM((AGG, PAIRS), jnp.int32),
             pltpu.VMEM((AGG, PAIRS), jnp.int32),
             pltpu.VMEM((AGG, PAIRS), f32),
-            pltpu.SemaphoreType.DMA((12,)),
+            pltpu.SemaphoreType.DMA((8 + AGG * PAIRED,)),
         ],
     )
     got = exchange(out)
@@ -709,14 +708,9 @@
         local_kernel,
         [square, square, local, local, broad, broad, ((WIDTH, WIDTH), f32), pair_tile, pair_tile, rows, rows]
         + [fields, modes, small, rows],
-        parity, *out, tab, stiffness[0, 0],
+        parity, *out, tab, tiles,
         scalars=1,
-        far=1,
-        scratch=[
-            pltpu.VMEM((AGG * LANES, AGG * LANES), f32),
-            pltpu.VMEM((AGG, PAIRED, DOF, LANES), f32),
-            pltpu.SemaphoreType.DMA((AGG * PAIRED,)),
-        ],
+        scratch=[pltpu.VMEM((AGG * LANES, AGG * LANES), f32)],
     )
     *out, xhi, xlo, rec, rech, qh, cdh, tco, tch, x2, r1, dlt, pg = run(
         second_kernel,
@@ -726,24 +720,28 @@
         scalars=1,
     )
     got = exchange(out)
-    pr, yhi, ylo, zhi, zlo, ghp, hhi, hlo, hhhi, hhlo, gchi, gclo, gxhi, gxlo, gohi, golo = run(
+    pr, yhi, ylo, zhi, zlo, vhi, vlo, q0, ghp, hhhi, hhlo, gchi, gclo, gxhi, gxlo, gohi, golo = run(
         inverse_kernel,
-        [fields, modes, modes, modes, modes, coarse] + [dense] * 10,
-        dlt, r1, pkhi, pklo, ghi, glo, qp, qh, dsum, cdh, tco, tch, xhi, xlo, big,
+        [fields] + [modes] * 6 + [coarse, coarse] + [dense] * 8,
+        pg, dlt, r1, pkhi, pklo, ghi, glo, qp, qh, dsum, cdh, tco, tch, xhi, xlo, big,
         scratch=[pltpu.VMEM((MODES, 2 * AGG, LANES), f32)],
     )
     *out, e1, d1, p2, dh = run(
         third_kernel,
         message(COLS, LANES) + [coarse, coarse, coarse, fields],
-        parity, *got, pg, ghp, yhi, ylo, hhi, hlo, hhhi, hhlo, gchi, gclo, gxhi, gxlo,
+        parity, *got, q0, ghp, vhi, vlo, hhhi, hhlo, gchi, gclo, gxhi, gxlo,
         scalars=1,
     )
     got = exchange(out)
-    r2, w2 = run(beside_third_kernel, [fields, coarse], dh, pr, xhi, xlo, d1, gohi, golo)
+    r2, ep, gshi, gslo = run(
+        beside_third_kernel,
+        [fields, coarse, dense, dense],
+        dh, pr, xhi, xlo, d1, e1, p2, gchi, gclo, gxhi, gxlo, gohi, golo,
+    )
     *out, e, f3, pr3 = run(
         fourth_kernel,
         message(COLS + 8, DOF) + [coarse, fields, fields],
-        parity, *got, p2, w2, e1, gchi, gclo, gxhi, gxlo, r2, qp, aqhi, aqlo, tco,
+        parity, *got, ep, gshi, gslo, gxhi, gxlo, r2, qp, aqhi, aqlo, tco,
         scalars=1,
     )
     got = exchange(out)

time: 61.7 us -> 61.3 us (level)
  Pallas kernels: 22.9 us -> 20.7 us
  waiting for transfers between devices: 12.2 us -> 13.6 us
    pallas_call x9, Pallas kernels: 22.9 us -> 20.7 us  [run(): pl.pallas_call(kernel, out_shape=[jax.ShapeDtypeStruct(shape, kind) for s...]
    ppermute x16, waiting for transfers between devices: 12.2 us -> 13.6 us  [swapped(): return lax.ppermute(x, axis, route)]
  transfers between devices with their start and end apart: 16 -> 16, of which waited for: 7 -> 8; matrix products, arithmetic and copies ran while one was open for 0% -> 0% of each run, Pallas kernels for 17% -> 14%
where the time goes in v4:
time: 61.3 us; the launch traced here: 61.2 us
  starting transfers between devices  26.1 us (43%)
  Pallas kernels  20.7 us (34%)
  waiting for transfers between devices  13.6 us (22%)
  between operations  0.75 us (1%)
    ppermute x16, starting transfers between devices, swapped(): return lax.ppermute(x, axis, route)  26.1 us
    pallas_call x9, Pallas kernels, run(): pl.pallas_call(kernel, out_shape=[jax.ShapeDtypeStruct(shape, kind) for s...  20.7 us
    ppermute x16, waiting for transfers between devices, swapped(): return lax.ppermute(x, axis, route)  13.6 us
  transfers between devices with their start and end apart: 16, of which 8 were waited for; matrix products, arithmetic and copies ran while one was open for 0% of the time, Pallas kernels for 14%

profile of v4, /device:TPU:32, one launch (start us, length us, event | category | flops | bytes accessed | tf_op | source)
XLA Modules:
  0.0 61.2 jit_solution(2175589414068896317)
XLA Ops:
  0.6 0.1 pad_add_fusion.parity
  0.7 3.9 %shard_map.95 = (f32[80,384]{1,0:T(8,128)S(1)}, f32[80,384]{1,0:T(8,128)S(1)}, f32[80,384]{1,0:T(8,128)S(1)}, f32[80,384]{1,0:T(8,128)S(1)}, f32[24,128]{1,0:T(8,128)S(1)}, /*index=5*/f32[4,3,384,128]{3,2,1,0:T(8,128)S(1)}) custom-call(s32[2]{0:T(128)S(1)} %pad_add_fusion.parity, f32[4,32,384]{2,1,0:T(8,128)} %bitcast.15, f32[4,384,384]{2,1,0:T(8,128)} %bitcast.14, ...), custom_call_target="tpu_custom_call" | custom-call | tf_op jit(solution)/shard_map/pallas_call | solution.py:634
  4.6 2.7 %collective-permute-start = (f32[80,384]{1,0:T(8,128)S(1)}, f32[80,384]{1,0:T(8,128)S(1)}, u32[]{:S(2)}, u32[]{:S(2)}) collective-permute-start(f32[80,384]{1,0:T(8,128)S(1)} %get-tuple-element.79.blk1), channel_id=1, source_target_pairs={{1,2},{2,1},{3,4},{4,3},{5,6},{6,5},{7,8},{8,7},{9,10},{10,9},{11,... | collective-permute-start | bytes 368648 | tf_op jit(solution)/shard_map/ppermute | solution.py:650
  7.3 2.3 %collective-permute-start.1 = (f32[80,384]{1,0:T(8,128)S(1)}, f32[80,384]{1,0:T(8,128)S(1)}, u32[]{:S(2)}, u32[]{:S(2)}) collective-permute-start(f32[80,384]{1,0:T(8,128)S(1)} %get-tuple-element.80.blk0), channel_id=1, source_target_pairs={{0,1},{1,0},{2,3},{3,2},{4,5},{5,4},{6,7},{7,6},{8,9},{9,8},{10,11... | collective-permute-start | bytes 368648 | tf_op jit(solution)/shard_map/ppermute | solution.py:650
  9.6 2.8 %collective-permute-start.2 = (f32[80,384]{1,0:T(8,128)S(1)}, f32[80,384]{1,0:T(8,128)S(1)}, u32[]{:S(2)}, u32[]{:S(2)}) collective-permute-start(f32[80,384]{1,0:T(8,128)S(1)} %get-tuple-element.81.band1), channel_id=1, source_target_pairs={{16,32},{32,16},{48,64},{64,48},{80,96},{96,80},{112,128},{128,112... | collective-permute-start | bytes 368648 | tf_op jit(solution)/shard_map/ppermute | solution.py:650
  12.4 0.0 collective-permute-start.3
  12.4 4.2 %shard_map.96 = (bf16[4,384,384]{2,1,0:T(8,128)(2,1)S(1)}, bf16[4,384,384]{2,1,0:T(8,128)(2,1)S(1)}, bf16[512,512]{1,0:T(8,128)(2,1)S(1)}, bf16[512,512]{1,0:T(8...) custom-call(s32[2]{0:T(128)S(1)} %pad_add_fusion.parity, ...), custom_call_target="tpu_custom_call" | custom-call | tf_op jit(solution)/shard_map/pallas_call | solution.py:634
  16.7 2.9 %collective-permute-done.2.band1 = f32[80,384]{1,0:T(8,128)S(1)} collective-permute-done((f32[80,384]{1,0:T(8,128)S(1)}, f32[80,384]{1,0:T(8,128)S(1)}, u32[]{:S(2)}, u32[]{:S(2)}) %collective-permute-start.2) | collective-permute-done | bytes 122912 | tf_op jit(solution)/shard_map/ppermute | solution.py:650
  19.6 3.0 %shard_map.97 = (f32[40,384]{1,0:T(8,128)S(1)}, f32[40,384]{1,0:T(8,128)S(1)}, f32[40,384]{1,0:T(8,128)S(1)}, f32[40,384]{1,0:T(8,128)S(1)}, bf16[4,128,128]{2,1...) custom-call(s32[2]{0:T(128)S(1)} %pad_add_fusion.parity, ...), custom_call_target="tpu_custom_call" | custom-call | tf_op jit(solution)/shard_map/pallas_call | solution.py:634
  22.6 4.3 %collective-permute-start.4 = (f32[40,384]{1,0:T(8,128)S(1)}, f32[40,384]{1,0:T(8,128)S(1)}, u32[]{:S(2)}, u32[]{:S(2)}) collective-permute-start(f32[40,384]{1,0:T(8,128)S(1)} %get-tuple-element.98), channel_id=1, source_target_pairs={{1,2},{2,1},{3,4},{4,3},{5,6},{6,5},{7,8},{8,7},{9,10},{10,9},{11,... | collective-permute-start | bytes 184328 | tf_op jit(solution)/shard_map/ppermute | solution.py:650
  26.8 0.7 %collective-permute-start.5 = (f32[40,384]{1,0:T(8,128)S(1)}, f32[40,384]{1,0:T(8,128)S(1)}, u32[]{:S(2)}, u32[]{:S(2)}) collective-permute-start(f32[40,384]{1,0:T(8,128)S(1)} %get-tuple-element.99), channel_id=1, source_target_pairs={{0,1},{1,0},{2,3},{3,2},{4,5},{5,4},{6,7},{7,6},{8,9},{9,8},{10,11... | collective-permute-start | bytes 184328 | tf_op jit(solution)/shard_map/ppermute | solution.py:650
  27.5 0.4 collective-permute-start.6
  27.9 0.0 collective-permute-start.7
  27.9 3.4 %shard_map.98 = (f32[4,32,384]{2,1,0:T(8,128)S(1)}, bf16[4,64,384]{2,1,0:T(8,128)(2,1)S(1)}, bf16[4,64,384]{2,1,0:T(8,128)(2,1)S(1)}, bf16[4,64,384]{2,1,0:T(8,1...) custom-call(f32[32,256]{1,0:T(8,128)S(1)} %get-tuple-element.102.pg,, ...), custom_call_target="tpu_custom_call" | custom-call | tf_op jit(solution)/shard_map/pallas_call | solution.py:634
  31.4 1.2 %collective-permute-done.5.blk0 = f32[40,384]{1,0:T(8,128)S(1)} collective-permute-done((f32[40,384]{1,0:T(8,128)S(1)}, f32[40,384]{1,0:T(8,128)S(1)}, u32[]{:S(2)}, u32[]{:S(2)}) %collective-permute-start.5) | collective-permute-done | bytes 61472 | tf_op jit(solution)/shard_map/ppermute | solution.py:650
  32.6 0.7 %collective-permute-done.6.band1 = f32[40,384]{1,0:T(8,128)S(1)} collective-permute-done((f32[40,384]{1,0:T(8,128)S(1)}, f32[40,384]{1,0:T(8,128)S(1)}, u32[]{:S(2)}, u32[]{:S(2)}) %collective-permute-start.6) | collective-permute-done | bytes 61472 | tf_op jit(solution)/shard_map/ppermute | solution.py:650
  33.3 1.3 %shard_map.99 = (f32[32,128]{1,0:T(8,128)S(1)}, f32[32,128]{1,0:T(8,128)S(1)}, f32[32,128]{1,0:T(8,128)S(1)}, f32[32,128]{1,0:T(8,128)S(1)}, f32[32,256]{1,0:T(8...) custom-call(s32[2]{0:T(128)S(1)} %pad_add_fusion.parity, ...), custom_call_target="tpu_custom_call" | custom-call | tf_op jit(solution)/shard_map/pallas_call | solution.py:634
  34.6 5.8 %collective-permute-start.8 = (f32[32,128]{1,0:T(8,128)S(1)}, f32[32,128]{1,0:T(8,128)S(1)}, u32[]{:S(2)}, u32[]{:S(2)}) collective-permute-start(f32[32,128]{1,0:T(8,128)S(1)} %get-tuple-element.123), channel_id=1, source_target_pairs={{1,2},{2,1},{3,4},{4,3},{5,6},{6,5},{7,8},{8,7},{9,10},{10,9},{11,... | collective-permute-start | bytes 49160 | tf_op jit(solution)/shard_map/ppermute | solution.py:650
  40.5 0.4 collective-permute-start.9
  40.8 1.0 %collective-permute-start.10 = (f32[32,128]{1,0:T(8,128)S(1)}, f32[32,128]{1,0:T(8,128)S(1)}, u32[]{:S(2)}, u32[]{:S(2)}) collective-permute-start(f32[32,128]{1,0:T(8,128)S(1)} %get-tuple-element.125), channel_id=1, source_target_pairs={{16,32},{32,16},{48,64},{64,48},{80,96},{96,80},{112,128},{128,112... | collective-permute-start | bytes 49160 | tf_op jit(solution)/shard_map/ppermute | solution.py:650
  41.9 0.5 shard_map.100
  42.4 3.3 %collective-permute-done.9.blk0 = f32[32,128]{1,0:T(8,128)S(1)} collective-permute-done((f32[32,128]{1,0:T(8,128)S(1)}, f32[32,128]{1,0:T(8,128)S(1)}, u32[]{:S(2)}, u32[]{:S(2)}) %collective-permute-start.9) | collective-permute-done | bytes 16416 | tf_op jit(solution)/shard_map/ppermute | solution.py:650
  45.7 0.4 collective-permute-done.10.band1
  46.1 1.3 %shard_map.101 = (f32[40,384]{1,0:T(8,128)S(1)}, f32[40,384]{1,0:T(8,128)S(1)}, f32[40,384]{1,0:T(8,128)S(1)}, f32[40,384]{1,0:T(8,128)S(1)}, f32[32,256]{1,0:T(...) custom-call(s32[2]{0:T(128)S(1)} %pad_add_fusion.parity, f32[32,128]{1,0:T(8,128)S(1)} %collective-permute-done.8.blk1, ...), custom_call_target="tpu_custom_call" | custom-call | tf_op jit(solution)/shard_map/pallas_call | solution.py:634
  47.4 3.7 %collective-permute-start.12 = (f32[40,384]{1,0:T(8,128)S(1)}, f32[40,384]{1,0:T(8,128)S(1)}, u32[]{:S(2)}, u32[]{:S(2)}) collective-permute-start(f32[40,384]{1,0:T(8,128)S(1)} %get-tuple-element.138), channel_id=1, source_target_pairs={{1,2},{2,1},{3,4},{4,3},{5,6},{6,5},{7,8},{8,7},{9,10},{10,9},{11,... | collective-permute-start | bytes 184328 | tf_op jit(solution)/shard_map/ppermute | solution.py:650
  51.1 1.6 %collective-permute-start.13 = (f32[40,384]{1,0:T(8,128)S(1)}, f32[40,384]{1,0:T(8,128)S(1)}, u32[]{:S(2)}, u32[]{:S(2)}) collective-permute-start(f32[40,384]{1,0:T(8,128)S(1)} %get-tuple-element.139), channel_id=1, source_target_pairs={{0,1},{1,0},{2,3},{3,2},{4,5},{5,4},{6,7},{7,6},{8,9},{9,8},{10,11... | collective-permute-start | bytes 184328 | tf_op jit(solution)/shard_map/ppermute | solution.py:650
  52.7 0.5 collective-permute-start.14
  53.2 0.3 shard_map.102
  53.4 0.7 %collective-permute-done.12.blk1 = f32[40,384]{1,0:T(8,128)S(1)} collective-permute-done((f32[40,384]{1,0:T(8,128)S(1)}, f32[40,384]{1,0:T(8,128)S(1)}, u32[]{:S(2)}, u32[]{:S(2)}) %collective-permute-start.12) | collective-permute-done | bytes 61472 | tf_op jit(solution)/shard_map/ppermute | solution.py:650
  54.1 2.7 %collective-permute-done.13.blk0 = f32[40,384]{1,0:T(8,128)S(1)} collective-permute-done((f32[40,384]{1,0:T(8,128)S(1)}, f32[40,384]{1,0:T(8,128)S(1)}, u32[]{:S(2)}, u32[]{:S(2)}) %collective-permute-start.13) | collective-permute-done | bytes 61472 | tf_op jit(solution)/shard_map/ppermute | solution.py:650
  56.9 1.6 %collective-permute-done.14.band1 = f32[40,384]{1,0:T(8,128)S(1)} collective-permute-done((f32[40,384]{1,0:T(8,128)S(1)}, f32[40,384]{1,0:T(8,128)S(1)}, u32[]{:S(2)}, u32[]{:S(2)}) %collective-permute-start.14) | collective-permute-done | bytes 61472 | tf_op jit(solution)/shard_map/ppermute | solution.py:650
  58.5 2.7 %shard_map.103 = (f32[4,32,384]{2,1,0:T(8,128)}, f32[4,32,384]{2,1,0:T(8,128)}) custom-call(s32[2]{0:T(128)S(1)} %pad_add_fusion.parity, f32[40,384]{1,0:T(8,128)S(1)} %collective-permute-done.12.blk1, f32[40,384]{1,0:T(8,128)S(1)} %collective-permute-done.13.blk0, f32[40,384]{1,0:T(8,128)S(1)} %collective-permute-done.14.band1, ...), custom_call_target="tpu_custom_call" | custom-call | tf_op jit(solution)/shard_map/pallas_call | solution.py:634
  (10 shorter events, 0.0 us)
Async XLA Ops:
  4.6 12.1 %collective-permute-start = (f32[80,384]{1,0:T(8,128)S(1)}, f32[80,384]{1,0:T(8,128)S(1)}, u32[]{:S(2)}, u32[]{:S(2)}) collective-permute-start(f32[80,384]{1,0:T(8,128)S(1)} %get-tuple-element.79.blk1), channel_id=1, source_target_pairs={{1,2},{2,1},{3,4},{4,3},{5,6},{6,5},{7,8},{8,7},{9,10},{10,9},{11,... | collective-permute-start | bytes 368648 | tf_op jit(solution)/shard_map/ppermute | solution.py:650
  7.3 9.4 %collective-permute-start.1 = (f32[80,384]{1,0:T(8,128)S(1)}, f32[80,384]{1,0:T(8,128)S(1)}, u32[]{:S(2)}, u32[]{:S(2)}) collective-permute-start(f32[80,384]{1,0:T(8,128)S(1)} %get-tuple-element.80.blk0), channel_id=1, source_target_pairs={{0,1},{1,0},{2,3},{3,2},{4,5},{5,4},{6,7},{7,6},{8,9},{9,8},{10,11... | collective-permute-start | bytes 368648 | tf_op jit(solution)/shard_map/ppermute | solution.py:650
  9.6 10.0 %collective-permute-start.2 = (f32[80,384]{1,0:T(8,128)S(1)}, f32[80,384]{1,0:T(8,128)S(1)}, u32[]{:S(2)}, u32[]{:S(2)}) collective-permute-start(f32[80,384]{1,0:T(8,128)S(1)} %get-tuple-element.81.band1), channel_id=1, source_target_pairs={{16,32},{32,16},{48,64},{64,48},{80,96},{96,80},{112,128},{128,112... | collective-permute-start | bytes 368648 | tf_op jit(solution)/shard_map/ppermute | solution.py:650
  12.4 7.1 %collective-permute-start.3 = (f32[80,384]{1,0:T(8,128)S(1)}, f32[80,384]{1,0:T(8,128)S(1)}, u32[]{:S(2)}, u32[]{:S(2)}) collective-permute-start(f32[80,384]{1,0:T(8,128)S(1)} %get-tuple-element.82.band0), channel_id=1, source_target_pairs={{0,16},{16,0},{32,48},{48,32},{64,80},{80,64},{96,112},{112,96},{1... | collective-permute-start | bytes 368648 | tf_op jit(solution)/shard_map/ppermute | solution.py:650
  22.6 8.8 %collective-permute-start.4 = (f32[40,384]{1,0:T(8,128)S(1)}, f32[40,384]{1,0:T(8,128)S(1)}, u32[]{:S(2)}, u32[]{:S(2)}) collective-permute-start(f32[40,384]{1,0:T(8,128)S(1)} %get-tuple-element.98), channel_id=1, source_target_pairs={{1,2},{2,1},{3,4},{4,3},{5,6},{6,5},{7,8},{8,7},{9,10},{10,9},{11,... | collective-permute-start | bytes 184328 | tf_op jit(solution)/shard_map/ppermute | solution.py:650
  26.8 5.7 %collective-permute-start.5 = (f32[40,384]{1,0:T(8,128)S(1)}, f32[40,384]{1,0:T(8,128)S(1)}, u32[]{:S(2)}, u32[]{:S(2)}) collective-permute-start(f32[40,384]{1,0:T(8,128)S(1)} %get-tuple-element.99), channel_id=1, source_target_pairs={{0,1},{1,0},{2,3},{3,2},{4,5},{5,4},{6,7},{7,6},{8,9},{9,8},{10,11... | collective-permute-start | bytes 184328 | tf_op jit(solution)/shard_map/ppermute | solution.py:650
  27.5 5.8 %collective-permute-start.6 = (f32[40,384]{1,0:T(8,128)S(1)}, f32[40,384]{1,0:T(8,128)S(1)}, u32[]{:S(2)}, u32[]{:S(2)}) collective-permute-start(f32[40,384]{1,0:T(8,128)S(1)} %get-tuple-element.100), channel_id=1, source_target_pairs={{16,32},{32,16},{48,64},{64,48},{80,96},{96,80},{112,128},{128,112... | collective-permute-start | bytes 184328 | tf_op jit(solution)/shard_map/ppermute | solution.py:650
  27.9 5.4 %collective-permute-start.7 = (f32[40,384]{1,0:T(8,128)S(1)}, f32[40,384]{1,0:T(8,128)S(1)}, u32[]{:S(2)}, u32[]{:S(2)}) collective-permute-start(f32[40,384]{1,0:T(8,128)S(1)} %get-tuple-element.101), channel_id=1, source_target_pairs={{0,16},{16,0},{32,48},{48,32},{64,80},{80,64},{96,112},{112,96},{1... | collective-permute-start | bytes 184328 | tf_op jit(solution)/shard_map/ppermute | solution.py:650
  34.6 7.7 %collective-permute-start.8 = (f32[32,128]{1,0:T(8,128)S(1)}, f32[32,128]{1,0:T(8,128)S(1)}, u32[]{:S(2)}, u32[]{:S(2)}) collective-permute-start(f32[32,128]{1,0:T(8,128)S(1)} %get-tuple-element.123), channel_id=1, source_target_pairs={{1,2},{2,1},{3,4},{4,3},{5,6},{6,5},{7,8},{8,7},{9,10},{10,9},{11,... | collective-permute-start | bytes 49160 | tf_op jit(solution)/shard_map/ppermute | solution.py:650
  40.5 5.2 %collective-permute-start.9 = (f32[32,128]{1,0:T(8,128)S(1)}, f32[32,128]{1,0:T(8,128)S(1)}, u32[]{:S(2)}, u32[]{:S(2)}) collective-permute-start(f32[32,128]{1,0:T(8,128)S(1)} %get-tuple-element.124), channel_id=1, source_target_pairs={{0,1},{1,0},{2,3},{3,2},{4,5},{5,4},{6,7},{7,6},{8,9},{9,8},{10,11... | collective-permute-start | bytes 49160 | tf_op jit(solution)/shard_map/ppermute | solution.py:650
  40.8 5.3 %collective-permute-start.10 = (f32[32,128]{1,0:T(8,128)S(1)}, f32[32,128]{1,0:T(8,128)S(1)}, u32[]{:S(2)}, u32[]{:S(2)}) collective-permute-start(f32[32,128]{1,0:T(8,128)S(1)} %get-tuple-element.125), channel_id=1, source_target_pairs={{16,32},{32,16},{48,64},{64,48},{80,96},{96,80},{112,128},{128,112... | collective-permute-start | bytes 49160 | tf_op jit(solution)/shard_map/ppermute | solution.py:650
  41.9 4.3 %collective-permute-start.11 = (f32[32,128]{1,0:T(8,128)S(1)}, f32[32,128]{1,0:T(8,128)S(1)}, u32[]{:S(2)}, u32[]{:S(2)}) collective-permute-start(f32[32,128]{1,0:T(8,128)S(1)} %get-tuple-element.126), channel_id=1, source_target_pairs={{0,16},{16,0},{32,48},{48,32},{64,80},{80,64},{96,112},{112,96},{1... | collective-permute-start | bytes 49160 | tf_op jit(solution)/shard_map/ppermute | solution.py:650
  47.4 6.7 %collective-permute-start.12 = (f32[40,384]{1,0:T(8,128)S(1)}, f32[40,384]{1,0:T(8,128)S(1)}, u32[]{:S(2)}, u32[]{:S(2)}) collective-permute-start(f32[40,384]{1,0:T(8,128)S(1)} %get-tuple-element.138), channel_id=1, source_target_pairs={{1,2},{2,1},{3,4},{4,3},{5,6},{6,5},{7,8},{8,7},{9,10},{10,9},{11,... | collective-permute-start | bytes 184328 | tf_op jit(solution)/shard_map/ppermute | solution.py:650
  51.1 5.7 %collective-permute-start.13 = (f32[40,384]{1,0:T(8,128)S(1)}, f32[40,384]{1,0:T(8,128)S(1)}, u32[]{:S(2)}, u32[]{:S(2)}) collective-permute-start(f32[40,384]{1,0:T(8,128)S(1)} %get-tuple-element.139), channel_id=1, source_target_pairs={{0,1},{1,0},{2,3},{3,2},{4,5},{5,4},{6,7},{7,6},{8,9},{9,8},{10,11... | collective-permute-start | bytes 184328 | tf_op jit(solution)/shard_map/ppermute | solution.py:650
  52.7 5.8 %collective-permute-start.14 = (f32[40,384]{1,0:T(8,128)S(1)}, f32[40,384]{1,0:T(8,128)S(1)}, u32[]{:S(2)}, u32[]{:S(2)}) collective-permute-start(f32[40,384]{1,0:T(8,128)S(1)} %get-tuple-element.140), channel_id=1, source_target_pairs={{16,32},{32,16},{48,64},{64,48},{80,96},{96,80},{112,128},{128,112... | collective-permute-start | bytes 184328 | tf_op jit(solution)/shard_map/ppermute | solution.py:650
  53.2 5.3 %collective-permute-start.15 = (f32[40,384]{1,0:T(8,128)S(1)}, f32[40,384]{1,0:T(8,128)S(1)}, u32[]{:S(2)}, u32[]{:S(2)}) collective-permute-start(f32[40,384]{1,0:T(8,128)S(1)} %get-tuple-element.141), channel_id=1, source_target_pairs={{0,16},{16,0},{32,48},{48,32},{64,80},{80,64},{96,112},{112,96},{1... | collective-permute-start | bytes 184328 | tf_op jit(solution)/shard_map/ppermute | solution.py:650

commit v5 on v4

--- a/solution.py
+++ b/solution.py
@@ -326,7 +326,7 @@
 
 def local_kernel(
     parity, blk1, blk0, band1, band0, tab, k,
-    pkhi, pklo, ghi, glo, aqhi, aqlo, big, xhi, xlo, tco, tch, bp, qp, dsum, dloc, work,
+    pkhi, pklo, ghi, glo, aqhi, aqlo, big, xhi, xlo, tco, tch, bp, qp, dsum, dloc, early, work,
 ):
     for a, sent in enumerate(receive(parity, blk1, blk0, band1, band0)):
         bp[a] = sent[0:COLS]
@@ -388,12 +388,15 @@
         tco[j : j + 1], tch[j : j + 1] = pair_weights(
             tab[j : j + 1], tab[4 + j : 5 + j], tab[16 + j : 17 + j], xhi, xlo, j - 2
         )
+    for j in range(2, AGG):
+        x = fine_damping / (dloc[j : j + 1] + tco[j : j + 1]) * bp[j]
+        early[j - 2] = mm3(x, pkhi[j], pklo[j])
     tco[0:2] = jnp.zeros((2, DOF), f32)
     tch[0:2] = jnp.zeros((2, DOF), f32)
 
 
 def second_kernel(
-    parity, blk1, blk0, band1, band0, bp, qp, dloc, khi, klo, ghi, glo, aqhi, aqlo, x2hi, x2lo, t2o, t2h,
+    parity, blk1, blk0, band1, band0, bp, qp, dloc, khi, klo, ghi, glo, aqhi, aqlo, x2hi, x2lo, t2o, t2h, early,
     oblk1, oblk0, oband1, oband0, xhi, xlo, rec, rech, qh, cdh, tco, tch, x2o, r1o, dlt, pgo,
 ):
     halo = receive(parity, blk1, blk0, band1, band0)
@@ -419,9 +422,11 @@
         cdh[j] = sent_diagonal(halo[j])
         xs.append(inverse * bp[j])
         xh.append(inverseh * halo[j][0:COLS])
-    kh = [khi[a] for a in range(AGG)]
-    kl = [klo[a] for a in range(AGG)]
-    y = local_product(xs, kh, kl, ghi[...], glo[...], cross)
+    springs = unstack_fields(mm3(stack_fields(xs), ghi[...], glo[...]), AGG)
+    y = []
+    for a in range(AGG):
+        bend = mm3(xs[a], khi[a], klo[a]) if a < 2 else early[a - 2]
+        y.append(bend + (springs[a] + xs[a] * cross[a]))
     d, pg = [], []
     for j in range(AGG):
         r1 = bp[j] - y[j] + to_own(xh[j], xhi[j], xlo[j])
@@ -704,10 +709,10 @@
     )
     got = exchange(out)
     pair_tile = ((2, LANES, LANES), bf16)
-    pkhi, pklo, ghi, glo, aqhi, aqlo, big, x2hi, x2lo, t2o, t2h, bp, qp, dsum, dloc = run(
+    pkhi, pklo, ghi, glo, aqhi, aqlo, big, x2hi, x2lo, t2o, t2h, bp, qp, dsum, dloc, early = run(
         local_kernel,
         [square, square, local, local, broad, broad, ((WIDTH, WIDTH), f32), pair_tile, pair_tile, rows, rows]
-        + [fields, modes, small, rows],
+        + [fields, modes, small, rows, ((2, COLS, DOF), f32)],
         parity, *out, tab, tiles,
         scalars=1,
         scratch=[pltpu.VMEM((AGG * LANES, AGG * LANES), f32)],
@@ -716,7 +721,7 @@
         second_kernel,
         message(COLS + 8, DOF)
         + [tile, tile, rows, rows, modes, small, rows, rows, fields, fields, fields, coarse],
-        parity, *got, bp, qp, dloc, pkhi, pklo, ghi, glo, aqhi, aqlo, x2hi, x2lo, t2o, t2h,
+        parity, *got, bp, qp, dloc, pkhi, pklo, ghi, glo, aqhi, aqlo, x2hi, x2lo, t2o, t2h, early,
         scalars=1,
     )
     got = exchange(out)

time: 61.3 us -> 61.1 us (level)
  no operation moved by 1% of the time
where the time goes in v5:
time: 61.1 us; the launch traced here: 61 us
  starting transfers between devices  26.1 us (43%)
  Pallas kernels  20.6 us (34%)
  waiting for transfers between devices  13.5 us (22%)
  between operations  0.73 us (1%)
    ppermute x16, starting transfers between devices, swapped(): return lax.ppermute(x, axis, route)  26.1 us
    pallas_call x9, Pallas kernels, run(): pl.pallas_call(kernel, out_shape=[jax.ShapeDtypeStruct(shape, kind) for s...  20.6 us
    ppermute x16, waiting for transfers between devices, swapped(): return lax.ppermute(x, axis, route)  13.5 us
  transfers between devices with their start and end apart: 16, of which 8 were waited for; matrix products, arithmetic and copies ran while one was open for 0% of the time, Pallas kernels for 14%

profile of v5, /device:TPU:32, one launch (start us, length us, event | category | flops | bytes accessed | tf_op | source)
XLA Modules:
  0.0 61.0 jit_solution(14296852715093618475)
XLA Ops:
  0.6 0.1 pad_add_fusion.parity
  0.7 3.9 %shard_map.95 = (f32[80,384]{1,0:T(8,128)S(1)}, f32[80,384]{1,0:T(8,128)S(1)}, f32[80,384]{1,0:T(8,128)S(1)}, f32[80,384]{1,0:T(8,128)S(1)}, f32[24,128]{1,0:T(8,128)S(1)}, /*index=5*/f32[4,3,384,128]{3,2,1,0:T(8,128)S(1)}) custom-call(s32[2]{0:T(128)S(1)} %pad_add_fusion.parity, f32[4,32,384]{2,1,0:T(8,128)} %bitcast.15, f32[4,384,384]{2,1,0:T(8,128)} %bitcast.14, ...), custom_call_target="tpu_custom_call" | custom-call | tf_op jit(solution)/shard_map/pallas_call | solution.py:639
  4.6 2.7 %collective-permute-start = (f32[80,384]{1,0:T(8,128)S(1)}, f32[80,384]{1,0:T(8,128)S(1)}, u32[]{:S(2)}, u32[]{:S(2)}) collective-permute-start(f32[80,384]{1,0:T(8,128)S(1)} %get-tuple-element.80.blk1), channel_id=1, source_target_pairs={{1,2},{2,1},{3,4},{4,3},{5,6},{6,5},{7,8},{8,7},{9,10},{10,9},{11,... | collective-permute-start | bytes 368648 | tf_op jit(solution)/shard_map/ppermute | solution.py:655
  7.3 2.3 %collective-permute-start.1 = (f32[80,384]{1,0:T(8,128)S(1)}, f32[80,384]{1,0:T(8,128)S(1)}, u32[]{:S(2)}, u32[]{:S(2)}) collective-permute-start(f32[80,384]{1,0:T(8,128)S(1)} %get-tuple-element.81.blk0), channel_id=1, source_target_pairs={{0,1},{1,0},{2,3},{3,2},{4,5},{5,4},{6,7},{7,6},{8,9},{9,8},{10,11... | collective-permute-start | bytes 368648 | tf_op jit(solution)/shard_map/ppermute | solution.py:655
  9.6 2.8 %collective-permute-start.2 = (f32[80,384]{1,0:T(8,128)S(1)}, f32[80,384]{1,0:T(8,128)S(1)}, u32[]{:S(2)}, u32[]{:S(2)}) collective-permute-start(f32[80,384]{1,0:T(8,128)S(1)} %get-tuple-element.82.band1), channel_id=1, source_target_pairs={{16,32},{32,16},{48,64},{64,48},{80,96},{96,80},{112,128},{128,112... | collective-permute-start | bytes 368648 | tf_op jit(solution)/shard_map/ppermute | solution.py:655
  12.4 4.3 %shard_map.96 = (bf16[4,384,384]{2,1,0:T(8,128)(2,1)S(1)}, bf16[4,384,384]{2,1,0:T(8,128)(2,1)S(1)}, bf16[512,512]{1,0:T(8,128)(2,1)S(1)}, bf16[512,512]{1,0:T(8...) custom-call(s32[2]{0:T(128)S(1)} %pad_add_fusion.parity, ...), custom_call_target="tpu_custom_call" | custom-call | tf_op jit(solution)/shard_map/pallas_call | solution.py:639
  16.7 0.0 collective-permute-done.1.blk0
  16.8 2.8 %collective-permute-done.2.band1 = f32[80,384]{1,0:T(8,128)S(1)} collective-permute-done((f32[80,384]{1,0:T(8,128)S(1)}, f32[80,384]{1,0:T(8,128)S(1)}, u32[]{:S(2)}, u32[]{:S(2)}) %collective-permute-start.2) | collective-permute-done | bytes 122912 | tf_op jit(solution)/shard_map/ppermute | solution.py:655
  19.6 2.8 %shard_map.97 = (f32[40,384]{1,0:T(8,128)S(1)}, f32[40,384]{1,0:T(8,128)S(1)}, f32[40,384]{1,0:T(8,128)S(1)}, f32[40,384]{1,0:T(8,128)S(1)}, bf16[4,128,128]{2,1...) custom-call(s32[2]{0:T(128)S(1)} %pad_add_fusion.parity, ...), custom_call_target="tpu_custom_call" | custom-call | tf_op jit(solution)/shard_map/pallas_call | solution.py:639
  22.4 4.3 %collective-permute-start.4 = (f32[40,384]{1,0:T(8,128)S(1)}, f32[40,384]{1,0:T(8,128)S(1)}, u32[]{:S(2)}, u32[]{:S(2)}) collective-permute-start(f32[40,384]{1,0:T(8,128)S(1)} %get-tuple-element.100), channel_id=1, source_target_pairs={{1,2},{2,1},{3,4},{4,3},{5,6},{6,5},{7,8},{8,7},{9,10},{10,9},{11,... | collective-permute-start | bytes 184328 | tf_op jit(solution)/shard_map/ppermute | solution.py:655
  26.7 0.7 %collective-permute-start.5 = (f32[40,384]{1,0:T(8,128)S(1)}, f32[40,384]{1,0:T(8,128)S(1)}, u32[]{:S(2)}, u32[]{:S(2)}) collective-permute-start(f32[40,384]{1,0:T(8,128)S(1)} %get-tuple-element.101), channel_id=1, source_target_pairs={{0,1},{1,0},{2,3},{3,2},{4,5},{5,4},{6,7},{7,6},{8,9},{9,8},{10,11... | collective-permute-start | bytes 184328 | tf_op jit(solution)/shard_map/ppermute | solution.py:655
  27.3 0.4 collective-permute-start.6
  27.7 0.0 collective-permute-start.7
  27.7 3.4 %shard_map.98 = (f32[4,32,384]{2,1,0:T(8,128)S(1)}, bf16[4,64,384]{2,1,0:T(8,128)(2,1)S(1)}, bf16[4,64,384]{2,1,0:T(8,128)(2,1)S(1)}, bf16[4,64,384]{2,1,0:T(8,1...) custom-call(f32[32,256]{1,0:T(8,128)S(1)} %get-tuple-element.104.pg,, ...), custom_call_target="tpu_custom_call" | custom-call | tf_op jit(solution)/shard_map/pallas_call | solution.py:639
  31.2 1.2 %collective-permute-done.5.blk0 = f32[40,384]{1,0:T(8,128)S(1)} collective-permute-done((f32[40,384]{1,0:T(8,128)S(1)}, f32[40,384]{1,0:T(8,128)S(1)}, u32[]{:S(2)}, u32[]{:S(2)}) %collective-permute-start.5) | collective-permute-done | bytes 61472 | tf_op jit(solution)/shard_map/ppermute | solution.py:655
  32.4 0.7 %collective-permute-done.6.band1 = f32[40,384]{1,0:T(8,128)S(1)} collective-permute-done((f32[40,384]{1,0:T(8,128)S(1)}, f32[40,384]{1,0:T(8,128)S(1)}, u32[]{:S(2)}, u32[]{:S(2)}) %collective-permute-start.6) | collective-permute-done | bytes 61472 | tf_op jit(solution)/shard_map/ppermute | solution.py:655
  33.1 1.3 %shard_map.99 = (f32[32,128]{1,0:T(8,128)S(1)}, f32[32,128]{1,0:T(8,128)S(1)}, f32[32,128]{1,0:T(8,128)S(1)}, f32[32,128]{1,0:T(8,128)S(1)}, f32[32,256]{1,0:T(8...) custom-call(s32[2]{0:T(128)S(1)} %pad_add_fusion.parity, ...), custom_call_target="tpu_custom_call" | custom-call | tf_op jit(solution)/shard_map/pallas_call | solution.py:639
  34.5 5.8 %collective-permute-start.8 = (f32[32,128]{1,0:T(8,128)S(1)}, f32[32,128]{1,0:T(8,128)S(1)}, u32[]{:S(2)}, u32[]{:S(2)}) collective-permute-start(f32[32,128]{1,0:T(8,128)S(1)} %get-tuple-element.125), channel_id=1, source_target_pairs={{1,2},{2,1},{3,4},{4,3},{5,6},{6,5},{7,8},{8,7},{9,10},{10,9},{11,... | collective-permute-start | bytes 49160 | tf_op jit(solution)/shard_map/ppermute | solution.py:655
  40.3 0.4 collective-permute-start.9
  40.6 1.0 %collective-permute-start.10 = (f32[32,128]{1,0:T(8,128)S(1)}, f32[32,128]{1,0:T(8,128)S(1)}, u32[]{:S(2)}, u32[]{:S(2)}) collective-permute-start(f32[32,128]{1,0:T(8,128)S(1)} %get-tuple-element.127), channel_id=1, source_target_pairs={{16,32},{32,16},{48,64},{64,48},{80,96},{96,80},{112,128},{128,112... | collective-permute-start | bytes 49160 | tf_op jit(solution)/shard_map/ppermute | solution.py:655
  41.7 0.5 shard_map.100
  42.2 3.3 %collective-permute-done.9.blk0 = f32[32,128]{1,0:T(8,128)S(1)} collective-permute-done((f32[32,128]{1,0:T(8,128)S(1)}, f32[32,128]{1,0:T(8,128)S(1)}, u32[]{:S(2)}, u32[]{:S(2)}) %collective-permute-start.9) | collective-permute-done | bytes 16416 | tf_op jit(solution)/shard_map/ppermute | solution.py:655
  45.5 0.4 collective-permute-done.10.band1
  45.9 1.3 %shard_map.101 = (f32[40,384]{1,0:T(8,128)S(1)}, f32[40,384]{1,0:T(8,128)S(1)}, f32[40,384]{1,0:T(8,128)S(1)}, f32[40,384]{1,0:T(8,128)S(1)}, f32[32,256]{1,0:T(...) custom-call(s32[2]{0:T(128)S(1)} %pad_add_fusion.parity, f32[32,128]{1,0:T(8,128)S(1)} %collective-permute-done.8.blk1, ...), custom_call_target="tpu_custom_call" | custom-call | tf_op jit(solution)/shard_map/pallas_call | solution.py:639
  47.2 3.7 %collective-permute-start.12 = (f32[40,384]{1,0:T(8,128)S(1)}, f32[40,384]{1,0:T(8,128)S(1)}, u32[]{:S(2)}, u32[]{:S(2)}) collective-permute-start(f32[40,384]{1,0:T(8,128)S(1)} %get-tuple-element.140), channel_id=1, source_target_pairs={{1,2},{2,1},{3,4},{4,3},{5,6},{6,5},{7,8},{8,7},{9,10},{10,9},{11,... | collective-permute-start | bytes 184328 | tf_op jit(solution)/shard_map/ppermute | solution.py:655
  50.9 1.6 %collective-permute-start.13 = (f32[40,384]{1,0:T(8,128)S(1)}, f32[40,384]{1,0:T(8,128)S(1)}, u32[]{:S(2)}, u32[]{:S(2)}) collective-permute-start(f32[40,384]{1,0:T(8,128)S(1)} %get-tuple-element.141), channel_id=1, source_target_pairs={{0,1},{1,0},{2,3},{3,2},{4,5},{5,4},{6,7},{7,6},{8,9},{9,8},{10,11... | collective-permute-start | bytes 184328 | tf_op jit(solution)/shard_map/ppermute | solution.py:655
  52.5 0.5 collective-permute-start.14
  53.0 0.3 shard_map.102
  53.3 0.7 %collective-permute-done.12.blk1 = f32[40,384]{1,0:T(8,128)S(1)} collective-permute-done((f32[40,384]{1,0:T(8,128)S(1)}, f32[40,384]{1,0:T(8,128)S(1)}, u32[]{:S(2)}, u32[]{:S(2)}) %collective-permute-start.12) | collective-permute-done | bytes 61472 | tf_op jit(solution)/shard_map/ppermute | solution.py:655
  53.9 2.7 %collective-permute-done.13.blk0 = f32[40,384]{1,0:T(8,128)S(1)} collective-permute-done((f32[40,384]{1,0:T(8,128)S(1)}, f32[40,384]{1,0:T(8,128)S(1)}, u32[]{:S(2)}, u32[]{:S(2)}) %collective-permute-start.13) | collective-permute-done | bytes 61472 | tf_op jit(solution)/shard_map/ppermute | solution.py:655
  56.7 1.6 %collective-permute-done.14.band1 = f32[40,384]{1,0:T(8,128)S(1)} collective-permute-done((f32[40,384]{1,0:T(8,128)S(1)}, f32[40,384]{1,0:T(8,128)S(1)}, u32[]{:S(2)}, u32[]{:S(2)}) %collective-permute-start.14) | collective-permute-done | bytes 61472 | tf_op jit(solution)/shard_map/ppermute | solution.py:655
  58.3 2.7 %shard_map.103 = (f32[4,32,384]{2,1,0:T(8,128)}, f32[4,32,384]{2,1,0:T(8,128)}) custom-call(s32[2]{0:T(128)S(1)} %pad_add_fusion.parity, f32[40,384]{1,0:T(8,128)S(1)} %collective-permute-done.12.blk1, f32[40,384]{1,0:T(8,128)S(1)} %collective-permute-done.13.blk0, f32[40,384]{1,0:T(8,128)S(1)} %collective-permute-done.14.band1, ...), custom_call_target="tpu_custom_call" | custom-call | tf_op jit(solution)/shard_map/pallas_call | solution.py:639
  (10 shorter events, 0.0 us)
Async XLA Ops:
  4.6 12.1 %collective-permute-start = (f32[80,384]{1,0:T(8,128)S(1)}, f32[80,384]{1,0:T(8,128)S(1)}, u32[]{:S(2)}, u32[]{:S(2)}) collective-permute-start(f32[80,384]{1,0:T(8,128)S(1)} %get-tuple-element.80.blk1), channel_id=1, source_target_pairs={{1,2},{2,1},{3,4},{4,3},{5,6},{6,5},{7,8},{8,7},{9,10},{10,9},{11,... | collective-permute-start | bytes 368648 | tf_op jit(solution)/shard_map/ppermute | solution.py:655
  7.3 9.5 %collective-permute-start.1 = (f32[80,384]{1,0:T(8,128)S(1)}, f32[80,384]{1,0:T(8,128)S(1)}, u32[]{:S(2)}, u32[]{:S(2)}) collective-permute-start(f32[80,384]{1,0:T(8,128)S(1)} %get-tuple-element.81.blk0), channel_id=1, source_target_pairs={{0,1},{1,0},{2,3},{3,2},{4,5},{5,4},{6,7},{7,6},{8,9},{9,8},{10,11... | collective-permute-start | bytes 368648 | tf_op jit(solution)/shard_map/ppermute | solution.py:655
  9.6 10.0 %collective-permute-start.2 = (f32[80,384]{1,0:T(8,128)S(1)}, f32[80,384]{1,0:T(8,128)S(1)}, u32[]{:S(2)}, u32[]{:S(2)}) collective-permute-start(f32[80,384]{1,0:T(8,128)S(1)} %get-tuple-element.82.band1), channel_id=1, source_target_pairs={{16,32},{32,16},{48,64},{64,48},{80,96},{96,80},{112,128},{128,112... | collective-permute-start | bytes 368648 | tf_op jit(solution)/shard_map/ppermute | solution.py:655
  12.4 7.1 %collective-permute-start.3 = (f32[80,384]{1,0:T(8,128)S(1)}, f32[80,384]{1,0:T(8,128)S(1)}, u32[]{:S(2)}, u32[]{:S(2)}) collective-permute-start(f32[80,384]{1,0:T(8,128)S(1)} %get-tuple-element.83.band0), channel_id=1, source_target_pairs={{0,16},{16,0},{32,48},{48,32},{64,80},{80,64},{96,112},{112,96},{1... | collective-permute-start | bytes 368648 | tf_op jit(solution)/shard_map/ppermute | solution.py:655
  22.4 8.8 %collective-permute-start.4 = (f32[40,384]{1,0:T(8,128)S(1)}, f32[40,384]{1,0:T(8,128)S(1)}, u32[]{:S(2)}, u32[]{:S(2)}) collective-permute-start(f32[40,384]{1,0:T(8,128)S(1)} %get-tuple-element.100), channel_id=1, source_target_pairs={{1,2},{2,1},{3,4},{4,3},{5,6},{6,5},{7,8},{8,7},{9,10},{10,9},{11,... | collective-permute-start | bytes 184328 | tf_op jit(solution)/shard_map/ppermute | solution.py:655
  26.7 5.7 %collective-permute-start.5 = (f32[40,384]{1,0:T(8,128)S(1)}, f32[40,384]{1,0:T(8,128)S(1)}, u32[]{:S(2)}, u32[]{:S(2)}) collective-permute-start(f32[40,384]{1,0:T(8,128)S(1)} %get-tuple-element.101), channel_id=1, source_target_pairs={{0,1},{1,0},{2,3},{3,2},{4,5},{5,4},{6,7},{7,6},{8,9},{9,8},{10,11... | collective-permute-start | bytes 184328 | tf_op jit(solution)/shard_map/ppermute | solution.py:655
  27.3 5.8 %collective-permute-start.6 = (f32[40,384]{1,0:T(8,128)S(1)}, f32[40,384]{1,0:T(8,128)S(1)}, u32[]{:S(2)}, u32[]{:S(2)}) collective-permute-start(f32[40,384]{1,0:T(8,128)S(1)} %get-tuple-element.102), channel_id=1, source_target_pairs={{16,32},{32,16},{48,64},{64,48},{80,96},{96,80},{112,128},{128,112... | collective-permute-start | bytes 184328 | tf_op jit(solution)/shard_map/ppermute | solution.py:655
  27.7 5.4 %collective-permute-start.7 = (f32[40,384]{1,0:T(8,128)S(1)}, f32[40,384]{1,0:T(8,128)S(1)}, u32[]{:S(2)}, u32[]{:S(2)}) collective-permute-start(f32[40,384]{1,0:T(8,128)S(1)} %get-tuple-element.103), channel_id=1, source_target_pairs={{0,16},{16,0},{32,48},{48,32},{64,80},{80,64},{96,112},{112,96},{1... | collective-permute-start | bytes 184328 | tf_op jit(solution)/shard_map/ppermute | solution.py:655
  34.5 7.7 %collective-permute-start.8 = (f32[32,128]{1,0:T(8,128)S(1)}, f32[32,128]{1,0:T(8,128)S(1)}, u32[]{:S(2)}, u32[]{:S(2)}) collective-permute-start(f32[32,128]{1,0:T(8,128)S(1)} %get-tuple-element.125), channel_id=1, source_target_pairs={{1,2},{2,1},{3,4},{4,3},{5,6},{6,5},{7,8},{8,7},{9,10},{10,9},{11,... | collective-permute-start | bytes 49160 | tf_op jit(solution)/shard_map/ppermute | solution.py:655
  40.3 5.2 %collective-permute-start.9 = (f32[32,128]{1,0:T(8,128)S(1)}, f32[32,128]{1,0:T(8,128)S(1)}, u32[]{:S(2)}, u32[]{:S(2)}) collective-permute-start(f32[32,128]{1,0:T(8,128)S(1)} %get-tuple-element.126), channel_id=1, source_target_pairs={{0,1},{1,0},{2,3},{3,2},{4,5},{5,4},{6,7},{7,6},{8,9},{9,8},{10,11... | collective-permute-start | bytes 49160 | tf_op jit(solution)/shard_map/ppermute | solution.py:655
  40.6 5.3 %collective-permute-start.10 = (f32[32,128]{1,0:T(8,128)S(1)}, f32[32,128]{1,0:T(8,128)S(1)}, u32[]{:S(2)}, u32[]{:S(2)}) collective-permute-start(f32[32,128]{1,0:T(8,128)S(1)} %get-tuple-element.127), channel_id=1, source_target_pairs={{16,32},{32,16},{48,64},{64,48},{80,96},{96,80},{112,128},{128,112... | collective-permute-start | bytes 49160 | tf_op jit(solution)/shard_map/ppermute | solution.py:655
  41.7 4.3 %collective-permute-start.11 = (f32[32,128]{1,0:T(8,128)S(1)}, f32[32,128]{1,0:T(8,128)S(1)}, u32[]{:S(2)}, u32[]{:S(2)}) collective-permute-start(f32[32,128]{1,0:T(8,128)S(1)} %get-tuple-element.128), channel_id=1, source_target_pairs={{0,16},{16,0},{32,48},{48,32},{64,80},{80,64},{96,112},{112,96},{1... | collective-permute-start | bytes 49160 | tf_op jit(solution)/shard_map/ppermute | solution.py:655
  47.2 6.7 %collective-permute-start.12 = (f32[40,384]{1,0:T(8,128)S(1)}, f32[40,384]{1,0:T(8,128)S(1)}, u32[]{:S(2)}, u32[]{:S(2)}) collective-permute-start(f32[40,384]{1,0:T(8,128)S(1)} %get-tuple-element.140), channel_id=1, source_target_pairs={{1,2},{2,1},{3,4},{4,3},{5,6},{6,5},{7,8},{8,7},{9,10},{10,9},{11,... | collective-permute-start | bytes 184328 | tf_op jit(solution)/shard_map/ppermute | solution.py:655
  50.9 5.7 %collective-permute-start.13 = (f32[40,384]{1,0:T(8,128)S(1)}, f32[40,384]{1,0:T(8,128)S(1)}, u32[]{:S(2)}, u32[]{:S(2)}) collective-permute-start(f32[40,384]{1,0:T(8,128)S(1)} %get-tuple-element.141), channel_id=1, source_target_pairs={{0,1},{1,0},{2,3},{3,2},{4,5},{5,4},{6,7},{7,6},{8,9},{9,8},{10,11... | collective-permute-start | bytes 184328 | tf_op jit(solution)/shard_map/ppermute | solution.py:655
  52.5 5.8 %collective-permute-start.14 = (f32[40,384]{1,0:T(8,128)S(1)}, f32[40,384]{1,0:T(8,128)S(1)}, u32[]{:S(2)}, u32[]{:S(2)}) collective-permute-start(f32[40,384]{1,0:T(8,128)S(1)} %get-tuple-element.142), channel_id=1, source_target_pairs={{16,32},{32,16},{48,64},{64,48},{80,96},{96,80},{112,128},{128,112... | collective-permute-start | bytes 184328 | tf_op jit(solution)/shard_map/ppermute | solution.py:655
  53.0 5.3 %collective-permute-start.15 = (f32[40,384]{1,0:T(8,128)S(1)}, f32[40,384]{1,0:T(8,128)S(1)}, u32[]{:S(2)}, u32[]{:S(2)}) collective-permute-start(f32[40,384]{1,0:T(8,128)S(1)} %get-tuple-element.143), channel_id=1, source_target_pairs={{0,16},{16,0},{32,48},{48,32},{64,80},{80,64},{96,112},{112,96},{1... | collective-permute-start | bytes 184328 | tf_op jit(solution)/shard_map/ppermute | solution.py:655
